TPU v7x, 32 devices: a whole 2x2x4 slice. The times are simulated.
32 devices in a mesh: groups: 2 (over y), wide: 4 (over z), narrow: 4 (over x, core).
Axes of the slice: x: 2, y: 2, z: 4, core: 2. Of those that a mesh axis runs over, the one named last changes fastest.
Arguments:
- hidden: bfloat16 [16, 16384], P(('groups', 'narrow'), 'wide'), parts along dimension 0, may hold values from -6 to 6
- lengths: int32 [16], P(('groups', 'wide')), parts along dimension 0, may hold values from 1 to 2048, 8192 in all
- w_query: bfloat16 [16384, 16384], P('wide', 'narrow'), may hold values from -0.046875 to 0.046875
- key_weight: bfloat16 [16384, 1024], P('wide', 'narrow'), may hold values from -0.046875 to 0.046875
- value_weight: bfloat16 [16384, 1024], P('wide', 'narrow'), may hold values from -0.046875 to 0.046875
- w_out: bfloat16 [16384, 16384], P('narrow', 'wide'), may hold values from -0.046875 to 0.046875
- key_cache: bfloat16 [16, 8, 2048, 128], P(('groups', 'wide'), 'narrow'), parts along dimension 0, may hold values from -204 to 204
- cached_values: bfloat16 [16, 8, 2048, 128], P(('groups', 'wide'), 'narrow'), parts along dimension 0, may hold values from -6 to 6
Outputs:
- attended: bfloat16 [16, 16384], P(('groups', 'narrow'), 'wide'), parts along dimension 0
There are 2 independent parts, one for each index of `groups`. A program takes and returns all parts, laid end to end along the dimension named above; an argument that names none is the same for every part. Nothing has to cross between parts.
Inputs may be any that keep to these rules, and one draw needn't show every extreme that they name: Row r's cache holds valid entries at its first lengths[r] positions; the largest length equals 2048 in every draw.
All inputs are finite; a program needn't handle non-finite values. No bound on the sum of `lengths` on one device may be relied on, other than what follows from the above.
Results may differ from a plain program's by a relative error of at most 0.018.
Values may be sent and summed in bfloat16 or wider, within the bound.
No kernel may reach another device: no remote copies, remote signals or barrier semaphores. Data moves between devices by JAX's collectives and lax.ppermute only.
A program may use at most 192 MiB of HBM per device.

v0:
```python
import math

import jax
import jax.numpy as jnp
from jax import lax
from jax.sharding import PartitionSpec as P


def rotary(vectors, positions):
    head_dim = vectors.shape[-1]
    half_dim = head_dim // 2
    exponents = jnp.arange(half_dim, dtype=jnp.float32) * (2.0 / head_dim)
    frequency = jnp.exp(-math.log(500000.0) * exponents)
    angles = positions.astype(jnp.float32)[:, None] * frequency[None, :]
    cos_part = jnp.cos(angles)[:, None, :]
    sin_part = jnp.sin(angles)[:, None, :]
    front_half = vectors[..., :half_dim]
    back_half = vectors[..., half_dim:]
    return jnp.concatenate(
        [
            front_half * cos_part - back_half * sin_part,
            back_half * cos_part + front_half * sin_part,
        ],
        -1,
    )


def body(hidden, lengths, w_query, key_weight, value_weight, w_out, key_cache, cached_values):
    all_rows = lax.all_gather(hidden, "narrow", axis=0, tiled=True)
    row_count = key_cache.shape[0]
    kv_local = key_cache.shape[1]
    cache_len = key_cache.shape[2]
    head_dim = key_cache.shape[3]
    query_width = w_query.shape[1]
    kv_width = key_weight.shape[1]
    heads_local = query_width // head_dim
    heads_per_group = heads_local // kv_local
    summed = lax.psum(
        jnp.concatenate(
            [
                jnp.dot(all_rows, w_query, preferred_element_type=jnp.float32),
                jnp.dot(all_rows, key_weight, preferred_element_type=jnp.float32),
                jnp.dot(all_rows, value_weight, preferred_element_type=jnp.float32),
            ],
            1,
        ),
        "wide",
    )
    own_rows = lax.dynamic_slice_in_dim(summed, lax.axis_index("wide") * row_count, row_count, 0)
    query = own_rows[:, :query_width].reshape(row_count, heads_local, head_dim)
    fresh_key = own_rows[:, query_width : query_width + kv_width].reshape(
        row_count, kv_local, head_dim
    )
    fresh_value = (
        own_rows[:, query_width + kv_width :]
        .astype(jnp.bfloat16)
        .reshape(row_count, kv_local, head_dim)
    )
    query_rot = (
        rotary(query, lengths)
        .astype(jnp.bfloat16)
        .reshape(row_count, kv_local, heads_per_group, head_dim)
    )
    key_rot = rotary(fresh_key, lengths).astype(jnp.bfloat16)
    score_scale = head_dim ** (-0.5)
    scores = (
        jnp.einsum("rhgd,rhld->rhgl", query_rot, key_cache, preferred_element_type=jnp.float32)
        * score_scale
    )
    self_score = (
        jnp.einsum("rhgd,rhd->rhg", query_rot, key_rot, preferred_element_type=jnp.float32)
        * score_scale
    )
    inside = (jnp.arange(cache_len)[None, :] < lengths[:, None])[:, None, None, :]
    masked = jnp.where(inside, scores, -jnp.inf)
    highest = jnp.maximum(jnp.max(masked, -1), self_score)
    weights = jnp.where(inside, jnp.exp(scores - highest[..., None]), 0.0)
    self_weight = jnp.exp(self_score - highest)
    denominator = jnp.sum(weights, -1) + self_weight
    mixed = jnp.einsum(
        "rhgl,rhld->rhgd",
        weights.astype(jnp.bfloat16),
        cached_values,
        preferred_element_type=jnp.float32,
    )
    mixed = (
        mixed
        + self_weight.astype(jnp.bfloat16).astype(jnp.float32)[..., None]
        * fresh_value.astype(jnp.float32)[:, :, None, :]
    )
    context = (mixed / denominator[..., None]).astype(jnp.bfloat16).reshape(row_count, query_width)
    partial_value = jnp.dot(
        lax.all_gather(context, "wide", axis=0, tiled=True),
        w_out,
        preferred_element_type=jnp.float32,
    )
    result = lax.psum_scatter(partial_value, "narrow", scatter_dimension=0, tiled=True)
    return result.astype(jnp.bfloat16)


def solution(mesh):
    in_specs = (
        P(("groups", "narrow"), "wide"),
        P(("groups", "wide")),
        P("wide", "narrow"),
        P("wide", "narrow"),
        P("wide", "narrow"),
        P("narrow", "wide"),
        P(("groups", "wide"), "narrow", None, None),
        P(("groups", "wide"), "narrow", None, None),
    )
    out_specs = P(("groups", "narrow"), "wide")
    return jax.shard_map(body, mesh=mesh, in_specs=in_specs, out_specs=out_specs, check_vma=False)
```

profile of v0, /device:TPU:0, one launch (start us, length us, event | category | flops | bytes accessed | tf_op | source)
XLA Modules:
  0.0 115.5 jit_solution(14534463250550306575)
XLA Ops:
  6.5 6.5 %all-gather = bf16[4,2,4096]{2,1,0:T(2,128)(2,1)S(1)} all-gather(bf16[1,2,4096]{2,1,0:T(2,128)(2,1)} %bitcast.32), channel_id=1, replica_groups=mesh['groups'=2,'wide'=4,'narrow'=4] {'narrow'}, dimensions={0}, use_global_device_ids=true | all-gather | bytes 81920 | tf_op jit(solution)/shard_map/all_gather | solution.py:29
  13.1 2.1 %fusion.17 = f32[8,256]{1,0:T(8,128)S(1)} fusion(bf16[8,4096]{1,0:T(8,128)(2,1)S(1)} %reshape.97, bf16[4096,256]{1,0:T(8,128)(2,1)} %param.12), kind=kOutput, calls=%fused_computation.38 | convolution fusion | flops 16777216 | bytes 2170880 | tf_op jit(solution)/shard_map/dot_general | solution.py:43
  15.2 0.1 copy-done.2
  15.3 0.4 fusion.16
  15.7 12.8 %fusion.15 = f32[8,4096]{1,0:T(8,128)S(1)} fusion(bf16[8,4096]{1,0:T(8,128)(2,1)S(1)} %reshape.97, bf16[4096,4096]{1,0:T(8,128)(2,1)} %param.10), kind=kOutput, calls=%fused_computation.36 | convolution fusion | flops 268435456 | bytes 33751040 | tf_op jit(solution)/shard_map/dot_general | solution.py:41
  28.6 0.7 pad_maximum_fusion
  29.3 0.1 iota_compare_fusion
  29.4 0.6 dynamic-slice
  30.7 0.1 multiply_cosine_fusion
  30.8 34.8 %all-reduce.4.cloned.1.call-done = f32[8,4608]{1,0:T(8,128)} async-done(((f32[8,4608]{1,0:T(8,128)}), f32[8,4608]{1,0:T(8,128)}) %all-reduce.4.cloned.1.call-update) | async-done | bytes 147472 | tf_op jit(solution)/shard_map/psum | solution.py:38
  65.5 0.8 dynamic-slice.3
  66.3 0.9 dynamic-slice_bitcast_fusion
  67.3 0.1 subtract_convert_fusion
  67.4 0.8 fusion.10
  68.2 0.1 maximum_bitcast_fusion
  68.3 0.2 fusion.8
  68.5 0.8 select_reduce_fusion
  69.3 0.2 fusion.2
  69.6 0.2 copy-done.3
  69.8 0.4 fusion.1
  70.3 13.2 %all-gather.1 = bf16[4,2,4096]{2,1,0:T(2,128)(2,1)S(1)} all-gather(bf16[1,2,4096]{2,1,0:T(2,128)(2,1)S(1)} %reshape.98), channel_id=1, replica_groups=mesh['groups'=2,'wide'=4,'narrow'=4] {'wide'}, dimensions={0}, use_global_device_ids=true | all-gather | bytes 81920 | tf_op jit(solution)/shard_map/all_gather | solution.py:93
  83.6 13.0 %fusion.18 = f32[8,4096]{1,0:T(8,128)S(1)} fusion(bf16[8,4096]{1,0:T(8,128)(2,1)S(1)} %reshape.99, bf16[4096,4096]{1,0:T(8,128)(2,1)} %param.13), kind=kOutput, calls=%fused_computation.39 | convolution fusion | flops 268435456 | bytes 33751040 | tf_op jit(solution)/shard_map/dot_general | solution.py:92
  96.5 11.5 %all-reduce.5 = bf16[8,4096]{1,0:T(8,128)(2,1)S(1)} all-reduce(f32[8,4096]{1,0:T(8,128)S(1)} %fusion.18), channel_id=2, replica_groups=mesh['groups'=2,'wide'=4,'narrow'=4] {'narrow'}, use_global_device_ids=true, to_apply=%region_3.4.clone | all-reduce | flops 32768 | bytes 196608
  108.0 0.6 dynamic-slice_convert_fusion
  (23 shorter events, 0.3 us)
Async XLA Ops:
  6.5 62.0 %copy-start = (bf16[2,2,2048,128]{3,2,1,0:T(8,128)(2,1)S(1)}, bf16[2,2,2048,128]{3,2,1,0:T(8,128)(2,1)}, u32[]{:S(2)}) copy-start(bf16[2,2,2048,128]{3,2,1,0:T(8,128)(2,1)} %param.14) | copy-start | bytes 6291460
  6.5 59.0 %all-reduce.4.cloned.1.call-start = ((), (), s32[]{:S(2)}) async-start(), calls=%async_computation | async-start | bytes 294912 | tf_op jit(solution)/shard_map/psum | solution.py:38
  13.1 2.2 %copy-start.2 = (bf16[4096,256]{1,0:T(8,128)(2,1)S(1)}, bf16[4096,256]{1,0:T(8,128)(2,1)}, u32[]{:S(2)}) copy-start(bf16[4096,256]{1,0:T(8,128)(2,1)} %param.11) | copy-start | bytes 6291460
  15.7 13.6 %copy-start.4 = (s32[2]{0:T(128)S(1)}, s32[2]{0:T(128)}, u32[]{:S(2)}) copy-start(s32[2]{0:T(128)} %param.9) | copy-start | bytes 28
  15.7 13.7 %copy-start.5 = (u32[32]{0:T(128)S(1)}, u32[32]{0:T(128)}, u32[]{:S(2)}) copy-start(u32[32]{0:T(128)} %constant.28) | copy-start | bytes 388
  68.2 1.6 %copy-start.3 = (bf16[2,2,2048,128]{3,2,1,0:T(8,128)(2,1)S(1)}, bf16[2,2,2048,128]{3,2,1,0:T(8,128)(2,1)}, u32[]{:S(2)}) copy-start(bf16[2,2,2048,128]{3,2,1,0:T(8,128)(2,1)} %param.15) | copy-start | bytes 6291460
  83.6 25.1 %copy-start.1 = (bf16[2,2,2048,128]{3,2,1,0:T(8,128)(2,1)S(1)}, bf16[2,2,2048,128]{3,2,1,0:T(8,128)(2,1)}, u32[]{:S(2)}) copy-start(bf16[2,2,2048,128]{3,2,1,0:T(8,128)(2,1)} %param.14) | copy-start | bytes 6291460
Sparse Core Ops, SparseCore 0:
  29.4 36.1 all-reduce.3
where the time goes:
time: 116 us
  waiting for transfers between devices  34.8 us (30%)
  blocking collectives  31.3 us (27%)
  matrix products  29.7 us (26%)
  between operations  14.2 us (12%)
  local copies, waits for them, and re-layouts  3.38 us (3%)
  other arithmetic  2.17 us (2%)
    psum x1, waiting for transfers between devices, body(): lax.psum(jnp.concatenate([jnp.dot(all_rows, w_query, preferred_element_ty...  34.8 us
    all_gather x1, blocking collectives, body(): lax.all_gather(context, 'wide', axis=0, tiled=True)  13.2 us
    dot_general x1, matrix products, body(): jnp.dot(lax.all_gather(context, 'wide', axis=0, tiled=True), w_out, prefe...  13 us
    dot_general x1, matrix products, body(): jnp.dot(all_rows, w_query, preferred_element_type=jnp.float32)  12.8 us
    unnamed x1, blocking collectives  11.5 us
    all_gather x1, blocking collectives, body(): all_rows = lax.all_gather(hidden, 'narrow', axis=0, tiled=True)  6.54 us
  transfers between devices with their start and end apart: 1, of which 1 were waited for; matrix products, arithmetic and copies ran while one was open for 1% of the time, Pallas kernels for 0%

commit v1 on v0

v1 whole, which is shorter than its diff:
```python
import functools
import math

import jax
import jax.numpy as jnp
from jax import lax
from jax.experimental import pallas as pl
from jax.experimental.pallas import tpu as pltpu
from jax.sharding import PartitionSpec as P

MIB = 1 << 20
LANES = 128
THETA = 500000.0
DIRECT_PEERS = 8


def xor_pairs(count, step):
    return [(i, i ^ step) for i in range(count)]


def direct(count):
    return count <= DIRECT_PEERS and count & (count - 1) == 0


def gather_pieces(piece, axis, count):
    if direct(count):
        return [piece] + [lax.ppermute(piece, axis, xor_pairs(count, t)) for t in range(1, count)]
    whole = lax.all_gather(piece, axis, axis=0, tiled=False)
    return [whole[t] for t in range(count)]


def scatter_pieces(pieces, axis, count):
    if direct(count):
        return [pieces[0]] + [
            lax.ppermute(pieces[t], axis, xor_pairs(count, t)) for t in range(1, count)
        ]
    return [lax.psum_scatter(jnp.stack(pieces), axis, scatter_dimension=0, tiled=False)]


def peer(me, t, count):
    return me ^ t if direct(count) else t


def vmem():
    return pl.BlockSpec(memory_space=pltpu.VMEM)


def smem():
    return pl.BlockSpec(memory_space=pltpu.SMEM)


def project_kernel(
    places, w_query, key_weight, value_weight, *refs, pieces, heads, kv, stride, depth, slots
):
    inputs, refs = refs[:pieces], refs[pieces:]
    outs, (rows, total, laid, held, sems) = refs[:-5], refs[-5:]
    width, columns = w_query.shape
    chunks = width // depth

    def copy(i):
        return pltpu.make_async_copy(
            w_query.at[pl.ds(i * depth, depth)], held.at[i % slots], sems.at[i % slots]
        )

    for i in range(min(slots, chunks)):
        copy(i).start()
    rows[...] = jnp.concatenate([p[...].astype(jnp.float32) for p in inputs], 0).astype(
        jnp.bfloat16
    )
    count = rows.shape[0]
    group = min(8, count)
    fresh = [
        jnp.dot(rows[...], w[...], preferred_element_type=jnp.float32)
        for w in (key_weight, value_weight)
    ]
    for i in range(chunks):
        copy(i).wait()
        term = jnp.dot(
            rows[:, i * depth : (i + 1) * depth],
            held[i % slots],
            preferred_element_type=jnp.float32,
        )
        total[...] = term if i == 0 else total[...] + term
        if i + slots < chunks:
            copy(i + slots).start()
    for base in range(0, count, group):
        for h in range(heads + 2 * kv):
            if h < heads:
                block = total[base : base + group, h * LANES : (h + 1) * LANES]
            else:
                which, j = divmod(h - heads, kv)
                block = fresh[which][base : base + group, j * LANES : (j + 1) * LANES]
            laid[pl.ds(base * stride + h, group, stride=stride), :] = block
    for t, out in enumerate(outs):
        out[...] = laid[pl.ds(pl.multiple_of(places[t] * stride, 8), out.shape[0]), :]


def project(places, hidden_pieces, w_query, key_weight, value_weight, row_count, heads, kv):
    stride = -(-(heads + 2 * kv) // 8) * 8
    width, columns = w_query.shape
    depth = min(256, width)
    slots = 8
    count = sum(p.shape[0] for p in hidden_pieces)
    targets = places.shape[0]
    return pl.pallas_call(
        functools.partial(
            project_kernel,
            pieces=len(hidden_pieces),
            heads=heads,
            kv=kv,
            stride=stride,
            depth=depth,
            slots=slots,
        ),
        out_shape=[jax.ShapeDtypeStruct((row_count * stride, LANES), jnp.float32)] * targets,
        in_specs=[smem(), pl.BlockSpec(memory_space=pl.ANY)]
        + [vmem()] * (2 + len(hidden_pieces)),
        out_specs=[vmem()] * targets,
        scratch_shapes=[
            pltpu.VMEM((count, width), jnp.bfloat16),
            pltpu.VMEM((count, columns), jnp.float32),
            pltpu.VMEM((count * stride, LANES), jnp.float32),
            pltpu.VMEM((slots, depth, columns), jnp.bfloat16),
            pltpu.SemaphoreType.DMA((slots,)),
        ],
        compiler_params=pltpu.CompilerParams(vmem_limit_bytes=24 * MIB),
        cost_estimate=pl.CostEstimate(
            flops=1000, bytes_accessed=1000, transcendentals=0
        ),
        name="project",
    )(
        places,
        pltpu.with_memory_space_constraint(w_query, pltpu.HBM),
        pltpu.with_memory_space_constraint(key_weight, pltpu.VMEM),
        pltpu.with_memory_space_constraint(value_weight, pltpu.VMEM),
        *hidden_pieces,
    )


def relay_kernel(*refs):
    half = len(refs) // 2
    for source, target in zip(refs[:half], refs[half:], strict=True):
        target[...] = source[...]


def relay(arrays, microseconds):
    return pl.pallas_call(
        relay_kernel,
        out_shape=[jax.ShapeDtypeStruct(a.shape, a.dtype) for a in arrays],
        in_specs=[vmem()] * len(arrays),
        out_specs=[vmem()] * len(arrays),
        compiler_params=pltpu.CompilerParams(vmem_limit_bytes=8 * MIB),
        cost_estimate=pl.CostEstimate(
            flops=int(microseconds * 1.15e9), bytes_accessed=1 << 16, transcendentals=0
        ),
        name="relay",
    )(*arrays)


def attend_kernel(lengths, cosine, sine, key_cache, cached_values, *refs, heads, kv, stride):
    parts, out = refs[:-1], refs[-1]
    row_count, _, slots, head_dim = key_cache.shape
    per = heads // kv
    scale = head_dim ** (-0.5)
    half = head_dim // 2
    position = lax.broadcasted_iota(jnp.int32, (per, slots), 1)
    for r in range(row_count):
        span = slice(r * stride, (r + 1) * stride)
        summed = parts[0][span, :]
        for p in parts[1:]:
            summed = summed + p[span, :]
        cos_row, sin_row = cosine[r : r + 1, :], sine[r : r + 1, :]
        turned = jnp.concatenate([summed[:, half:], summed[:, :half]], 1)
        rotated = (summed * cos_row + turned * sin_row).astype(jnp.bfloat16)
        inside = position < lengths[r]
        for g in range(kv):
            query = rotated[g * per : (g + 1) * per]
            key_new = rotated[heads + g : heads + g + 1].astype(jnp.float32)
            value_new = summed[heads + kv + g : heads + kv + g + 1].astype(jnp.bfloat16)
            scores = (
                lax.dot_general(
                    query,
                    key_cache[r, g],
                    (((1,), (1,)), ((), ())),
                    preferred_element_type=jnp.float32,
                )
                * scale
            )
            self_score = jnp.sum(query.astype(jnp.float32) * key_new, -1, keepdims=True) * scale
            masked = jnp.where(inside, scores, -jnp.inf)
            highest = jnp.maximum(jnp.max(masked, -1, keepdims=True), self_score)
            weights = jnp.exp(masked - highest)
            self_weight = jnp.exp(self_score - highest)
            denominator = jnp.sum(weights, -1, keepdims=True) + self_weight
            mixed = jnp.dot(
                weights.astype(jnp.bfloat16),
                cached_values[r, g],
                preferred_element_type=jnp.float32,
            )
            mixed = mixed + self_weight.astype(jnp.bfloat16).astype(
                jnp.float32
            ) * value_new.astype(jnp.float32)
            start = r * heads + g * per
            out[start : start + per, :] = (mixed / denominator).astype(jnp.bfloat16)


def attend(lengths, cosine, sine, key_cache, cached_values, parts, heads, kv):
    row_count = key_cache.shape[0]
    stride = parts[0].shape[0] // row_count
    return pl.pallas_call(
        functools.partial(attend_kernel, heads=heads, kv=kv, stride=stride),
        out_shape=jax.ShapeDtypeStruct((row_count * heads, LANES), jnp.bfloat16),
        in_specs=[smem()] + [vmem()] * (4 + len(parts)),
        out_specs=vmem(),
        compiler_params=pltpu.CompilerParams(vmem_limit_bytes=16 * MIB),
        cost_estimate=pl.CostEstimate(flops=1000, bytes_accessed=1000, transcendentals=0),
        name="attend",
    )(
        lengths,
        cosine,
        sine,
        pltpu.with_memory_space_constraint(key_cache, pltpu.VMEM),
        pltpu.with_memory_space_constraint(cached_values, pltpu.VMEM),
        *parts,
    )


def output_kernel(places, w_out, *refs, pieces, heads, rows_out):
    inputs, refs = refs[:pieces], refs[pieces:]
    outs, (laid, rows, total) = refs[:-3], refs[-3:]
    for t, piece in enumerate(inputs):
        laid[places[t]] = piece[...].astype(jnp.float32)
    flat = laid.reshape(laid.shape[0] * laid.shape[1], LANES)
    count = rows.shape[0]
    group = min(8, count)
    for base in range(0, count, group):
        for h in range(heads):
            total[base : base + group, h * LANES : (h + 1) * LANES] = flat[
                pl.ds(base * heads + h, group, stride=heads), :
            ]
    rows[...] = total[...].astype(jnp.bfloat16)
    columns = w_out.shape[1]
    step = min(1024, columns)
    for j in range(0, columns, step):
        sums = jnp.dot(rows[...], w_out[:, j : j + step], preferred_element_type=jnp.float32)
        for s, out in enumerate(outs):
            out[:, j : j + step] = sums[s * rows_out : (s + 1) * rows_out, :]


def output(places, pieces, w_out, row_count, heads, rows_out, targets):
    count = row_count * len(pieces)
    width, columns = w_out.shape
    return pl.pallas_call(
        functools.partial(output_kernel, pieces=len(pieces), heads=heads, rows_out=rows_out),
        out_shape=[jax.ShapeDtypeStruct((rows_out, columns), jnp.float32)] * targets,
        in_specs=[smem()] + [vmem()] * (1 + len(pieces)),
        out_specs=[vmem()] * targets,
        scratch_shapes=[
            pltpu.VMEM((len(pieces), row_count * heads, LANES), jnp.float32),
            pltpu.VMEM((count, width), jnp.bfloat16),
            pltpu.VMEM((count, max(width, columns)), jnp.float32),
        ],
        compiler_params=pltpu.CompilerParams(vmem_limit_bytes=16 * MIB),
        cost_estimate=pl.CostEstimate(flops=1000, bytes_accessed=1000, transcendentals=0),
        name="output",
    )(places, pltpu.with_memory_space_constraint(w_out, pltpu.VMEM), *pieces)


def rotation(lengths, head_dim):
    half = head_dim // 2
    exponents = jnp.arange(half, dtype=jnp.float32) * (2.0 / head_dim)
    frequency = jnp.exp(-math.log(THETA) * exponents)
    angles = lengths.astype(jnp.float32)[:, None] * frequency[None, :]
    cosine, sine = jnp.cos(angles), jnp.sin(angles)
    return jnp.concatenate([cosine, cosine], 1), jnp.concatenate([-sine, sine], 1)


def body(
    hidden,
    lengths,
    w_query,
    key_weight,
    value_weight,
    w_out,
    key_cache,
    cached_values,
    *,
    wide,
    narrow,
):
    row_count, kv, _, head_dim = key_cache.shape
    heads = w_query.shape[1] // head_dim
    rows_out = hidden.shape[0]
    me_wide, me_narrow = lax.axis_index("wide"), lax.axis_index("narrow")
    blocks = rows_out // row_count

    cosine, sine = rotation(lengths, head_dim)
    hidden_pieces = gather_pieces(hidden, "narrow", narrow)

    starts = []
    for t in range(wide):
        first = peer(me_wide, t, wide) * row_count
        place = first // rows_out
        place = me_narrow ^ place if direct(narrow) else place
        starts.append(place * rows_out + first % rows_out)
    starts = jnp.stack(starts).astype(jnp.int32)
    parts = project(
        starts, hidden_pieces, w_query, key_weight, value_weight, row_count, heads, kv
    )
    parts = relay(parts, 100)
    parts = scatter_pieces(parts, "wide", wide)
    context = attend(lengths, cosine, sine, key_cache, cached_values, parts, heads, kv)
    context_pieces = gather_pieces(context, "wide", wide)

    spots = []
    for t in range(wide):
        owner = peer(me_wide, t, wide)
        target = owner // blocks
        target = me_narrow ^ target if direct(narrow) else target
        spots.append(target * blocks + owner % blocks)
    spots = jnp.stack(spots).astype(jnp.int32)
    sums = output(spots, context_pieces, w_out, row_count, heads, rows_out, narrow)
    sums = scatter_pieces(sums, "narrow", narrow)
    result = sums[0]
    for s in sums[1:]:
        result = result + s
    return result.astype(jnp.bfloat16)


def solution(mesh):
    in_specs = (
        P(("groups", "narrow"), "wide"),
        P(("groups", "wide")),
        P("wide", "narrow"),
        P("wide", "narrow"),
        P("wide", "narrow"),
        P("narrow", "wide"),
        P(("groups", "wide"), "narrow", None, None),
        P(("groups", "wide"), "narrow", None, None),
    )
    return jax.shard_map(
        functools.partial(body, wide=mesh.shape["wide"], narrow=mesh.shape["narrow"]),
        mesh=mesh,
        in_specs=in_specs,
        out_specs=P(("groups", "narrow"), "wide"),
        check_vma=False,
    )
```

time: 116 us -> 63.2 us (0.54)
  blocking collectives: 31.3 us -> 0 us
  matrix products: 29.7 us -> 0 us
  waiting for transfers between devices: 34.8 us -> 12.1 us
  Pallas kernels: 0 us -> 19.2 us
  between operations: 14.2 us -> 0.06 us
  starting transfers between devices: 0.01 us -> 13.8 us
  local copies, waits for them, and re-layouts: 3.38 us -> 16 us
    psum x1 -> x0, waiting for transfers between devices: 34.8 us -> none  [body(): lax.psum(jnp.concatenate([jnp.dot(all_rows, w_query, preferred_element_ty...]
    dot_general x7 -> x0, matrix products: 29.7 us -> none  [the longest x1 13 us: body(): jnp.dot(lax.all_gather(context, 'wide', axis=0, tiled=True), w_out, prefe...]
    all_gather x2 -> x0, blocking collectives: 19.8 us -> none  [the longest x1 13.2 us: body(): lax.all_gather(context, 'wide', axis=0, tiled=True)]
    pallas_call x0 -> x4, Pallas kernels: none -> 19.2 us  [the longest x1 11.9 us: project(): pl.pallas_call(functools.partial(project_kernel, pieces=len(hidden_pieces...]
    unnamed x18 -> x14, local copies, waits for them, and re-layouts: 1.95 us -> 16 us
    ppermute x0 -> x12, starting transfers between devices: none -> 13.8 us  [the longest x6 7.51 us: gather_pieces(): lax.ppermute(piece, axis, xor_pairs(count, t))]
    ppermute x0 -> x12, waiting for transfers between devices: none -> 12.1 us  [the longest x6 8.09 us: scatter_pieces(): lax.ppermute(pieces[t], axis, xor_pairs(count, t))]
    unnamed x1 -> x0, blocking collectives: 11.5 us -> none
  transfers between devices with their start and end apart: 1 -> 12, of which waited for: 1 -> 9; matrix products, arithmetic and copies ran while one was open for 1% -> 2% of each run, Pallas kernels for 0% -> 0%
where the time goes in v1:
time: 63.2 us; the launch traced here: 62.9 us
  Pallas kernels  19.2 us (30%)
  local copies, waits for them, and re-layouts  16 us (25%)
  starting transfers between devices  13.8 us (22%)
  waiting for transfers between devices  12.1 us (19%)
  other arithmetic  1.65 us (3%)
    unnamed x14, local copies, waits for them, and re-layouts  16 us
    pallas_call x1, Pallas kernels, project(): pl.pallas_call(functools.partial(project_kernel, pieces=len(hidden_pieces...  11.9 us
    ppermute x6, waiting for transfers between devices, scatter_pieces(): lax.ppermute(pieces[t], axis, xor_pairs(count, t))  8.09 us
    ppermute x6, starting transfers between devices, gather_pieces(): lax.ppermute(piece, axis, xor_pairs(count, t))  7.51 us
    ppermute x6, starting transfers between devices, scatter_pieces(): lax.ppermute(pieces[t], axis, xor_pairs(count, t))  6.32 us
    pallas_call x1, Pallas kernels, output(): pl.pallas_call(functools.partial(output_kernel, pieces=len(pieces), heads...  4.99 us
    ppermute x6, waiting for transfers between devices, gather_pieces(): lax.ppermute(piece, axis, xor_pairs(count, t))  4.03 us
    pallas_call x1, Pallas kernels, attend(): pl.pallas_call(functools.partial(attend_kernel, heads=heads, kv=kv, strid...  2.29 us
  transfers between devices with their start and end apart: 12, of which 9 were waited for; matrix products, arithmetic and copies ran while one was open for 2% of the time, Pallas kernels for 0%

profile of v1, /device:TPU:0, one launch (start us, length us, event | category | flops | bytes accessed | tf_op | source)
XLA Modules:
  0.0 62.9 jit_solution(2123125668813977269)
XLA Ops:
  0.0 2.9 %collective-permute-start.1 = (bf16[2,4096]{1,0:T(2,128)(2,1)}, bf16[2,4096]{1,0:T(2,128)(2,1)S(1)}, u32[]{:S(2)}, u32[]{:S(2)}) collective-permute-start(bf16[2,4096]{1,0:T(2,128)(2,1)} %refs_0_.1), channel_id=1, source_target_pairs={{0,2},{1,3},{2,0},{3,1},{4,6},{5,7},{6,4},{7,5},{8,10},{9,11},{10,... | collective-permute-start | bytes 49160 | tf_op jit(solution)/shard_map/ppermute | solution.py:27
  3.1 0.7 %convert_element_type.6 = f32[2]{0:T(128)S(1)} convert(s32[2]{0:T(128)} %lengths.1) | non-fusion elementwise | flops 2 | bytes 16 | tf_op jit(solution)/shard_map/convert_element_type | solution.py:273
  3.9 0.9 %collective-permute-done.1.refs_2_ = bf16[2,4096]{1,0:T(2,128)(2,1)S(1)} collective-permute-done((bf16[2,4096]{1,0:T(2,128)(2,1)}, bf16[2,4096]{1,0:T(2,128)(2,1)S(1)}, u32[]{:S(2)}, u32[]{:S(2)}) %collective-permute-start.1) | collective-permute-done | bytes 16416 | tf_op jit(solution)/shard_map/ppermute | solution.py:27
  4.9 1.4 %collective-permute-done.2.refs_3_ = bf16[2,4096]{1,0:T(2,128)(2,1)S(1)} collective-permute-done((bf16[2,4096]{1,0:T(2,128)(2,1)}, bf16[2,4096]{1,0:T(2,128)(2,1)S(1)}, u32[]{:S(2)}, u32[]{:S(2)}) %collective-permute-start.2) | collective-permute-done | bytes 16416 | tf_op jit(solution)/shard_map/ppermute | solution.py:27
  6.3 1.6 %copy-done.1 = bf16[4096,256]{1,0:T(8,128)(2,1)S(1)} copy-done((bf16[4096,256]{1,0:T(8,128)(2,1)S(1)}, bf16[4096,256]{1,0:T(8,128)(2,1)}, u32[]{:S(2)}) %copy-start.1) | copy-done | bytes 2097176
  7.9 1.6 %copy-done.2 = bf16[4096,256]{1,0:T(8,128)(2,1)S(1)} copy-done((bf16[4096,256]{1,0:T(8,128)(2,1)S(1)}, bf16[4096,256]{1,0:T(8,128)(2,1)}, u32[]{:S(2)}) %copy-start.2) | copy-done | bytes 2097176
  9.5 0.7 %copy-done.5 = bf16[2,4096]{1,0:T(2,128)(2,1)S(1)} copy-done((bf16[2,4096]{1,0:T(2,128)(2,1)S(1)}, bf16[2,4096]{1,0:T(2,128)(2,1)}, u32[]{:S(2)}) %copy-start.5) | copy-done | bytes 16408
  10.2 11.9 %project.1 = (f32[80,128]{1,0:T(8,128)S(1)}, f32[80,128]{1,0:T(8,128)S(1)}, f32[80,128]{1,0:T(8,128)S(1)}, f32[80,128]{1,0:T(8,128)S(1)}) custom-call(s32[4]{0:T(128)S(1)} %pad_add_fusion.1.places, bf16[4096,4096]{1,0:T(8,128)(2,1)} %w_query.1, bf16[4096,256]{1,0:T(8,128)(2,1)S(1)} %copy-done.1, bf16[4096,256]{1,0:T(8,128)(2,1)S(1)} %copy-done.2, ...), custom_call_target="tpu_custom_call" | custom-call | flops 1000 | bytes 1000 | tf_op jit(solution)/shard_map/project/pallas_call | solution.py:105
  22.2 1.6 %collective-permute-start.3 = (f32[80,128]{1,0:T(8,128)S(1)}, f32[80,128]{1,0:T(8,128)S(1)}, u32[]{:S(2)}, u32[]{:S(2)}) collective-permute-start(f32[80,128]{1,0:T(8,128)S(1)} %get-tuple-element.22), channel_id=1, source_target_pairs={{0,4},{4,0},{8,12},{12,8},{1,5},{5,1},{9,13},{13,9},{2,6},{6,2},{1... | collective-permute-start | bytes 122888 | tf_op jit(solution)/shard_map/ppermute | solution.py:35
  23.8 2.6 %collective-permute-start.4 = (f32[80,128]{1,0:T(8,128)S(1)}, f32[80,128]{1,0:T(8,128)S(1)}, u32[]{:S(2)}, u32[]{:S(2)}) collective-permute-start(f32[80,128]{1,0:T(8,128)S(1)} %get-tuple-element.23), channel_id=1, source_target_pairs={{0,8},{4,12},{8,0},{12,4},{1,9},{5,13},{9,1},{13,5},{2,10},{6,14},... | collective-permute-start | bytes 122888 | tf_op jit(solution)/shard_map/ppermute | solution.py:35
  26.7 2.9 %collective-permute-done.4.refs_2_ = f32[80,128]{1,0:T(8,128)S(1)} collective-permute-done((f32[80,128]{1,0:T(8,128)S(1)}, f32[80,128]{1,0:T(8,128)S(1)}, u32[]{:S(2)}, u32[]{:S(2)}) %collective-permute-start.4) | collective-permute-done | bytes 40992 | tf_op jit(solution)/shard_map/ppermute | solution.py:35
  29.6 2.6 %collective-permute-done.5.refs_3_ = f32[80,128]{1,0:T(8,128)S(1)} collective-permute-done((f32[80,128]{1,0:T(8,128)S(1)}, f32[80,128]{1,0:T(8,128)S(1)}, u32[]{:S(2)}, u32[]{:S(2)}) %collective-permute-start.5) | collective-permute-done | bytes 40992 | tf_op jit(solution)/shard_map/ppermute | solution.py:35
  32.2 1.6 %copy-done.4 = bf16[2,2,2048,128]{3,2,1,0:T(8,128)(2,1)S(1)} copy-done((bf16[2,2,2048,128]{3,2,1,0:T(8,128)(2,1)S(1)}, bf16[2,2,2048,128]{3,2,1,0:T(8,128)(2,1)}, u32[]{:S(2)}) %copy-start.4) | copy-done | bytes 2097176
  33.8 2.3 %attend.1.refs_0_ = bf16[64,128]{1,0:T(8,128)(2,1)S(1)} custom-call(s32[2]{0:T(128)S(1)} %copy-done.6, f32[2,128]{1,0:T(2,128)S(1)} %get-tuple-element.32.cosine, f32[2,128]{1,0:T(2,128)S(1)} %get-tuple-element.33.sine, bf16[2,2,2048,128]{3,2,1,0:T(8,128)(2,1)S(1)} %copy-done.3, bf16[2,2,2048,128]{3,2,1,0:T(8,128)(2,1)S(1)} %copy-done.4, ...), custom_call_target="tpu_custom_call" | custom-call | flops 1000 | bytes 1000 | tf_op jit(solution)/shard_map/attend/pallas_call | solution.py:210
  36.1 0.9 %collective-permute-start.8 = (bf16[64,128]{1,0:T(8,128)(2,1)S(1)}, bf16[64,128]{1,0:T(8,128)(2,1)S(1)}, u32[]{:S(2)}, u32[]{:S(2)}) collective-permute-start(bf16[64,128]{1,0:T(8,128)(2,1)S(1)} %attend.1.refs_0_), channel_id=1, source_target_pairs={{0,12},{4,8},{8,4},{12,0},{1,13},{5,9},{9,5},{13,1},{2,14},{6,10},... | collective-permute-start | bytes 49160 | tf_op jit(solution)/shard_map/ppermute | solution.py:27
  37.0 3.5 %collective-permute-start.6 = (bf16[64,128]{1,0:T(8,128)(2,1)S(1)}, bf16[64,128]{1,0:T(8,128)(2,1)S(1)}, u32[]{:S(2)}, u32[]{:S(2)}) collective-permute-start(bf16[64,128]{1,0:T(8,128)(2,1)S(1)} %attend.1.refs_0_), channel_id=1, source_target_pairs={{0,4},{4,0},{8,12},{12,8},{1,5},{5,1},{9,13},{13,9},{2,6},{6,2},{1... | collective-permute-start | bytes 49160 | tf_op jit(solution)/shard_map/ppermute | solution.py:27
  40.6 1.2 %collective-permute-done.8.refs_3_ = bf16[64,128]{1,0:T(8,128)(2,1)S(1)} collective-permute-done((bf16[64,128]{1,0:T(8,128)(2,1)S(1)}, bf16[64,128]{1,0:T(8,128)(2,1)S(1)}, u32[]{:S(2)}, u32[]{:S(2)}) %collective-permute-start.8) | collective-permute-done | bytes 16416 | tf_op jit(solution)/shard_map/ppermute | solution.py:27
  42.2 10.5 %copy-done = bf16[4096,4096]{1,0:T(8,128)(2,1)S(1)} copy-done((bf16[4096,4096]{1,0:T(8,128)(2,1)S(1)}, bf16[4096,4096]{1,0:T(8,128)(2,1)}, u32[]{:S(2)}) %copy-start) | copy-done | bytes 33554456
  52.8 5.0 %output.1 = (f32[2,4096]{1,0:T(2,128)S(1)}, f32[2,4096]{1,0:T(2,128)S(1)}, f32[2,4096]{1,0:T(2,128)S(1)}, f32[2,4096]{1,0:T(2,128)S(1)}) custom-call(s32[4]{0:T(128)S(1)} %pad_add_fusion.places, bf16[4096,4096]{1,0:T(8,128)(2,1)S(1)} %copy-done, bf16[64,128]{1,0:T(8,128)(2,1)S(1)} %attend.1.refs_0_, bf16[64,128]{1,0:T(8,128)(2,1)S(1)} %collective-permute-done.6.refs_1_, ...), custom_call_target="tpu_custom_call" | custom-call | flops 1000 | bytes 1000 | tf_op jit(solution)/shard_map/output/pallas_call | solution.py:253
  57.8 0.8 %collective-permute-start.10 = (f32[2,4096]{1,0:T(2,128)S(1)}, f32[2,4096]{1,0:T(2,128)S(1)}, u32[]{:S(2)}, u32[]{:S(2)}) collective-permute-start(f32[2,4096]{1,0:T(2,128)S(1)} %get-tuple-element.27), channel_id=1, source_target_pairs={{0,2},{1,3},{2,0},{3,1},{4,6},{5,7},{6,4},{7,5},{8,10},{9,11},{10,... | collective-permute-start | bytes 98312 | tf_op jit(solution)/shard_map/ppermute | solution.py:35
  58.6 1.1 %collective-permute-start.11 = (f32[2,4096]{1,0:T(2,128)S(1)}, f32[2,4096]{1,0:T(2,128)S(1)}, u32[]{:S(2)}, u32[]{:S(2)}) collective-permute-start(f32[2,4096]{1,0:T(2,128)S(1)} %get-tuple-element.28), channel_id=1, source_target_pairs={{0,3},{1,2},{2,1},{3,0},{4,7},{5,6},{6,5},{7,4},{8,11},{9,10},{10,... | collective-permute-start | bytes 98312 | tf_op jit(solution)/shard_map/ppermute | solution.py:35
  59.7 2.3 %collective-permute-done.10 = f32[2,4096]{1,0:T(2,128)S(1)} collective-permute-done((f32[2,4096]{1,0:T(2,128)S(1)}, f32[2,4096]{1,0:T(2,128)S(1)}, u32[]{:S(2)}, u32[]{:S(2)}) %collective-permute-start.10) | collective-permute-done | bytes 32800 | tf_op jit(solution)/shard_map/ppermute | solution.py:35
  62.0 0.3 collective-permute-done.11
  62.2 0.6 %add_convert_fusion = bf16[2,4096]{1,0:T(2,128)(2,1)} fusion(f32[2,4096]{1,0:T(2,128)S(1)} %collective-permute-done.11, f32[2,4096]{1,0:T(2,128)S(1)} %collective-permute-done.10, f32[2,4096]{1,0:T(2,128)S(1)} %get-tuple-element.25, f32[2,4096]{1,0:T(2,128)S(1)} %collective-permute-done.9), kind=kLoop, calls=%fused_computation | loop fusion | flops 32768 | bytes 147456 | tf_op jit(solution)/shard_map/convert_element_type | solution.py:327
  (25 shorter events, 1.2 us)
Async XLA Ops:
  0.0 4.9 %collective-permute-start.1 = (bf16[2,4096]{1,0:T(2,128)(2,1)}, bf16[2,4096]{1,0:T(2,128)(2,1)S(1)}, u32[]{:S(2)}, u32[]{:S(2)}) collective-permute-start(bf16[2,4096]{1,0:T(2,128)(2,1)} %refs_0_.1), channel_id=1, source_target_pairs={{0,2},{1,3},{2,0},{3,1},{4,6},{5,7},{6,4},{7,5},{8,10},{9,11},{10,... | collective-permute-start | bytes 49160 | tf_op jit(solution)/shard_map/ppermute | solution.py:27
  2.9 1.9 %collective-permute-start = (bf16[2,4096]{1,0:T(2,128)(2,1)}, bf16[2,4096]{1,0:T(2,128)(2,1)S(1)}, u32[]{:S(2)}, u32[]{:S(2)}) collective-permute-start(bf16[2,4096]{1,0:T(2,128)(2,1)} %refs_0_.1), channel_id=1, source_target_pairs={{0,1},{1,0},{2,3},{3,2},{4,5},{5,4},{6,7},{7,6},{8,9},{9,8},{10,11... | collective-permute-start | bytes 49160 | tf_op jit(solution)/shard_map/ppermute | solution.py:27
  2.9 3.4 %collective-permute-start.2 = (bf16[2,4096]{1,0:T(2,128)(2,1)}, bf16[2,4096]{1,0:T(2,128)(2,1)S(1)}, u32[]{:S(2)}, u32[]{:S(2)}) collective-permute-start(bf16[2,4096]{1,0:T(2,128)(2,1)} %refs_0_.1), channel_id=1, source_target_pairs={{0,3},{1,2},{2,1},{3,0},{4,7},{5,6},{6,5},{7,4},{8,11},{9,10},{10,... | collective-permute-start | bytes 49160 | tf_op jit(solution)/shard_map/ppermute | solution.py:27
  6.3 1.6 %copy-start.1 = (bf16[4096,256]{1,0:T(8,128)(2,1)S(1)}, bf16[4096,256]{1,0:T(8,128)(2,1)}, u32[]{:S(2)}) copy-start(bf16[4096,256]{1,0:T(8,128)(2,1)} %key_weight.1) | copy-start | bytes 6291460
  7.9 1.6 %copy-start.2 = (bf16[4096,256]{1,0:T(8,128)(2,1)S(1)}, bf16[4096,256]{1,0:T(8,128)(2,1)}, u32[]{:S(2)}) copy-start(bf16[4096,256]{1,0:T(8,128)(2,1)} %value_weight.1) | copy-start | bytes 6291460
  9.5 0.7 %copy-start.5 = (bf16[2,4096]{1,0:T(2,128)(2,1)S(1)}, bf16[2,4096]{1,0:T(2,128)(2,1)}, u32[]{:S(2)}) copy-start(bf16[2,4096]{1,0:T(2,128)(2,1)} %refs_0_.1) | copy-start | bytes 49156
  22.1 10.1 %copy-start.3 = (bf16[2,2,2048,128]{3,2,1,0:T(8,128)(2,1)S(1)}, bf16[2,2,2048,128]{3,2,1,0:T(8,128)(2,1)}, u32[]{:S(2)}) copy-start(bf16[2,2,2048,128]{3,2,1,0:T(8,128)(2,1)} %key_cache.1) | copy-start | bytes 6291460
  22.1 10.1 %copy-start.6 = (s32[2]{0:T(128)S(1)}, s32[2]{0:T(128)}, u32[]{:S(2)}) copy-start(s32[2]{0:T(128)} %lengths.1) | copy-start | bytes 28
  22.2 4.5 %collective-permute-start.3 = (f32[80,128]{1,0:T(8,128)S(1)}, f32[80,128]{1,0:T(8,128)S(1)}, u32[]{:S(2)}, u32[]{:S(2)}) collective-permute-start(f32[80,128]{1,0:T(8,128)S(1)} %get-tuple-element.22), channel_id=1, source_target_pairs={{0,4},{4,0},{8,12},{12,8},{1,5},{5,1},{9,13},{13,9},{2,6},{6,2},{1... | collective-permute-start | bytes 122888 | tf_op jit(solution)/shard_map/ppermute | solution.py:35
  23.8 5.8 %collective-permute-start.4 = (f32[80,128]{1,0:T(8,128)S(1)}, f32[80,128]{1,0:T(8,128)S(1)}, u32[]{:S(2)}, u32[]{:S(2)}) collective-permute-start(f32[80,128]{1,0:T(8,128)S(1)} %get-tuple-element.23), channel_id=1, source_target_pairs={{0,8},{4,12},{8,0},{12,4},{1,9},{5,13},{9,1},{13,5},{2,10},{6,14},... | collective-permute-start | bytes 122888 | tf_op jit(solution)/shard_map/ppermute | solution.py:35
  26.4 5.8 %collective-permute-start.5 = (f32[80,128]{1,0:T(8,128)S(1)}, f32[80,128]{1,0:T(8,128)S(1)}, u32[]{:S(2)}, u32[]{:S(2)}) collective-permute-start(f32[80,128]{1,0:T(8,128)S(1)} %get-tuple-element.24), channel_id=1, source_target_pairs={{0,12},{4,8},{8,4},{12,0},{1,13},{5,9},{9,5},{13,1},{2,14},{6,10},... | collective-permute-start | bytes 122888 | tf_op jit(solution)/shard_map/ppermute | solution.py:35
  32.2 1.6 %copy-start.4 = (bf16[2,2,2048,128]{3,2,1,0:T(8,128)(2,1)S(1)}, bf16[2,2,2048,128]{3,2,1,0:T(8,128)(2,1)}, u32[]{:S(2)}) copy-start(bf16[2,2,2048,128]{3,2,1,0:T(8,128)(2,1)} %cached_values.1) | copy-start | bytes 6291460
  36.1 5.7 %collective-permute-start.8 = (bf16[64,128]{1,0:T(8,128)(2,1)S(1)}, bf16[64,128]{1,0:T(8,128)(2,1)S(1)}, u32[]{:S(2)}, u32[]{:S(2)}) collective-permute-start(bf16[64,128]{1,0:T(8,128)(2,1)S(1)} %attend.1.refs_0_), channel_id=1, source_target_pairs={{0,12},{4,8},{8,4},{12,0},{1,13},{5,9},{9,5},{13,1},{2,14},{6,10},... | collective-permute-start | bytes 49160 | tf_op jit(solution)/shard_map/ppermute | solution.py:27
  37.0 5.0 %collective-permute-start.7 = (bf16[64,128]{1,0:T(8,128)(2,1)S(1)}, bf16[64,128]{1,0:T(8,128)(2,1)S(1)}, u32[]{:S(2)}, u32[]{:S(2)}) collective-permute-start(bf16[64,128]{1,0:T(8,128)(2,1)S(1)} %attend.1.refs_0_), channel_id=1, source_target_pairs={{0,8},{4,12},{8,0},{12,4},{1,9},{5,13},{9,1},{13,5},{2,10},{6,14},... | collective-permute-start | bytes 49160 | tf_op jit(solution)/shard_map/ppermute | solution.py:27
  37.0 5.2 %collective-permute-start.6 = (bf16[64,128]{1,0:T(8,128)(2,1)S(1)}, bf16[64,128]{1,0:T(8,128)(2,1)S(1)}, u32[]{:S(2)}, u32[]{:S(2)}) collective-permute-start(bf16[64,128]{1,0:T(8,128)(2,1)S(1)} %attend.1.refs_0_), channel_id=1, source_target_pairs={{0,4},{4,0},{8,12},{12,8},{1,5},{5,1},{9,13},{13,9},{2,6},{6,2},{1... | collective-permute-start | bytes 49160 | tf_op jit(solution)/shard_map/ppermute | solution.py:27
  42.2 10.5 %copy-start = (bf16[4096,4096]{1,0:T(8,128)(2,1)S(1)}, bf16[4096,4096]{1,0:T(8,128)(2,1)}, u32[]{:S(2)}) copy-start(bf16[4096,4096]{1,0:T(8,128)(2,1)} %w_out.1) | copy-start | bytes 100663296
  57.8 1.9 %collective-permute-start.9 = (f32[2,4096]{1,0:T(2,128)S(1)}, f32[2,4096]{1,0:T(2,128)S(1)}, u32[]{:S(2)}, u32[]{:S(2)}) collective-permute-start(f32[2,4096]{1,0:T(2,128)S(1)} %get-tuple-element.26), channel_id=1, source_target_pairs={{0,1},{1,0},{2,3},{3,2},{4,5},{5,4},{6,7},{7,6},{8,9},{9,8},{10,11... | collective-permute-start | bytes 98312 | tf_op jit(solution)/shard_map/ppermute | solution.py:35
  57.8 4.2 %collective-permute-start.10 = (f32[2,4096]{1,0:T(2,128)S(1)}, f32[2,4096]{1,0:T(2,128)S(1)}, u32[]{:S(2)}, u32[]{:S(2)}) collective-permute-start(f32[2,4096]{1,0:T(2,128)S(1)} %get-tuple-element.27), channel_id=1, source_target_pairs={{0,2},{1,3},{2,0},{3,1},{4,6},{5,7},{6,4},{7,5},{8,10},{9,11},{10,... | collective-permute-start | bytes 98312 | tf_op jit(solution)/shard_map/ppermute | solution.py:35
  58.6 3.7 %collective-permute-start.11 = (f32[2,4096]{1,0:T(2,128)S(1)}, f32[2,4096]{1,0:T(2,128)S(1)}, u32[]{:S(2)}, u32[]{:S(2)}) collective-permute-start(f32[2,4096]{1,0:T(2,128)S(1)} %get-tuple-element.28), channel_id=1, source_target_pairs={{0,3},{1,2},{2,1},{3,0},{4,7},{5,6},{6,5},{7,4},{8,11},{9,10},{10,... | collective-permute-start | bytes 98312 | tf_op jit(solution)/shard_map/ppermute | solution.py:35

commit v2 on v1

--- a/solution.py
+++ b/solution.py
@@ -38,7 +38,7 @@
 
 
 def peer(me, t, count):
-    return me ^ t if direct(count) else t
+    return lax.bitwise_xor(me, t) if direct(count) else jnp.int32(t)
 
 
 def vmem():
@@ -50,10 +50,10 @@
 
 
 def project_kernel(
-    places, w_query, key_weight, value_weight, *refs, pieces, heads, kv, stride, depth, slots
+    w_query, key_weight, value_weight, *refs, pieces, heads, kv, stride, depth, slots, place
 ):
     inputs, refs = refs[:pieces], refs[pieces:]
-    outs, (rows, total, laid, held, sems) = refs[:-5], refs[-5:]
+    outs, (rows, total, laid, held, fresh_held, sems, fresh_sems) = refs[:-7], refs[-7:]
     width, columns = w_query.shape
     chunks = width // depth
 
@@ -62,6 +62,12 @@
             w_query.at[pl.ds(i * depth, depth)], held.at[i % slots], sems.at[i % slots]
         )
 
+    fresh_copies = [
+        pltpu.make_async_copy(w, fresh_held.at[i], fresh_sems.at[i])
+        for i, w in enumerate((key_weight, value_weight))
+    ]
+    for c in fresh_copies:
+        c.start()
     for i in range(min(slots, chunks)):
         copy(i).start()
     rows[...] = jnp.concatenate([p[...].astype(jnp.float32) for p in inputs], 0).astype(
@@ -69,10 +75,10 @@
     )
     count = rows.shape[0]
     group = min(8, count)
-    fresh = [
-        jnp.dot(rows[...], w[...], preferred_element_type=jnp.float32)
-        for w in (key_weight, value_weight)
-    ]
+    fresh = []
+    for i, c in enumerate(fresh_copies):
+        c.wait()
+        fresh.append(jnp.dot(rows[...], fresh_held[i], preferred_element_type=jnp.float32))
     for i in range(chunks):
         copy(i).wait()
         term = jnp.dot(
@@ -92,16 +98,15 @@
                 block = fresh[which][base : base + group, j * LANES : (j + 1) * LANES]
             laid[pl.ds(base * stride + h, group, stride=stride), :] = block
     for t, out in enumerate(outs):
-        out[...] = laid[pl.ds(pl.multiple_of(places[t] * stride, 8), out.shape[0]), :]
-
-
-def project(places, hidden_pieces, w_query, key_weight, value_weight, row_count, heads, kv):
+        out[...] = laid[pl.ds(pl.multiple_of(place(t) * stride, 8), out.shape[0]), :]
+
+
+def project(place, hidden_pieces, w_query, key_weight, value_weight, targets, row_count, heads, kv):
     stride = -(-(heads + 2 * kv) // 8) * 8
     width, columns = w_query.shape
     depth = min(256, width)
-    slots = 8
+    slots = 6
     count = sum(p.shape[0] for p in hidden_pieces)
-    targets = places.shape[0]
     return pl.pallas_call(
         functools.partial(
             project_kernel,
@@ -111,28 +116,27 @@
             stride=stride,
             depth=depth,
             slots=slots,
+            place=place,
         ),
         out_shape=[jax.ShapeDtypeStruct((row_count * stride, LANES), jnp.float32)] * targets,
-        in_specs=[smem(), pl.BlockSpec(memory_space=pl.ANY)]
-        + [vmem()] * (2 + len(hidden_pieces)),
+        in_specs=[pl.BlockSpec(memory_space=pltpu.HBM)] * 3 + [vmem()] * len(hidden_pieces),
         out_specs=[vmem()] * targets,
         scratch_shapes=[
             pltpu.VMEM((count, width), jnp.bfloat16),
             pltpu.VMEM((count, columns), jnp.float32),
             pltpu.VMEM((count * stride, LANES), jnp.float32),
             pltpu.VMEM((slots, depth, columns), jnp.bfloat16),
+            pltpu.VMEM((2,) + key_weight.shape, jnp.bfloat16),
             pltpu.SemaphoreType.DMA((slots,)),
+            pltpu.SemaphoreType.DMA((2,)),
         ],
-        compiler_params=pltpu.CompilerParams(vmem_limit_bytes=24 * MIB),
+        compiler_params=pltpu.CompilerParams(vmem_limit_bytes=18 * MIB),
         cost_estimate=pl.CostEstimate(
             flops=1000, bytes_accessed=1000, transcendentals=0
         ),
         name="project",
     )(
-        places,
-        pltpu.with_memory_space_constraint(w_query, pltpu.HBM),
-        pltpu.with_memory_space_constraint(key_weight, pltpu.VMEM),
-        pltpu.with_memory_space_constraint(value_weight, pltpu.VMEM),
+        *(pltpu.with_memory_space_constraint(w, pltpu.HBM) for w in (w_query, key_weight, value_weight)),
         *hidden_pieces,
     )
 
@@ -149,7 +153,7 @@
         out_shape=[jax.ShapeDtypeStruct(a.shape, a.dtype) for a in arrays],
         in_specs=[vmem()] * len(arrays),
         out_specs=[vmem()] * len(arrays),
-        compiler_params=pltpu.CompilerParams(vmem_limit_bytes=8 * MIB),
+        compiler_params=pltpu.CompilerParams(vmem_limit_bytes=2 * MIB),
         cost_estimate=pl.CostEstimate(
             flops=int(microseconds * 1.15e9), bytes_accessed=1 << 16, transcendentals=0
         ),
@@ -212,24 +216,23 @@
         out_shape=jax.ShapeDtypeStruct((row_count * heads, LANES), jnp.bfloat16),
         in_specs=[smem()] + [vmem()] * (4 + len(parts)),
         out_specs=vmem(),
-        compiler_params=pltpu.CompilerParams(vmem_limit_bytes=16 * MIB),
+        compiler_params=pltpu.CompilerParams(vmem_limit_bytes=6 * MIB),
         cost_estimate=pl.CostEstimate(flops=1000, bytes_accessed=1000, transcendentals=0),
         name="attend",
     )(
         lengths,
         cosine,
         sine,
-        pltpu.with_memory_space_constraint(key_cache, pltpu.VMEM),
-        pltpu.with_memory_space_constraint(cached_values, pltpu.VMEM),
+        key_cache,
+        cached_values,
         *parts,
     )
 
 
-def output_kernel(places, w_out, *refs, pieces, heads, rows_out):
-    inputs, refs = refs[:pieces], refs[pieces:]
-    outs, (laid, rows, total) = refs[:-3], refs[-3:]
+def arrange_kernel(*refs, pieces, heads, place):
+    inputs, (rows, laid, total) = refs[:pieces], refs[pieces:]
     for t, piece in enumerate(inputs):
-        laid[places[t]] = piece[...].astype(jnp.float32)
+        laid[place(t)] = piece[...].astype(jnp.float32)
     flat = laid.reshape(laid.shape[0] * laid.shape[1], LANES)
     count = rows.shape[0]
     group = min(8, count)
@@ -239,6 +242,26 @@
                 pl.ds(base * heads + h, group, stride=heads), :
             ]
     rows[...] = total[...].astype(jnp.bfloat16)
+
+
+def arrange(place, pieces, row_count, heads):
+    count = row_count * len(pieces)
+    return pl.pallas_call(
+        functools.partial(arrange_kernel, pieces=len(pieces), heads=heads, place=place),
+        out_shape=jax.ShapeDtypeStruct((count, heads * LANES), jnp.bfloat16),
+        in_specs=[vmem()] * len(pieces),
+        out_specs=vmem(),
+        scratch_shapes=[
+            pltpu.VMEM((len(pieces), row_count * heads, LANES), jnp.float32),
+            pltpu.VMEM((count, heads * LANES), jnp.float32),
+        ],
+        compiler_params=pltpu.CompilerParams(vmem_limit_bytes=6 * MIB),
+        cost_estimate=pl.CostEstimate(flops=1000, bytes_accessed=1000, transcendentals=0),
+        name="arrange",
+    )(*pieces)
+
+
+def output_kernel(rows, w_out, *outs, rows_out):
     columns = w_out.shape[1]
     step = min(1024, columns)
     for j in range(0, columns, step):
@@ -247,23 +270,17 @@
             out[:, j : j + step] = sums[s * rows_out : (s + 1) * rows_out, :]
 
 
-def output(places, pieces, w_out, row_count, heads, rows_out, targets):
-    count = row_count * len(pieces)
-    width, columns = w_out.shape
-    return pl.pallas_call(
-        functools.partial(output_kernel, pieces=len(pieces), heads=heads, rows_out=rows_out),
+def output(rows, w_out, rows_out, targets):
+    columns = w_out.shape[1]
+    return pl.pallas_call(
+        functools.partial(output_kernel, rows_out=rows_out),
         out_shape=[jax.ShapeDtypeStruct((rows_out, columns), jnp.float32)] * targets,
-        in_specs=[smem()] + [vmem()] * (1 + len(pieces)),
+        in_specs=[vmem()] * 2,
         out_specs=[vmem()] * targets,
-        scratch_shapes=[
-            pltpu.VMEM((len(pieces), row_count * heads, LANES), jnp.float32),
-            pltpu.VMEM((count, width), jnp.bfloat16),
-            pltpu.VMEM((count, max(width, columns)), jnp.float32),
-        ],
-        compiler_params=pltpu.CompilerParams(vmem_limit_bytes=16 * MIB),
+        compiler_params=pltpu.CompilerParams(vmem_limit_bytes=20 * MIB),
         cost_estimate=pl.CostEstimate(flops=1000, bytes_accessed=1000, transcendentals=0),
         name="output",
-    )(places, pltpu.with_memory_space_constraint(w_out, pltpu.VMEM), *pieces)
+    )(rows, w_out)
 
 
 def rotation(lengths, head_dim):
@@ -291,35 +308,36 @@
     row_count, kv, _, head_dim = key_cache.shape
     heads = w_query.shape[1] // head_dim
     rows_out = hidden.shape[0]
-    me_wide, me_narrow = lax.axis_index("wide"), lax.axis_index("narrow")
     blocks = rows_out // row_count
+
+    def target(owner):
+        first, rest = lax.div(owner, blocks), lax.rem(owner, blocks)
+        if direct(narrow):
+            first = lax.bitwise_xor(lax.axis_index("narrow"), first)
+        return first * blocks + rest
+
+    def place(t):
+        return target(peer(lax.axis_index("wide"), t, wide))
 
     cosine, sine = rotation(lengths, head_dim)
     hidden_pieces = gather_pieces(hidden, "narrow", narrow)
-
-    starts = []
-    for t in range(wide):
-        first = peer(me_wide, t, wide) * row_count
-        place = first // rows_out
-        place = me_narrow ^ place if direct(narrow) else place
-        starts.append(place * rows_out + first % rows_out)
-    starts = jnp.stack(starts).astype(jnp.int32)
     parts = project(
-        starts, hidden_pieces, w_query, key_weight, value_weight, row_count, heads, kv
-    )
-    parts = relay(parts, 100)
+        lambda t: place(t) * row_count,
+        hidden_pieces,
+        w_query,
+        key_weight,
+        value_weight,
+        wide,
+        row_count,
+        heads,
+        kv,
+    )
+    *parts, cosine, sine = relay([*parts, cosine, sine], 100)
     parts = scatter_pieces(parts, "wide", wide)
     context = attend(lengths, cosine, sine, key_cache, cached_values, parts, heads, kv)
     context_pieces = gather_pieces(context, "wide", wide)
-
-    spots = []
-    for t in range(wide):
-        owner = peer(me_wide, t, wide)
-        target = owner // blocks
-        target = me_narrow ^ target if direct(narrow) else target
-        spots.append(target * blocks + owner % blocks)
-    spots = jnp.stack(spots).astype(jnp.int32)
-    sums = output(spots, context_pieces, w_out, row_count, heads, rows_out, narrow)
+    rows = arrange(place, context_pieces, row_count, heads)
+    sums = output(rows, w_out, rows_out, narrow)
     sums = scatter_pieces(sums, "narrow", narrow)
     result = sums[0]
     for s in sums[1:]:

time: 63.2 us -> 49.7 us (0.79)
  local copies, waits for them, and re-layouts: 16 us -> 0.78 us
  Pallas kernels: 19.2 us -> 20.8 us
    unnamed x14 -> x24, local copies, waits for them, and re-layouts: 16 us -> 0.78 us
    pallas_call x1, Pallas kernels: 11.9 us -> 14 us  [project(): pl.pallas_call(functools.partial(project_kernel, pieces=len(hidden_pieces...]
    pallas_call x1 -> x2, Pallas kernels: 4.99 us -> 4.53 us  [the longest x1 4.44 us: output(): pl.pallas_call(functools.partial(output_kernel, rows_out=rows_out), out_s...]
where the time goes in v2:
time: 49.7 us; the launch traced here: 49.4 us
  Pallas kernels  20.8 us (42%)
  starting transfers between devices  13.8 us (28%)
  waiting for transfers between devices  12.3 us (25%)
  other arithmetic  1.5 us (3%)
  local copies, waits for them, and re-layouts  0.78 us (2%)
    pallas_call x1, Pallas kernels, project(): pl.pallas_call(functools.partial(project_kernel, pieces=len(hidden_pieces...  14 us
    ppermute x6, waiting for transfers between devices, scatter_pieces(): lax.ppermute(pieces[t], axis, xor_pairs(count, t))  8.16 us
    ppermute x6, starting transfers between devices, gather_pieces(): lax.ppermute(piece, axis, xor_pairs(count, t))  7.51 us
    ppermute x6, starting transfers between devices, scatter_pieces(): lax.ppermute(pieces[t], axis, xor_pairs(count, t))  6.32 us
    pallas_call x1, Pallas kernels, output(): pl.pallas_call(functools.partial(output_kernel, rows_out=rows_out), out_s...  4.44 us
    ppermute x6, waiting for transfers between devices, gather_pieces(): lax.ppermute(piece, axis, xor_pairs(count, t))  4.11 us
    pallas_call x1, Pallas kernels, attend(): pl.pallas_call(functools.partial(attend_kernel, heads=heads, kv=kv, strid...  2.29 us
  transfers between devices with their start and end apart: 12, of which 9 were waited for; matrix products, arithmetic and copies ran while one was open for 2% of the time, Pallas kernels for 0%

profile of v2, /device:TPU:0, one launch (start us, length us, event | category | flops | bytes accessed | tf_op | source)
XLA Modules:
  0.0 49.4 jit_solution(9374091406624234278)
XLA Ops:
  0.0 2.9 %collective-permute-start.1 = (bf16[2,4096]{1,0:T(2,128)(2,1)}, bf16[2,4096]{1,0:T(2,128)(2,1)S(1)}, u32[]{:S(2)}, u32[]{:S(2)}) collective-permute-start(bf16[2,4096]{1,0:T(2,128)(2,1)} %refs_0_.1), channel_id=1, source_target_pairs={{0,2},{1,3},{2,0},{3,1},{4,6},{5,7},{6,4},{7,5},{8,10},{9,11},{10,... | collective-permute-start | bytes 49160 | tf_op jit(solution)/shard_map/ppermute | solution.py:27
  2.9 0.1 collective-permute-start.2
  3.1 0.7 %convert_element_type.6 = f32[2]{0:T(128)S(1)} convert(s32[2]{0:T(128)} %lengths.1) | non-fusion elementwise | flops 2 | bytes 16 | tf_op jit(solution)/shard_map/convert_element_type | solution.py:290
  3.9 0.9 %collective-permute-done.1.refs_2_ = bf16[2,4096]{1,0:T(2,128)(2,1)S(1)} collective-permute-done((bf16[2,4096]{1,0:T(2,128)(2,1)}, bf16[2,4096]{1,0:T(2,128)(2,1)S(1)}, u32[]{:S(2)}, u32[]{:S(2)}) %collective-permute-start.1) | collective-permute-done | bytes 16416 | tf_op jit(solution)/shard_map/ppermute | solution.py:27
  4.9 1.4 %collective-permute-done.2.refs_3_ = bf16[2,4096]{1,0:T(2,128)(2,1)S(1)} collective-permute-done((bf16[2,4096]{1,0:T(2,128)(2,1)}, bf16[2,4096]{1,0:T(2,128)(2,1)S(1)}, u32[]{:S(2)}, u32[]{:S(2)}) %collective-permute-start.2) | collective-permute-done | bytes 16416 | tf_op jit(solution)/shard_map/ppermute | solution.py:27
  6.3 0.7 %copy-done.2 = bf16[2,4096]{1,0:T(2,128)(2,1)S(1)} copy-done((bf16[2,4096]{1,0:T(2,128)(2,1)S(1)}, bf16[2,4096]{1,0:T(2,128)(2,1)}, u32[]{:S(2)}) %copy-start.2) | copy-done | bytes 16408
  7.0 14.0 %project.1 = (f32[80,128]{1,0:T(8,128)S(1)}, f32[80,128]{1,0:T(8,128)S(1)}, f32[80,128]{1,0:T(8,128)S(1)}, f32[80,128]{1,0:T(8,128)S(1)}) custom-call(bf16[4096,4096]{1,0:T(8,128)(2,1)} %w_query.1, bf16[4096,256]{1,0:T(8,128)(2,1)} %key_weight.1, bf16[4096,256]{1,0:T(8,128)(2,1)} %value_weight.1, bf16[2,4096]{1,0:T(2,128)(2,1)S(1)} %copy-done.2, ...), custom_call_target="tpu_custom_call" | custom-call | flops 1000 | bytes 1000 | tf_op jit(solution)/shard_map/project/pallas_call | solution.py:110
  21.2 1.6 %collective-permute-start.3 = (f32[80,128]{1,0:T(8,128)S(1)}, f32[80,128]{1,0:T(8,128)S(1)}, u32[]{:S(2)}, u32[]{:S(2)}) collective-permute-start(f32[80,128]{1,0:T(8,128)S(1)} %get-tuple-element.26), channel_id=1, source_target_pairs={{0,4},{4,0},{8,12},{12,8},{1,5},{5,1},{9,13},{13,9},{2,6},{6,2},{1... | collective-permute-start | bytes 122888 | tf_op jit(solution)/shard_map/ppermute | solution.py:35
  22.8 2.6 %collective-permute-start.4 = (f32[80,128]{1,0:T(8,128)S(1)}, f32[80,128]{1,0:T(8,128)S(1)}, u32[]{:S(2)}, u32[]{:S(2)}) collective-permute-start(f32[80,128]{1,0:T(8,128)S(1)} %get-tuple-element.27), channel_id=1, source_target_pairs={{0,8},{4,12},{8,0},{12,4},{1,9},{5,13},{9,1},{13,5},{2,10},{6,14},... | collective-permute-start | bytes 122888 | tf_op jit(solution)/shard_map/ppermute | solution.py:35
  25.4 0.2 collective-permute-start.5
  25.7 3.0 %collective-permute-done.4.refs_2_ = f32[80,128]{1,0:T(8,128)S(1)} collective-permute-done((f32[80,128]{1,0:T(8,128)S(1)}, f32[80,128]{1,0:T(8,128)S(1)}, u32[]{:S(2)}, u32[]{:S(2)}) %collective-permute-start.4) | collective-permute-done | bytes 40992 | tf_op jit(solution)/shard_map/ppermute | solution.py:35
  28.7 2.6 %collective-permute-done.5.refs_3_ = f32[80,128]{1,0:T(8,128)S(1)} collective-permute-done((f32[80,128]{1,0:T(8,128)S(1)}, f32[80,128]{1,0:T(8,128)S(1)}, u32[]{:S(2)}, u32[]{:S(2)}) %collective-permute-start.5) | collective-permute-done | bytes 40992 | tf_op jit(solution)/shard_map/ppermute | solution.py:35
  31.2 2.3 %attend.1.refs_0_ = bf16[64,128]{1,0:T(8,128)(2,1)S(1)} custom-call(s32[2]{0:T(128)S(1)} %copy-done.3, f32[2,128]{1,0:T(2,128)S(1)} %get-tuple-element.23.cosine, f32[2,128]{1,0:T(2,128)S(1)} %get-tuple-element.24.sine, bf16[2,2,2048,128]{3,2,1,0:T(8,128)(2,1)S(1)} %copy-done, bf16[2,2,2048,128]{3,2,1,0:T(8,128)(2,1)S(1)} %copy-done.1, ...), custom_call_target="tpu_custom_call" | custom-call | flops 1000 | bytes 1000 | tf_op jit(solution)/shard_map/attend/pallas_call | solution.py:214
  33.5 1.0 %collective-permute-start.8 = (bf16[64,128]{1,0:T(8,128)(2,1)S(1)}, bf16[64,128]{1,0:T(8,128)(2,1)S(1)}, u32[]{:S(2)}, u32[]{:S(2)}) collective-permute-start(bf16[64,128]{1,0:T(8,128)(2,1)S(1)} %attend.1.refs_0_), channel_id=1, source_target_pairs={{0,12},{4,8},{8,4},{12,0},{1,13},{5,9},{9,5},{13,1},{2,14},{6,10},... | collective-permute-start | bytes 49160 | tf_op jit(solution)/shard_map/ppermute | solution.py:27
  34.5 3.5 %collective-permute-start.6 = (bf16[64,128]{1,0:T(8,128)(2,1)S(1)}, bf16[64,128]{1,0:T(8,128)(2,1)S(1)}, u32[]{:S(2)}, u32[]{:S(2)}) collective-permute-start(bf16[64,128]{1,0:T(8,128)(2,1)S(1)} %attend.1.refs_0_), channel_id=1, source_target_pairs={{0,4},{4,0},{8,12},{12,8},{1,5},{5,1},{9,13},{13,9},{2,6},{6,2},{1... | collective-permute-start | bytes 49160 | tf_op jit(solution)/shard_map/ppermute | solution.py:27
  38.0 1.2 %collective-permute-done.8.refs_3_ = bf16[64,128]{1,0:T(8,128)(2,1)S(1)} collective-permute-done((bf16[64,128]{1,0:T(8,128)(2,1)S(1)}, bf16[64,128]{1,0:T(8,128)(2,1)S(1)}, u32[]{:S(2)}, u32[]{:S(2)}) %collective-permute-start.8) | collective-permute-done | bytes 16416 | tf_op jit(solution)/shard_map/ppermute | solution.py:27
  39.2 0.2 collective-permute-done.7.refs_2_
  39.5 0.2 collective-permute-done.6.refs_1_
  39.9 4.4 %output.1 = (f32[2,4096]{1,0:T(2,128)S(1)}, f32[2,4096]{1,0:T(2,128)S(1)}, f32[2,4096]{1,0:T(2,128)S(1)}, f32[2,4096]{1,0:T(2,128)S(1)}) custom-call(bf16[8,4096]{1,0:T(8,128)(2,1)S(1)} %arrange.1.rows, bf16[4096,4096]{1,0:T(8,128)(2,1)S(1)} %bitcast.1), custom_call_target="tpu_custom_call" | custom-call | flops 1000 | bytes 1000 | tf_op jit(solution)/shard_map/output/pallas_call | solution.py:275
  44.3 0.8 %collective-permute-start.10 = (f32[2,4096]{1,0:T(2,128)S(1)}, f32[2,4096]{1,0:T(2,128)S(1)}, u32[]{:S(2)}, u32[]{:S(2)}) collective-permute-start(f32[2,4096]{1,0:T(2,128)S(1)} %get-tuple-element.31), channel_id=1, source_target_pairs={{0,2},{1,3},{2,0},{3,1},{4,6},{5,7},{6,4},{7,5},{8,10},{9,11},{10,... | collective-permute-start | bytes 98312 | tf_op jit(solution)/shard_map/ppermute | solution.py:35
  45.1 1.1 %collective-permute-start.11 = (f32[2,4096]{1,0:T(2,128)S(1)}, f32[2,4096]{1,0:T(2,128)S(1)}, u32[]{:S(2)}, u32[]{:S(2)}) collective-permute-start(f32[2,4096]{1,0:T(2,128)S(1)} %get-tuple-element.32), channel_id=1, source_target_pairs={{0,3},{1,2},{2,1},{3,0},{4,7},{5,6},{6,5},{7,4},{8,11},{9,10},{10,... | collective-permute-start | bytes 98312 | tf_op jit(solution)/shard_map/ppermute | solution.py:35
  46.2 2.3 %collective-permute-done.10 = f32[2,4096]{1,0:T(2,128)S(1)} collective-permute-done((f32[2,4096]{1,0:T(2,128)S(1)}, f32[2,4096]{1,0:T(2,128)S(1)}, u32[]{:S(2)}, u32[]{:S(2)}) %collective-permute-start.10) | collective-permute-done | bytes 32800 | tf_op jit(solution)/shard_map/ppermute | solution.py:35
  48.5 0.3 collective-permute-done.11
  48.8 0.6 %add_convert_fusion = bf16[2,4096]{1,0:T(2,128)(2,1)} fusion(f32[2,4096]{1,0:T(2,128)S(1)} %collective-permute-done.11, f32[2,4096]{1,0:T(2,128)S(1)} %collective-permute-done.10, f32[2,4096]{1,0:T(2,128)S(1)} %get-tuple-element.29, f32[2,4096]{1,0:T(2,128)S(1)} %collective-permute-done.9), kind=kLoop, calls=%fused_computation | loop fusion | flops 32768 | bytes 147456 | tf_op jit(solution)/shard_map/convert_element_type | solution.py:345
  (35 shorter events, 0.4 us)
Async XLA Ops:
  0.0 4.9 %collective-permute-start.1 = (bf16[2,4096]{1,0:T(2,128)(2,1)}, bf16[2,4096]{1,0:T(2,128)(2,1)S(1)}, u32[]{:S(2)}, u32[]{:S(2)}) collective-permute-start(bf16[2,4096]{1,0:T(2,128)(2,1)} %refs_0_.1), channel_id=1, source_target_pairs={{0,2},{1,3},{2,0},{3,1},{4,6},{5,7},{6,4},{7,5},{8,10},{9,11},{10,... | collective-permute-start | bytes 49160 | tf_op jit(solution)/shard_map/ppermute | solution.py:27
  2.9 1.9 %collective-permute-start = (bf16[2,4096]{1,0:T(2,128)(2,1)}, bf16[2,4096]{1,0:T(2,128)(2,1)S(1)}, u32[]{:S(2)}, u32[]{:S(2)}) collective-permute-start(bf16[2,4096]{1,0:T(2,128)(2,1)} %refs_0_.1), channel_id=1, source_target_pairs={{0,1},{1,0},{2,3},{3,2},{4,5},{5,4},{6,7},{7,6},{8,9},{9,8},{10,11... | collective-permute-start | bytes 49160 | tf_op jit(solution)/shard_map/ppermute | solution.py:27
  2.9 3.4 %collective-permute-start.2 = (bf16[2,4096]{1,0:T(2,128)(2,1)}, bf16[2,4096]{1,0:T(2,128)(2,1)S(1)}, u32[]{:S(2)}, u32[]{:S(2)}) collective-permute-start(bf16[2,4096]{1,0:T(2,128)(2,1)} %refs_0_.1), channel_id=1, source_target_pairs={{0,3},{1,2},{2,1},{3,0},{4,7},{5,6},{6,5},{7,4},{8,11},{9,10},{10,... | collective-permute-start | bytes 49160 | tf_op jit(solution)/shard_map/ppermute | solution.py:27
  6.3 0.7 %copy-start.2 = (bf16[2,4096]{1,0:T(2,128)(2,1)S(1)}, bf16[2,4096]{1,0:T(2,128)(2,1)}, u32[]{:S(2)}) copy-start(bf16[2,4096]{1,0:T(2,128)(2,1)} %refs_0_.1) | copy-start | bytes 49156
  7.0 32.8 %slice-start = ((s8[33554432]{0:T(1024)(128)(4,1)}), s8[4194304]{0:T(1024)(128)(4,1)S(1)}, s32[]{:S(2)}) async-start(s8[33554432]{0:T(1024)(128)(4,1)} %bitcast), calls=%async_computation | async-start | bytes 8388608
  21.1 10.2 %copy-start = (bf16[2,2,2048,128]{3,2,1,0:T(8,128)(2,1)S(1)}, bf16[2,2,2048,128]{3,2,1,0:T(8,128)(2,1)}, u32[]{:S(2)}) copy-start(bf16[2,2,2048,128]{3,2,1,0:T(8,128)(2,1)} %key_cache.1) | copy-start | bytes 6291460
  21.1 10.2 %copy-start.1 = (bf16[2,2,2048,128]{3,2,1,0:T(8,128)(2,1)S(1)}, bf16[2,2,2048,128]{3,2,1,0:T(8,128)(2,1)}, u32[]{:S(2)}) copy-start(bf16[2,2,2048,128]{3,2,1,0:T(8,128)(2,1)} %cached_values.1) | copy-start | bytes 6291460
  21.1 10.2 %copy-start.3 = (s32[2]{0:T(128)S(1)}, s32[2]{0:T(128)}, u32[]{:S(2)}) copy-start(s32[2]{0:T(128)} %lengths.1) | copy-start | bytes 28
  21.1 18.7 %slice-start.1 = ((s8[33554432]{0:T(1024)(128)(4,1)}), s8[4194304]{0:T(1024)(128)(4,1)S(1)}, s32[]{:S(2)}) async-start(s8[33554432]{0:T(1024)(128)(4,1)} %bitcast), calls=%async_computation.1 | async-start | bytes 8388608
  21.1 18.7 %slice-start.2 = ((s8[33554432]{0:T(1024)(128)(4,1)}), s8[4194304]{0:T(1024)(128)(4,1)S(1)}, s32[]{:S(2)}) async-start(s8[33554432]{0:T(1024)(128)(4,1)} %bitcast), calls=%async_computation.2 | async-start | bytes 8388608
  21.1 18.7 %slice-start.3 = ((s8[33554432]{0:T(1024)(128)(4,1)}), s8[4194304]{0:T(1024)(128)(4,1)S(1)}, s32[]{:S(2)}) async-start(s8[33554432]{0:T(1024)(128)(4,1)} %bitcast), calls=%async_computation.3 | async-start | bytes 8388608
  21.1 18.7 %slice-start.4 = ((s8[33554432]{0:T(1024)(128)(4,1)}), s8[4194304]{0:T(1024)(128)(4,1)S(1)}, s32[]{:S(2)}) async-start(s8[33554432]{0:T(1024)(128)(4,1)} %bitcast), calls=%async_computation.4 | async-start | bytes 8388608
  21.1 18.7 %slice-start.5 = ((s8[33554432]{0:T(1024)(128)(4,1)}), s8[4194304]{0:T(1024)(128)(4,1)S(1)}, s32[]{:S(2)}) async-start(s8[33554432]{0:T(1024)(128)(4,1)} %bitcast), calls=%async_computation.5 | async-start | bytes 8388608
  21.2 18.7 %slice-start.6 = ((s8[33554432]{0:T(1024)(128)(4,1)}), s8[4194304]{0:T(1024)(128)(4,1)S(1)}, s32[]{:S(2)}) async-start(s8[33554432]{0:T(1024)(128)(4,1)} %bitcast), calls=%async_computation.6 | async-start | bytes 8388608
  21.2 18.7 %slice-start.7 = ((s8[33554432]{0:T(1024)(128)(4,1)}), s8[4194304]{0:T(1024)(128)(4,1)S(1)}, s32[]{:S(2)}) async-start(s8[33554432]{0:T(1024)(128)(4,1)} %bitcast), calls=%async_computation.7 | async-start | bytes 8388608
  21.2 4.5 %collective-permute-start.3 = (f32[80,128]{1,0:T(8,128)S(1)}, f32[80,128]{1,0:T(8,128)S(1)}, u32[]{:S(2)}, u32[]{:S(2)}) collective-permute-start(f32[80,128]{1,0:T(8,128)S(1)} %get-tuple-element.26), channel_id=1, source_target_pairs={{0,4},{4,0},{8,12},{12,8},{1,5},{5,1},{9,13},{13,9},{2,6},{6,2},{1... | collective-permute-start | bytes 122888 | tf_op jit(solution)/shard_map/ppermute | solution.py:35
  22.8 5.8 %collective-permute-start.4 = (f32[80,128]{1,0:T(8,128)S(1)}, f32[80,128]{1,0:T(8,128)S(1)}, u32[]{:S(2)}, u32[]{:S(2)}) collective-permute-start(f32[80,128]{1,0:T(8,128)S(1)} %get-tuple-element.27), channel_id=1, source_target_pairs={{0,8},{4,12},{8,0},{12,4},{1,9},{5,13},{9,1},{13,5},{2,10},{6,14},... | collective-permute-start | bytes 122888 | tf_op jit(solution)/shard_map/ppermute | solution.py:35
  25.4 5.8 %collective-permute-start.5 = (f32[80,128]{1,0:T(8,128)S(1)}, f32[80,128]{1,0:T(8,128)S(1)}, u32[]{:S(2)}, u32[]{:S(2)}) collective-permute-start(f32[80,128]{1,0:T(8,128)S(1)} %get-tuple-element.28), channel_id=1, source_target_pairs={{0,12},{4,8},{8,4},{12,0},{1,13},{5,9},{9,5},{13,1},{2,14},{6,10},... | collective-permute-start | bytes 122888 | tf_op jit(solution)/shard_map/ppermute | solution.py:35
  33.5 5.7 %collective-permute-start.8 = (bf16[64,128]{1,0:T(8,128)(2,1)S(1)}, bf16[64,128]{1,0:T(8,128)(2,1)S(1)}, u32[]{:S(2)}, u32[]{:S(2)}) collective-permute-start(bf16[64,128]{1,0:T(8,128)(2,1)S(1)} %attend.1.refs_0_), channel_id=1, source_target_pairs={{0,12},{4,8},{8,4},{12,0},{1,13},{5,9},{9,5},{13,1},{2,14},{6,10},... | collective-permute-start | bytes 49160 | tf_op jit(solution)/shard_map/ppermute | solution.py:27
  34.5 5.0 %collective-permute-start.7 = (bf16[64,128]{1,0:T(8,128)(2,1)S(1)}, bf16[64,128]{1,0:T(8,128)(2,1)S(1)}, u32[]{:S(2)}, u32[]{:S(2)}) collective-permute-start(bf16[64,128]{1,0:T(8,128)(2,1)S(1)} %attend.1.refs_0_), channel_id=1, source_target_pairs={{0,8},{4,12},{8,0},{12,4},{1,9},{5,13},{9,1},{13,5},{2,10},{6,14},... | collective-permute-start | bytes 49160 | tf_op jit(solution)/shard_map/ppermute | solution.py:27
  34.5 5.2 %collective-permute-start.6 = (bf16[64,128]{1,0:T(8,128)(2,1)S(1)}, bf16[64,128]{1,0:T(8,128)(2,1)S(1)}, u32[]{:S(2)}, u32[]{:S(2)}) collective-permute-start(bf16[64,128]{1,0:T(8,128)(2,1)S(1)} %attend.1.refs_0_), channel_id=1, source_target_pairs={{0,4},{4,0},{8,12},{12,8},{1,5},{5,1},{9,13},{13,9},{2,6},{6,2},{1... | collective-permute-start | bytes 49160 | tf_op jit(solution)/shard_map/ppermute | solution.py:27
  44.3 1.9 %collective-permute-start.9 = (f32[2,4096]{1,0:T(2,128)S(1)}, f32[2,4096]{1,0:T(2,128)S(1)}, u32[]{:S(2)}, u32[]{:S(2)}) collective-permute-start(f32[2,4096]{1,0:T(2,128)S(1)} %get-tuple-element.30), channel_id=1, source_target_pairs={{0,1},{1,0},{2,3},{3,2},{4,5},{5,4},{6,7},{7,6},{8,9},{9,8},{10,11... | collective-permute-start | bytes 98312 | tf_op jit(solution)/shard_map/ppermute | solution.py:35
  44.3 4.2 %collective-permute-start.10 = (f32[2,4096]{1,0:T(2,128)S(1)}, f32[2,4096]{1,0:T(2,128)S(1)}, u32[]{:S(2)}, u32[]{:S(2)}) collective-permute-start(f32[2,4096]{1,0:T(2,128)S(1)} %get-tuple-element.31), channel_id=1, source_target_pairs={{0,2},{1,3},{2,0},{3,1},{4,6},{5,7},{6,4},{7,5},{8,10},{9,11},{10,... | collective-permute-start | bytes 98312 | tf_op jit(solution)/shard_map/ppermute | solution.py:35
  45.1 3.7 %collective-permute-start.11 = (f32[2,4096]{1,0:T(2,128)S(1)}, f32[2,4096]{1,0:T(2,128)S(1)}, u32[]{:S(2)}, u32[]{:S(2)}) collective-permute-start(f32[2,4096]{1,0:T(2,128)S(1)} %get-tuple-element.32), channel_id=1, source_target_pairs={{0,3},{1,2},{2,1},{3,0},{4,7},{5,6},{6,5},{7,4},{8,11},{9,10},{10,... | collective-permute-start | bytes 98312 | tf_op jit(solution)/shard_map/ppermute | solution.py:35

commit v3 on v2

--- a/solution.py
+++ b/solution.py
@@ -11,6 +11,10 @@
 MIB = 1 << 20
 LANES = 128
 THETA = 500000.0
+HEAD_SHARE = 4
+LOADS = 4
+SLOTS = 6
+CUTS = 2
 DIRECT_PEERS = 8
 
 
@@ -31,9 +35,10 @@
 
 def scatter_pieces(pieces, axis, count):
     if direct(count):
-        return [pieces[0]] + [
-            lax.ppermute(pieces[t], axis, xor_pairs(count, t)) for t in range(1, count)
+        arrived = [
+            lax.ppermute(pieces[t], axis, xor_pairs(count, t)) for t in reversed(range(1, count))
         ]
+        return [pieces[0]] + arrived
     return [lax.psum_scatter(jnp.stack(pieces), axis, scatter_dimension=0, tiled=False)]
 
 
@@ -49,95 +54,143 @@
     return pl.BlockSpec(memory_space=pltpu.SMEM)
 
 
+def collect_kernel(*refs):
+    refs[-1][...] = jnp.concatenate([r[...].astype(jnp.float32) for r in refs[:-1]], 0).astype(
+        jnp.bfloat16
+    )
+
+
+def collect(pieces):
+    count = sum(p.shape[0] for p in pieces)
+    return pl.pallas_call(
+        collect_kernel,
+        out_shape=jax.ShapeDtypeStruct((count, pieces[0].shape[1]), jnp.bfloat16),
+        in_specs=[vmem()] * len(pieces),
+        out_specs=vmem(),
+        compiler_params=pltpu.CompilerParams(vmem_limit_bytes=6 * MIB),
+        cost_estimate=pl.CostEstimate(flops=1000, bytes_accessed=1000, transcendentals=0),
+        name="collect",
+    )(*pieces)
+
+
+def head_depth(w_query):
+    return w_query.shape[0] // HEAD_SHARE
+
+
+def load_kernel(w_query, key_weight, value_weight, head, sems):
+    del key_weight, value_weight
+    depth = head.shape[0] // LOADS
+    copies = [
+        pltpu.make_async_copy(
+            w_query.at[pl.ds(i * depth, depth)], head.at[pl.ds(i * depth, depth)], sems.at[i]
+        )
+        for i in range(LOADS)
+    ]
+    for copy in copies:
+        copy.start()
+    for copy in copies:
+        copy.wait()
+
+
+def load(w_query, key_weight, value_weight):
+    shape = (head_depth(w_query), w_query.shape[1])
+    return pl.pallas_call(
+        load_kernel,
+        out_shape=jax.ShapeDtypeStruct(shape, w_query.dtype),
+        in_specs=[pl.BlockSpec(memory_space=pltpu.HBM), vmem(), vmem()],
+        out_specs=vmem(),
+        scratch_shapes=[pltpu.SemaphoreType.DMA((LOADS,))],
+        compiler_params=pltpu.CompilerParams(vmem_limit_bytes=2 * MIB),
+        cost_estimate=pl.CostEstimate(
+            flops=1000, bytes_accessed=2 * math.prod(shape), transcendentals=0
+        ),
+        name="load",
+    )(pltpu.with_memory_space_constraint(w_query, pltpu.HBM), key_weight, value_weight)
+
+
 def project_kernel(
-    w_query, key_weight, value_weight, *refs, pieces, heads, kv, stride, depth, slots, place
+    rows, head, key_weight, value_weight, w_query, *refs, heads, kv, stride, place, depth, slots
 ):
-    inputs, refs = refs[:pieces], refs[pieces:]
-    outs, (rows, total, laid, held, fresh_held, sems, fresh_sems) = refs[:-7], refs[-7:]
-    width, columns = w_query.shape
-    chunks = width // depth
+    outs, (total, laid, held, sems) = refs[:-4], refs[-4:]
+    count, width = rows.shape
+    done = head.shape[0]
+    cut = held.shape[2]
+    cuts = w_query.shape[1] // cut
+    chunks = (width - done) // depth * cuts
+    group = min(8, count)
 
     def copy(i):
+        start, first = done + i // cuts * depth, i % cuts * cut
         return pltpu.make_async_copy(
-            w_query.at[pl.ds(i * depth, depth)], held.at[i % slots], sems.at[i % slots]
+            w_query.at[pl.ds(start, depth), pl.ds(first, cut)],
+            held.at[i % slots],
+            sems.at[i % slots],
         )
 
-    fresh_copies = [
-        pltpu.make_async_copy(w, fresh_held.at[i], fresh_sems.at[i])
-        for i, w in enumerate((key_weight, value_weight))
-    ]
-    for c in fresh_copies:
-        c.start()
+    def lay(sums, first):
+        for base in range(0, count, group):
+            for h in range(sums.shape[1] // LANES):
+                laid[pl.ds(base * stride + first + h, group, stride=stride), :] = sums[
+                    base : base + group, h * LANES : (h + 1) * LANES
+                ]
+
     for i in range(min(slots, chunks)):
         copy(i).start()
-    rows[...] = jnp.concatenate([p[...].astype(jnp.float32) for p in inputs], 0).astype(
-        jnp.bfloat16
-    )
-    count = rows.shape[0]
-    group = min(8, count)
-    fresh = []
-    for i, c in enumerate(fresh_copies):
-        c.wait()
-        fresh.append(jnp.dot(rows[...], fresh_held[i], preferred_element_type=jnp.float32))
+    half = width // 2
+    for i, w in enumerate((key_weight, value_weight)):
+        lay(
+            jnp.dot(rows[:, :half], w[:half], preferred_element_type=jnp.float32)
+            + jnp.dot(rows[:, half:], w[half:], preferred_element_type=jnp.float32),
+            heads + i * kv,
+        )
+    total[...] = jnp.dot(rows[:, :done], head[...], preferred_element_type=jnp.float32)
     for i in range(chunks):
         copy(i).wait()
-        term = jnp.dot(
-            rows[:, i * depth : (i + 1) * depth],
-            held[i % slots],
-            preferred_element_type=jnp.float32,
+        start, first = done + i // cuts * depth, i % cuts * cut
+        total[:, first : first + cut] += jnp.dot(
+            rows[:, start : start + depth], held[i % slots], preferred_element_type=jnp.float32
         )
-        total[...] = term if i == 0 else total[...] + term
         if i + slots < chunks:
             copy(i + slots).start()
-    for base in range(0, count, group):
-        for h in range(heads + 2 * kv):
-            if h < heads:
-                block = total[base : base + group, h * LANES : (h + 1) * LANES]
-            else:
-                which, j = divmod(h - heads, kv)
-                block = fresh[which][base : base + group, j * LANES : (j + 1) * LANES]
-            laid[pl.ds(base * stride + h, group, stride=stride), :] = block
+    lay(total, 0)
     for t, out in enumerate(outs):
         out[...] = laid[pl.ds(pl.multiple_of(place(t) * stride, 8), out.shape[0]), :]
 
 
-def project(place, hidden_pieces, w_query, key_weight, value_weight, targets, row_count, heads, kv):
+def project(place, rows, head, key_weight, value_weight, w_query, targets, row_count, heads, kv):
     stride = -(-(heads + 2 * kv) // 8) * 8
-    width, columns = w_query.shape
-    depth = min(256, width)
-    slots = 6
-    count = sum(p.shape[0] for p in hidden_pieces)
+    count, width = rows.shape
+    columns = w_query.shape[1]
+    depth = math.gcd(256, width - head.shape[0])
+    scratch = SLOTS * depth * (columns // CUTS) * 2 + count * (columns + stride * LANES) * 4
     return pl.pallas_call(
         functools.partial(
             project_kernel,
-            pieces=len(hidden_pieces),
             heads=heads,
             kv=kv,
             stride=stride,
+            place=place,
             depth=depth,
-            slots=slots,
-            place=place,
+            slots=SLOTS,
         ),
         out_shape=[jax.ShapeDtypeStruct((row_count * stride, LANES), jnp.float32)] * targets,
-        in_specs=[pl.BlockSpec(memory_space=pltpu.HBM)] * 3 + [vmem()] * len(hidden_pieces),
+        in_specs=[vmem()] * 4 + [pl.BlockSpec(memory_space=pltpu.HBM)],
         out_specs=[vmem()] * targets,
         scratch_shapes=[
-            pltpu.VMEM((count, width), jnp.bfloat16),
             pltpu.VMEM((count, columns), jnp.float32),
             pltpu.VMEM((count * stride, LANES), jnp.float32),
-            pltpu.VMEM((slots, depth, columns), jnp.bfloat16),
-            pltpu.VMEM((2,) + key_weight.shape, jnp.bfloat16),
-            pltpu.SemaphoreType.DMA((slots,)),
-            pltpu.SemaphoreType.DMA((2,)),
+            pltpu.VMEM((SLOTS, depth, columns // CUTS), jnp.bfloat16),
+            pltpu.SemaphoreType.DMA((SLOTS,)),
         ],
-        compiler_params=pltpu.CompilerParams(vmem_limit_bytes=18 * MIB),
-        cost_estimate=pl.CostEstimate(
-            flops=1000, bytes_accessed=1000, transcendentals=0
-        ),
+        compiler_params=pltpu.CompilerParams(vmem_limit_bytes=(scratch // MIB + 1 + count // 16) * MIB),
+        cost_estimate=pl.CostEstimate(flops=1000, bytes_accessed=1000, transcendentals=0),
         name="project",
     )(
-        *(pltpu.with_memory_space_constraint(w, pltpu.HBM) for w in (w_query, key_weight, value_weight)),
-        *hidden_pieces,
+        rows,
+        head,
+        key_weight,
+        value_weight,
+        pltpu.with_memory_space_constraint(w_query, pltpu.HBM),
     )
 
 
@@ -168,6 +221,8 @@
     scale = head_dim ** (-0.5)
     half = head_dim // 2
     position = lax.broadcasted_iota(jnp.int32, (per, slots), 1)
+    pairs = [(r, g) for r in range(row_count) for g in range(kv)]
+    queries, self_scores, values_new, scores = {}, {}, {}, {}
     for r in range(row_count):
         span = slice(r * stride, (r + 1) * stride)
         summed = parts[0][span, :]
@@ -176,36 +231,35 @@
         cos_row, sin_row = cosine[r : r + 1, :], sine[r : r + 1, :]
         turned = jnp.concatenate([summed[:, half:], summed[:, :half]], 1)
         rotated = (summed * cos_row + turned * sin_row).astype(jnp.bfloat16)
-        inside = position < lengths[r]
         for g in range(kv):
-            query = rotated[g * per : (g + 1) * per]
+            queries[r, g] = rotated[g * per : (g + 1) * per]
             key_new = rotated[heads + g : heads + g + 1].astype(jnp.float32)
-            value_new = summed[heads + kv + g : heads + kv + g + 1].astype(jnp.bfloat16)
-            scores = (
-                lax.dot_general(
-                    query,
-                    key_cache[r, g],
-                    (((1,), (1,)), ((), ())),
-                    preferred_element_type=jnp.float32,
-                )
-                * scale
+            self_scores[r, g] = (
+                jnp.sum(queries[r, g].astype(jnp.float32) * key_new, -1, keepdims=True) * scale
             )
-            self_score = jnp.sum(query.astype(jnp.float32) * key_new, -1, keepdims=True) * scale
-            masked = jnp.where(inside, scores, -jnp.inf)
-            highest = jnp.maximum(jnp.max(masked, -1, keepdims=True), self_score)
-            weights = jnp.exp(masked - highest)
-            self_weight = jnp.exp(self_score - highest)
-            denominator = jnp.sum(weights, -1, keepdims=True) + self_weight
-            mixed = jnp.dot(
-                weights.astype(jnp.bfloat16),
-                cached_values[r, g],
-                preferred_element_type=jnp.float32,
-            )
-            mixed = mixed + self_weight.astype(jnp.bfloat16).astype(
-                jnp.float32
-            ) * value_new.astype(jnp.float32)
-            start = r * heads + g * per
-            out[start : start + per, :] = (mixed / denominator).astype(jnp.bfloat16)
+            values_new[r, g] = summed[heads + kv + g : heads + kv + g + 1].astype(jnp.bfloat16)
+    for r, g in pairs:
+        scores[r, g] = lax.dot_general(
+            queries[r, g],
+            key_cache[r, g],
+            (((1,), (1,)), ((), ())),
+            preferred_element_type=jnp.float32,
+        )
+    weights, self_weights, denominators = {}, {}, {}
+    for r, g in pairs:
+        masked = jnp.where(position < lengths[r], scores[r, g] * scale, -jnp.inf)
+        highest = jnp.maximum(jnp.max(masked, -1, keepdims=True), self_scores[r, g])
+        raised = jnp.exp(masked - highest)
+        self_weight = jnp.exp(self_scores[r, g] - highest)
+        denominators[r, g] = jnp.sum(raised, -1, keepdims=True) + self_weight
+        weights[r, g] = raised.astype(jnp.bfloat16)
+        self_weights[r, g] = self_weight.astype(jnp.bfloat16).astype(jnp.float32)
+    for r, g in pairs:
+        mixed = jnp.dot(
+            weights[r, g], cached_values[r, g], preferred_element_type=jnp.float32
+        ) + self_weights[r, g] * values_new[r, g].astype(jnp.float32)
+        start = r * heads + g * per
+        out[start : start + per, :] = (mixed / denominators[r, g]).astype(jnp.bfloat16)
 
 
 def attend(lengths, cosine, sine, key_cache, cached_values, parts, heads, kv):
@@ -283,13 +337,31 @@
     )(rows, w_out)
 
 
-def rotation(lengths, head_dim):
-    half = head_dim // 2
-    exponents = jnp.arange(half, dtype=jnp.float32) * (2.0 / head_dim)
-    frequency = jnp.exp(-math.log(THETA) * exponents)
-    angles = lengths.astype(jnp.float32)[:, None] * frequency[None, :]
-    cosine, sine = jnp.cos(angles), jnp.sin(angles)
-    return jnp.concatenate([cosine, cosine], 1), jnp.concatenate([-sine, sine], 1)
+def frequency_kernel(out):
+    head_dim = out.shape[1]
+    lane = lax.broadcasted_iota(jnp.int32, out.shape, 1)
+    exponents = (lane % (head_dim // 2)).astype(jnp.float32) * (2.0 / head_dim)
+    out[...] = jnp.exp(-math.log(THETA) * exponents)
+
+
+def frequencies(head_dim, microseconds):
+    return pl.pallas_call(
+        frequency_kernel,
+        out_shape=jax.ShapeDtypeStruct((8, head_dim), jnp.float32),
+        out_specs=vmem(),
+        compiler_params=pltpu.CompilerParams(vmem_limit_bytes=2 * MIB),
+        cost_estimate=pl.CostEstimate(
+            flops=int(microseconds * 1.15e9), bytes_accessed=1 << 16, transcendentals=0
+        ),
+        name="frequencies",
+    )()
+
+
+def rotation(lengths, frequency):
+    angles = lengths.astype(jnp.float32)[:, None] * frequency[:1]
+    half = frequency.shape[1] // 2
+    sine = jnp.sin(angles)
+    return jnp.cos(angles), jnp.where(jnp.arange(2 * half) < half, -sine, sine)
 
 
 def body(
@@ -319,20 +391,22 @@
     def place(t):
         return target(peer(lax.axis_index("wide"), t, wide))
 
-    cosine, sine = rotation(lengths, head_dim)
+    frequency, hidden = lax.optimization_barrier((frequencies(head_dim, 100), hidden))
+    cosine, sine = rotation(lengths, frequency)
     hidden_pieces = gather_pieces(hidden, "narrow", narrow)
     parts = project(
         lambda t: place(t) * row_count,
-        hidden_pieces,
-        w_query,
+        collect(hidden_pieces),
+        load(w_query, key_weight, value_weight),
         key_weight,
         value_weight,
+        w_query,
         wide,
         row_count,
         heads,
         kv,
     )
-    *parts, cosine, sine = relay([*parts, cosine, sine], 100)
+    *parts, cosine, sine = relay(relay([*parts, cosine, sine], 0), 100)
     parts = scatter_pieces(parts, "wide", wide)
     context = attend(lengths, cosine, sine, key_cache, cached_values, parts, heads, kv)
     context_pieces = gather_pieces(context, "wide", wide)

time: 49.7 us -> 43.7 us (0.88)
  waiting for transfers between devices: 12.3 us -> 8.53 us
  Pallas kernels: 20.8 us -> 19.2 us
  other arithmetic: 1.5 us -> 0.76 us
    ppermute x6, waiting for transfers between devices: 4.11 us -> 2.09 us  [gather_pieces(): lax.ppermute(piece, axis, xor_pairs(count, t))]
    ppermute x6, waiting for transfers between devices: 8.16 us -> 6.44 us  [scatter_pieces(): lax.ppermute(pieces[t], axis, xor_pairs(count, t))]
    pallas_call x1 -> x4, Pallas kernels: 14 us -> 13.1 us  [the longest x1 9.56 us: project(): pl.pallas_call(functools.partial(project_kernel, heads=heads, kv=kv, stri...]
    pallas_call x1, Pallas kernels: 2.29 us -> 1.52 us  [attend(): pl.pallas_call(functools.partial(attend_kernel, heads=heads, kv=kv, strid...]
    convert_element_type x1, other arithmetic: 0.66 us -> 0.01 us  [rotation(): angles = lengths.astype(jnp.float32)[:, None] * frequency[:1]]
  transfers between devices with their start and end apart: 12 -> 12, of which waited for: 9 -> 6; matrix products, arithmetic and copies ran while one was open for 2% -> 0% of each run, Pallas kernels for 0% -> 8%
where the time goes in v3:
time: 43.7 us; the launch traced here: 43.5 us
  Pallas kernels  19.2 us (44%)
  starting transfers between devices  13.9 us (32%)
  waiting for transfers between devices  8.53 us (20%)
  local copies, waits for them, and re-layouts  0.77 us (2%)
  other arithmetic  0.76 us (2%)
    pallas_call x1, Pallas kernels, project(): pl.pallas_call(functools.partial(project_kernel, heads=heads, kv=kv, stri...  9.56 us
    ppermute x6, starting transfers between devices, gather_pieces(): lax.ppermute(piece, axis, xor_pairs(count, t))  7.51 us
    ppermute x6, waiting for transfers between devices, scatter_pieces(): lax.ppermute(pieces[t], axis, xor_pairs(count, t))  6.44 us
    ppermute x6, starting transfers between devices, scatter_pieces(): lax.ppermute(pieces[t], axis, xor_pairs(count, t))  6.43 us
    pallas_call x1, Pallas kernels, output(): pl.pallas_call(functools.partial(output_kernel, rows_out=rows_out), out_s...  4.44 us
    pallas_call x1, Pallas kernels, load(): pl.pallas_call(load_kernel, out_shape=jax.ShapeDtypeStruct(shape, w_query...  3.51 us
    ppermute x6, waiting for transfers between devices, gather_pieces(): lax.ppermute(piece, axis, xor_pairs(count, t))  2.09 us
    pallas_call x1, Pallas kernels, attend(): pl.pallas_call(functools.partial(attend_kernel, heads=heads, kv=kv, strid...  1.52 us
  transfers between devices with their start and end apart: 12, of which 6 were waited for; matrix products, arithmetic and copies ran while one was open for 0% of the time, Pallas kernels for 8%

profile of v3, /device:TPU:0, one launch (start us, length us, event | category | flops | bytes accessed | tf_op | source)
XLA Modules:
  0.0 43.5 jit_solution(804955807754034110)
XLA Ops:
  0.0 0.7 %copy-done.4 = bf16[2,4096]{1,0:T(2,128)(2,1)S(1)} copy-done((bf16[2,4096]{1,0:T(2,128)(2,1)S(1)}, bf16[2,4096]{1,0:T(2,128)(2,1)}, u32[]{:S(2)}) %copy-start.4) | copy-done | bytes 16408
  0.7 2.4 %collective-permute-start.2 = (bf16[2,4096]{1,0:T(2,128)(2,1)S(1)}, bf16[2,4096]{1,0:T(2,128)(2,1)S(1)}, u32[]{:S(2)}, u32[]{:S(2)}) collective-permute-start(bf16[2,4096]{1,0:T(2,128)(2,1)S(1)} %copy-done.4), channel_id=1, source_target_pairs={{0,3},{1,2},{2,1},{3,0},{4,7},{5,6},{6,5},{7,4},{8,11},{9,10},{10,... | collective-permute-start | bytes 49160 | tf_op jit(solution)/shard_map/ppermute | solution.py:31
  3.1 0.6 %collective-permute-start.1 = (bf16[2,4096]{1,0:T(2,128)(2,1)S(1)}, bf16[2,4096]{1,0:T(2,128)(2,1)S(1)}, u32[]{:S(2)}, u32[]{:S(2)}) collective-permute-start(bf16[2,4096]{1,0:T(2,128)(2,1)S(1)} %copy-done.4), channel_id=1, source_target_pairs={{0,2},{1,3},{2,0},{3,1},{4,6},{5,7},{6,4},{7,5},{8,10},{9,11},{10,... | collective-permute-start | bytes 49160 | tf_op jit(solution)/shard_map/ppermute | solution.py:31
  3.7 0.1 collective-permute-start
  3.8 3.5 %load.1.head = bf16[1024,4096]{1,0:T(8,128)(2,1)S(1)} custom-call(bf16[4096,4096]{1,0:T(8,128)(2,1)} %w_query.3, bf16[4096,256]{1,0:T(8,128)(2,1)S(1)} %copy-done, bf16[4096,256]{1,0:T(8,128)(2,1)S(1)} %copy-done.1), custom_call_target="tpu_custom_call" | custom-call | flops 1000 | bytes 8388608 | tf_op jit(solution)/shard_map/load/pallas_call | solution.py:97
  7.4 0.1 negate_select_fusion
  7.6 9.6 %project.1 = (f32[80,128]{1,0:T(8,128)S(1)}, f32[80,128]{1,0:T(8,128)S(1)}, f32[80,128]{1,0:T(8,128)S(1)}, f32[80,128]{1,0:T(8,128)S(1)}) custom-call(bf16[8,4096]{1,0:T(8,128)(2,1)S(1)} %collect.1.rows, bf16[1024,4096]{1,0:T(8,128)(2,1)S(1)} %load.1.head, bf16[4096,256]{1,0:T(8,128)(2,1)S(1)} %copy-done, bf16[4096,256]{1,0:T(8,128)(2,1)S(1)} %copy-done.1, ...), custom_call_target="tpu_custom_call" | custom-call | flops 1000 | bytes 1000 | tf_op jit(solution)/shard_map/project/pallas_call | solution.py:166
  17.3 3.9 %collective-permute-start.3 = (f32[80,128]{1,0:T(8,128)S(1)}, f32[80,128]{1,0:T(8,128)S(1)}, u32[]{:S(2)}, u32[]{:S(2)}) collective-permute-start(f32[80,128]{1,0:T(8,128)S(1)} %get-tuple-element.42), channel_id=1, source_target_pairs={{0,12},{4,8},{8,4},{12,0},{1,13},{5,9},{9,5},{13,1},{2,14},{6,10},... | collective-permute-start | bytes 122888 | tf_op jit(solution)/shard_map/ppermute | solution.py:39
  21.2 0.6 %collective-permute-start.5 = (f32[80,128]{1,0:T(8,128)S(1)}, f32[80,128]{1,0:T(8,128)S(1)}, u32[]{:S(2)}, u32[]{:S(2)}) collective-permute-start(f32[80,128]{1,0:T(8,128)S(1)} %get-tuple-element.44), channel_id=1, source_target_pairs={{0,4},{4,0},{8,12},{12,8},{1,5},{5,1},{9,13},{13,9},{2,6},{6,2},{1... | collective-permute-start | bytes 122888 | tf_op jit(solution)/shard_map/ppermute | solution.py:39
  21.8 1.4 %collective-permute-done.3.refs_1_ = f32[80,128]{1,0:T(8,128)S(1)} collective-permute-done((f32[80,128]{1,0:T(8,128)S(1)}, f32[80,128]{1,0:T(8,128)S(1)}, u32[]{:S(2)}, u32[]{:S(2)}) %collective-permute-start.3) | collective-permute-done | bytes 40992 | tf_op jit(solution)/shard_map/ppermute | solution.py:39
  23.2 2.9 %collective-permute-done.4.refs_2_ = f32[80,128]{1,0:T(8,128)S(1)} collective-permute-done((f32[80,128]{1,0:T(8,128)S(1)}, f32[80,128]{1,0:T(8,128)S(1)}, u32[]{:S(2)}, u32[]{:S(2)}) %collective-permute-start.4) | collective-permute-done | bytes 40992 | tf_op jit(solution)/shard_map/ppermute | solution.py:39
  26.1 1.5 %attend.1.refs_0_ = bf16[64,128]{1,0:T(8,128)(2,1)S(1)} custom-call(s32[2]{0:T(128)S(1)} %copy-done.5, f32[2,128]{1,0:T(2,128)S(1)} %get-tuple-element.39.cosine, f32[2,128]{1,0:T(2,128)S(1)} %get-tuple-element.40.sine, bf16[2,2,2048,128]{3,2,1,0:T(8,128)(2,1)S(1)} %copy-done.2, bf16[2,2,2048,128]{3,2,1,0:T(8,128)(2,1)S(1)} %copy-done.3, ...), custom_call_target="tpu_custom_call" | custom-call | flops 1000 | bytes 1000 | tf_op jit(solution)/shard_map/attend/pallas_call | solution.py:268
  27.6 1.9 %collective-permute-start.8 = (bf16[64,128]{1,0:T(8,128)(2,1)S(1)}, bf16[64,128]{1,0:T(8,128)(2,1)S(1)}, u32[]{:S(2)}, u32[]{:S(2)}) collective-permute-start(bf16[64,128]{1,0:T(8,128)(2,1)S(1)} %attend.1.refs_0_), channel_id=1, source_target_pairs={{0,12},{4,8},{8,4},{12,0},{1,13},{5,9},{9,5},{13,1},{2,14},{6,10},... | collective-permute-start | bytes 49160 | tf_op jit(solution)/shard_map/ppermute | solution.py:31
  29.5 0.3 collective-permute-start.7
  29.8 2.3 %collective-permute-start.6 = (bf16[64,128]{1,0:T(8,128)(2,1)S(1)}, bf16[64,128]{1,0:T(8,128)(2,1)S(1)}, u32[]{:S(2)}, u32[]{:S(2)}) collective-permute-start(bf16[64,128]{1,0:T(8,128)(2,1)S(1)} %attend.1.refs_0_), channel_id=1, source_target_pairs={{0,4},{4,0},{8,12},{12,8},{1,5},{5,1},{9,13},{13,9},{2,6},{6,2},{1... | collective-permute-start | bytes 49160 | tf_op jit(solution)/shard_map/ppermute | solution.py:31
  32.1 1.2 %collective-permute-done.8.refs_3_ = bf16[64,128]{1,0:T(8,128)(2,1)S(1)} collective-permute-done((bf16[64,128]{1,0:T(8,128)(2,1)S(1)}, bf16[64,128]{1,0:T(8,128)(2,1)S(1)}, u32[]{:S(2)}, u32[]{:S(2)}) %collective-permute-start.8) | collective-permute-done | bytes 16416 | tf_op jit(solution)/shard_map/ppermute | solution.py:31
  33.3 0.9 %collective-permute-done.7.refs_2_ = bf16[64,128]{1,0:T(8,128)(2,1)S(1)} collective-permute-done((bf16[64,128]{1,0:T(8,128)(2,1)S(1)}, bf16[64,128]{1,0:T(8,128)(2,1)S(1)}, u32[]{:S(2)}, u32[]{:S(2)}) %collective-permute-start.7) | collective-permute-done | bytes 16416 | tf_op jit(solution)/shard_map/ppermute | solution.py:31
  34.2 0.1 arrange.1.rows
  34.4 4.4 %output.1 = (f32[2,4096]{1,0:T(2,128)S(1)}, f32[2,4096]{1,0:T(2,128)S(1)}, f32[2,4096]{1,0:T(2,128)S(1)}, f32[2,4096]{1,0:T(2,128)S(1)}) custom-call(bf16[8,4096]{1,0:T(8,128)(2,1)S(1)} %arrange.1.rows, bf16[4096,4096]{1,0:T(8,128)(2,1)S(1)} %bitcast.3), custom_call_target="tpu_custom_call" | custom-call | flops 1000 | bytes 1000 | tf_op jit(solution)/shard_map/output/pallas_call | solution.py:329
  38.8 1.5 %collective-permute-start.10 = (f32[2,4096]{1,0:T(2,128)S(1)}, f32[2,4096]{1,0:T(2,128)S(1)}, u32[]{:S(2)}, u32[]{:S(2)}) collective-permute-start(f32[2,4096]{1,0:T(2,128)S(1)} %get-tuple-element.47), channel_id=1, source_target_pairs={{0,2},{1,3},{2,0},{3,1},{4,6},{5,7},{6,4},{7,5},{8,10},{9,11},{10,... | collective-permute-start | bytes 98312 | tf_op jit(solution)/shard_map/ppermute | solution.py:39
  40.3 0.4 collective-permute-start.11
  40.7 1.8 %collective-permute-done.9 = f32[2,4096]{1,0:T(2,128)S(1)} collective-permute-done((f32[2,4096]{1,0:T(2,128)S(1)}, f32[2,4096]{1,0:T(2,128)S(1)}, u32[]{:S(2)}, u32[]{:S(2)}) %collective-permute-start.9) | collective-permute-done | bytes 32800 | tf_op jit(solution)/shard_map/ppermute | solution.py:39
  42.5 0.4 collective-permute-done.10
  42.8 0.6 %add_convert_fusion = bf16[2,4096]{1,0:T(2,128)(2,1)} fusion(f32[2,4096]{1,0:T(2,128)S(1)} %collective-permute-done.11, f32[2,4096]{1,0:T(2,128)S(1)} %collective-permute-done.10, f32[2,4096]{1,0:T(2,128)S(1)} %get-tuple-element.45, f32[2,4096]{1,0:T(2,128)S(1)} %collective-permute-done.9), kind=kLoop, calls=%fused_computation | loop fusion | flops 32768 | bytes 147456 | tf_op jit(solution)/shard_map/convert_element_type | solution.py:419
  (43 shorter events, 0.2 us)
Async XLA Ops:
  0.0 3.8 %copy-start.1 = (bf16[4096,256]{1,0:T(8,128)(2,1)S(1)}, bf16[4096,256]{1,0:T(8,128)(2,1)}, u32[]{:S(2)}) copy-start(bf16[4096,256]{1,0:T(8,128)(2,1)} %value_weight.3) | copy-start | bytes 6291460
  0.0 3.8 %copy-start = (bf16[4096,256]{1,0:T(8,128)(2,1)S(1)}, bf16[4096,256]{1,0:T(8,128)(2,1)}, u32[]{:S(2)}) copy-start(bf16[4096,256]{1,0:T(8,128)(2,1)} %key_weight.3) | copy-start | bytes 6291460
  0.7 6.6 %collective-permute-start.2 = (bf16[2,4096]{1,0:T(2,128)(2,1)S(1)}, bf16[2,4096]{1,0:T(2,128)(2,1)S(1)}, u32[]{:S(2)}, u32[]{:S(2)}) collective-permute-start(bf16[2,4096]{1,0:T(2,128)(2,1)S(1)} %copy-done.4), channel_id=1, source_target_pairs={{0,3},{1,2},{2,1},{3,0},{4,7},{5,6},{6,5},{7,4},{8,11},{9,10},{10,... | collective-permute-start | bytes 49160 | tf_op jit(solution)/shard_map/ppermute | solution.py:31
  3.1 4.3 %collective-permute-start.1 = (bf16[2,4096]{1,0:T(2,128)(2,1)S(1)}, bf16[2,4096]{1,0:T(2,128)(2,1)S(1)}, u32[]{:S(2)}, u32[]{:S(2)}) collective-permute-start(bf16[2,4096]{1,0:T(2,128)(2,1)S(1)} %copy-done.4), channel_id=1, source_target_pairs={{0,2},{1,3},{2,0},{3,1},{4,6},{5,7},{6,4},{7,5},{8,10},{9,11},{10,... | collective-permute-start | bytes 49160 | tf_op jit(solution)/shard_map/ppermute | solution.py:31
  3.7 3.7 %collective-permute-start = (bf16[2,4096]{1,0:T(2,128)(2,1)S(1)}, bf16[2,4096]{1,0:T(2,128)(2,1)S(1)}, u32[]{:S(2)}, u32[]{:S(2)}) collective-permute-start(bf16[2,4096]{1,0:T(2,128)(2,1)S(1)} %copy-done.4), channel_id=1, source_target_pairs={{0,1},{1,0},{2,3},{3,2},{4,5},{5,4},{6,7},{7,6},{8,9},{9,8},{10,11... | collective-permute-start | bytes 49160 | tf_op jit(solution)/shard_map/ppermute | solution.py:31
  7.5 26.7 %slice-start = ((s8[33554432]{0:T(1024)(128)(4,1)}), s8[4194304]{0:T(1024)(128)(4,1)S(1)}, s32[]{:S(2)}) async-start(s8[33554432]{0:T(1024)(128)(4,1)} %bitcast.2), calls=%async_computation | async-start | bytes 8388608
  17.1 9.0 %copy-start.2 = (bf16[2,2,2048,128]{3,2,1,0:T(8,128)(2,1)S(1)}, bf16[2,2,2048,128]{3,2,1,0:T(8,128)(2,1)}, u32[]{:S(2)}) copy-start(bf16[2,2,2048,128]{3,2,1,0:T(8,128)(2,1)} %key_cache.1) | copy-start | bytes 6291460
  17.2 8.9 %copy-start.3 = (bf16[2,2,2048,128]{3,2,1,0:T(8,128)(2,1)S(1)}, bf16[2,2,2048,128]{3,2,1,0:T(8,128)(2,1)}, u32[]{:S(2)}) copy-start(bf16[2,2,2048,128]{3,2,1,0:T(8,128)(2,1)} %cached_values.1) | copy-start | bytes 6291460
  17.2 17.1 %slice-start.1 = ((s8[33554432]{0:T(1024)(128)(4,1)}), s8[4194304]{0:T(1024)(128)(4,1)S(1)}, s32[]{:S(2)}) async-start(s8[33554432]{0:T(1024)(128)(4,1)} %bitcast.2), calls=%async_computation.1 | async-start | bytes 8388608
  17.2 17.1 %slice-start.2 = ((s8[33554432]{0:T(1024)(128)(4,1)}), s8[4194304]{0:T(1024)(128)(4,1)S(1)}, s32[]{:S(2)}) async-start(s8[33554432]{0:T(1024)(128)(4,1)} %bitcast.2), calls=%async_computation.2 | async-start | bytes 8388608
  17.2 17.1 %slice-start.3 = ((s8[33554432]{0:T(1024)(128)(4,1)}), s8[4194304]{0:T(1024)(128)(4,1)S(1)}, s32[]{:S(2)}) async-start(s8[33554432]{0:T(1024)(128)(4,1)} %bitcast.2), calls=%async_computation.3 | async-start | bytes 8388608
  17.2 17.1 %slice-start.4 = ((s8[33554432]{0:T(1024)(128)(4,1)}), s8[4194304]{0:T(1024)(128)(4,1)S(1)}, s32[]{:S(2)}) async-start(s8[33554432]{0:T(1024)(128)(4,1)} %bitcast.2), calls=%async_computation.4 | async-start | bytes 8388608
  17.2 17.1 %slice-start.5 = ((s8[33554432]{0:T(1024)(128)(4,1)}), s8[4194304]{0:T(1024)(128)(4,1)S(1)}, s32[]{:S(2)}) async-start(s8[33554432]{0:T(1024)(128)(4,1)} %bitcast.2), calls=%async_computation.5 | async-start | bytes 8388608
  17.2 17.1 %slice-start.6 = ((s8[33554432]{0:T(1024)(128)(4,1)}), s8[4194304]{0:T(1024)(128)(4,1)S(1)}, s32[]{:S(2)}) async-start(s8[33554432]{0:T(1024)(128)(4,1)} %bitcast.2), calls=%async_computation.6 | async-start | bytes 8388608
  17.2 17.1 %slice-start.7 = ((s8[33554432]{0:T(1024)(128)(4,1)}), s8[4194304]{0:T(1024)(128)(4,1)S(1)}, s32[]{:S(2)}) async-start(s8[33554432]{0:T(1024)(128)(4,1)} %bitcast.2), calls=%async_computation.7 | async-start | bytes 8388608
  17.3 6.0 %collective-permute-start.3 = (f32[80,128]{1,0:T(8,128)S(1)}, f32[80,128]{1,0:T(8,128)S(1)}, u32[]{:S(2)}, u32[]{:S(2)}) collective-permute-start(f32[80,128]{1,0:T(8,128)S(1)} %get-tuple-element.42), channel_id=1, source_target_pairs={{0,12},{4,8},{8,4},{12,0},{1,13},{5,9},{9,5},{13,1},{2,14},{6,10},... | collective-permute-start | bytes 122888 | tf_op jit(solution)/shard_map/ppermute | solution.py:39
  21.2 4.9 %collective-permute-start.4 = (f32[80,128]{1,0:T(8,128)S(1)}, f32[80,128]{1,0:T(8,128)S(1)}, u32[]{:S(2)}, u32[]{:S(2)}) collective-permute-start(f32[80,128]{1,0:T(8,128)S(1)} %get-tuple-element.43), channel_id=1, source_target_pairs={{0,8},{4,12},{8,0},{12,4},{1,9},{5,13},{9,1},{13,5},{2,10},{6,14},... | collective-permute-start | bytes 122888 | tf_op jit(solution)/shard_map/ppermute | solution.py:39
  21.2 4.9 %collective-permute-start.5 = (f32[80,128]{1,0:T(8,128)S(1)}, f32[80,128]{1,0:T(8,128)S(1)}, u32[]{:S(2)}, u32[]{:S(2)}) collective-permute-start(f32[80,128]{1,0:T(8,128)S(1)} %get-tuple-element.44), channel_id=1, source_target_pairs={{0,4},{4,0},{8,12},{12,8},{1,5},{5,1},{9,13},{13,9},{2,6},{6,2},{1... | collective-permute-start | bytes 122888 | tf_op jit(solution)/shard_map/ppermute | solution.py:39
  27.6 5.7 %collective-permute-start.8 = (bf16[64,128]{1,0:T(8,128)(2,1)S(1)}, bf16[64,128]{1,0:T(8,128)(2,1)S(1)}, u32[]{:S(2)}, u32[]{:S(2)}) collective-permute-start(bf16[64,128]{1,0:T(8,128)(2,1)S(1)} %attend.1.refs_0_), channel_id=1, source_target_pairs={{0,12},{4,8},{8,4},{12,0},{1,13},{5,9},{9,5},{13,1},{2,14},{6,10},... | collective-permute-start | bytes 49160 | tf_op jit(solution)/shard_map/ppermute | solution.py:31
  29.5 4.6 %collective-permute-start.7 = (bf16[64,128]{1,0:T(8,128)(2,1)S(1)}, bf16[64,128]{1,0:T(8,128)(2,1)S(1)}, u32[]{:S(2)}, u32[]{:S(2)}) collective-permute-start(bf16[64,128]{1,0:T(8,128)(2,1)S(1)} %attend.1.refs_0_), channel_id=1, source_target_pairs={{0,8},{4,12},{8,0},{12,4},{1,9},{5,13},{9,1},{13,5},{2,10},{6,14},... | collective-permute-start | bytes 49160 | tf_op jit(solution)/shard_map/ppermute | solution.py:31
  29.8 4.4 %collective-permute-start.6 = (bf16[64,128]{1,0:T(8,128)(2,1)S(1)}, bf16[64,128]{1,0:T(8,128)(2,1)S(1)}, u32[]{:S(2)}, u32[]{:S(2)}) collective-permute-start(bf16[64,128]{1,0:T(8,128)(2,1)S(1)} %attend.1.refs_0_), channel_id=1, source_target_pairs={{0,4},{4,0},{8,12},{12,8},{1,5},{5,1},{9,13},{13,9},{2,6},{6,2},{1... | collective-permute-start | bytes 49160 | tf_op jit(solution)/shard_map/ppermute | solution.py:31
  38.8 3.7 %collective-permute-start.9 = (f32[2,4096]{1,0:T(2,128)S(1)}, f32[2,4096]{1,0:T(2,128)S(1)}, u32[]{:S(2)}, u32[]{:S(2)}) collective-permute-start(f32[2,4096]{1,0:T(2,128)S(1)} %get-tuple-element.46), channel_id=1, source_target_pairs={{0,3},{1,2},{2,1},{3,0},{4,7},{5,6},{6,5},{7,4},{8,11},{9,10},{10,... | collective-permute-start | bytes 98312 | tf_op jit(solution)/shard_map/ppermute | solution.py:39
  38.8 4.0 %collective-permute-start.10 = (f32[2,4096]{1,0:T(2,128)S(1)}, f32[2,4096]{1,0:T(2,128)S(1)}, u32[]{:S(2)}, u32[]{:S(2)}) collective-permute-start(f32[2,4096]{1,0:T(2,128)S(1)} %get-tuple-element.47), channel_id=1, source_target_pairs={{0,2},{1,3},{2,0},{3,1},{4,6},{5,7},{6,4},{7,5},{8,10},{9,11},{10,... | collective-permute-start | bytes 98312 | tf_op jit(solution)/shard_map/ppermute | solution.py:39
  40.3 2.6 %collective-permute-start.11 = (f32[2,4096]{1,0:T(2,128)S(1)}, f32[2,4096]{1,0:T(2,128)S(1)}, u32[]{:S(2)}, u32[]{:S(2)}) collective-permute-start(f32[2,4096]{1,0:T(2,128)S(1)} %get-tuple-element.48), channel_id=1, source_target_pairs={{0,1},{1,0},{2,3},{3,2},{4,5},{5,4},{6,7},{7,6},{8,9},{9,8},{10,11... | collective-permute-start | bytes 98312 | tf_op jit(solution)/shard_map/ppermute | solution.py:39
  (2 other events, 4.2 us)

commit v4 on v3

--- a/solution.py
+++ b/solution.py
@@ -46,31 +46,12 @@
     return lax.bitwise_xor(me, t) if direct(count) else jnp.int32(t)
 
 
+def smem():
+    return pl.BlockSpec(memory_space=pltpu.SMEM)
+
+
 def vmem():
     return pl.BlockSpec(memory_space=pltpu.VMEM)
-
-
-def smem():
-    return pl.BlockSpec(memory_space=pltpu.SMEM)
-
-
-def collect_kernel(*refs):
-    refs[-1][...] = jnp.concatenate([r[...].astype(jnp.float32) for r in refs[:-1]], 0).astype(
-        jnp.bfloat16
-    )
-
-
-def collect(pieces):
-    count = sum(p.shape[0] for p in pieces)
-    return pl.pallas_call(
-        collect_kernel,
-        out_shape=jax.ShapeDtypeStruct((count, pieces[0].shape[1]), jnp.bfloat16),
-        in_specs=[vmem()] * len(pieces),
-        out_specs=vmem(),
-        compiler_params=pltpu.CompilerParams(vmem_limit_bytes=6 * MIB),
-        cost_estimate=pl.CostEstimate(flops=1000, bytes_accessed=1000, transcendentals=0),
-        name="collect",
-    )(*pieces)
 
 
 def head_depth(w_query):
@@ -109,9 +90,10 @@
 
 
 def project_kernel(
-    rows, head, key_weight, value_weight, w_query, *refs, heads, kv, stride, place, depth, slots
+    head, key_weight, value_weight, w_query, *refs, pieces, heads, kv, stride, place, depth, slots
 ):
-    outs, (total, laid, held, sems) = refs[:-4], refs[-4:]
+    inputs, refs = refs[:pieces], refs[pieces:]
+    outs, (rows, total, laid, held, sems) = refs[:-5], refs[-5:]
     count, width = rows.shape
     done = head.shape[0]
     cut = held.shape[2]
@@ -136,6 +118,9 @@
 
     for i in range(min(slots, chunks)):
         copy(i).start()
+    rows[...] = jnp.concatenate([p[...].astype(jnp.float32) for p in inputs], 0).astype(
+        jnp.bfloat16
+    )
     half = width // 2
     for i, w in enumerate((key_weight, value_weight)):
         lay(
@@ -152,20 +137,24 @@
         )
         if i + slots < chunks:
             copy(i + slots).start()
-    lay(total, 0)
+        if i + cuts >= chunks:
+            lay(total[:, first : first + cut], first // LANES)
     for t, out in enumerate(outs):
         out[...] = laid[pl.ds(pl.multiple_of(place(t) * stride, 8), out.shape[0]), :]
 
 
-def project(place, rows, head, key_weight, value_weight, w_query, targets, row_count, heads, kv):
+def project(
+    place, hidden_pieces, head, key_weight, value_weight, w_query, targets, row_count, heads, kv
+):
     stride = -(-(heads + 2 * kv) // 8) * 8
-    count, width = rows.shape
-    columns = w_query.shape[1]
+    width, columns = w_query.shape
+    count = sum(p.shape[0] for p in hidden_pieces)
     depth = math.gcd(256, width - head.shape[0])
     scratch = SLOTS * depth * (columns // CUTS) * 2 + count * (columns + stride * LANES) * 4
     return pl.pallas_call(
         functools.partial(
             project_kernel,
+            pieces=len(hidden_pieces),
             heads=heads,
             kv=kv,
             stride=stride,
@@ -174,9 +163,12 @@
             slots=SLOTS,
         ),
         out_shape=[jax.ShapeDtypeStruct((row_count * stride, LANES), jnp.float32)] * targets,
-        in_specs=[vmem()] * 4 + [pl.BlockSpec(memory_space=pltpu.HBM)],
+        in_specs=[vmem()] * 3
+        + [pl.BlockSpec(memory_space=pltpu.HBM)]
+        + [vmem()] * len(hidden_pieces),
         out_specs=[vmem()] * targets,
         scratch_shapes=[
+            pltpu.VMEM((count, width), jnp.bfloat16),
             pltpu.VMEM((count, columns), jnp.float32),
             pltpu.VMEM((count * stride, LANES), jnp.float32),
             pltpu.VMEM((SLOTS, depth, columns // CUTS), jnp.bfloat16),
@@ -186,11 +178,11 @@
         cost_estimate=pl.CostEstimate(flops=1000, bytes_accessed=1000, transcendentals=0),
         name="project",
     )(
-        rows,
         head,
         key_weight,
         value_weight,
         pltpu.with_memory_space_constraint(w_query, pltpu.HBM),
+        *hidden_pieces,
     )
 
 
@@ -214,7 +206,7 @@
     )(*arrays)
 
 
-def attend_kernel(lengths, cosine, sine, key_cache, cached_values, *refs, heads, kv, stride):
+def attend_kernel(limits, cosine, sine, key_cache, cached_values, *refs, heads, kv, stride):
     parts, out = refs[:-1], refs[-1]
     row_count, _, slots, head_dim = key_cache.shape
     per = heads // kv
@@ -247,7 +239,7 @@
         )
     weights, self_weights, denominators = {}, {}, {}
     for r, g in pairs:
-        masked = jnp.where(position < lengths[r], scores[r, g] * scale, -jnp.inf)
+        masked = jnp.where(position < limits[r : r + 1, :1], scores[r, g] * scale, -jnp.inf)
         highest = jnp.maximum(jnp.max(masked, -1, keepdims=True), self_scores[r, g])
         raised = jnp.exp(masked - highest)
         self_weight = jnp.exp(self_scores[r, g] - highest)
@@ -262,21 +254,19 @@
         out[start : start + per, :] = (mixed / denominators[r, g]).astype(jnp.bfloat16)
 
 
-def attend(lengths, cosine, sine, key_cache, cached_values, parts, heads, kv):
+def attend(tables, key_cache, cached_values, parts, heads, kv):
     row_count = key_cache.shape[0]
     stride = parts[0].shape[0] // row_count
     return pl.pallas_call(
         functools.partial(attend_kernel, heads=heads, kv=kv, stride=stride),
         out_shape=jax.ShapeDtypeStruct((row_count * heads, LANES), jnp.bfloat16),
-        in_specs=[smem()] + [vmem()] * (4 + len(parts)),
+        in_specs=[vmem()] * (5 + len(parts)),
         out_specs=vmem(),
         compiler_params=pltpu.CompilerParams(vmem_limit_bytes=6 * MIB),
         cost_estimate=pl.CostEstimate(flops=1000, bytes_accessed=1000, transcendentals=0),
         name="attend",
     )(
-        lengths,
-        cosine,
-        sine,
+        *tables,
         key_cache,
         cached_values,
         *parts,
@@ -357,11 +347,29 @@
     )()
 
 
-def rotation(lengths, frequency):
-    angles = lengths.astype(jnp.float32)[:, None] * frequency[:1]
-    half = frequency.shape[1] // 2
-    sine = jnp.sin(angles)
-    return jnp.cos(angles), jnp.where(jnp.arange(2 * half) < half, -sine, sine)
+def tables_kernel(lengths, frequency, limits, cosine, sine):
+    row_count, head_dim = limits.shape
+    lane = lax.broadcasted_iota(jnp.int32, (1, head_dim), 1)
+    for r in range(row_count):
+        position = jnp.full((1, head_dim), lengths[r], jnp.int32)
+        angle = position.astype(jnp.float32) * frequency[:1]
+        turn = jnp.sin(angle)
+        limits[r : r + 1, :] = position
+        cosine[r : r + 1, :] = jnp.cos(angle)
+        sine[r : r + 1, :] = jnp.where(lane < head_dim // 2, -turn, turn)
+
+
+def tables_of(lengths, frequency):
+    shape = (lengths.shape[0], frequency.shape[1])
+    return pl.pallas_call(
+        tables_kernel,
+        out_shape=[jax.ShapeDtypeStruct(shape, t) for t in (jnp.int32, jnp.float32, jnp.float32)],
+        in_specs=[smem(), vmem()],
+        out_specs=[vmem()] * 3,
+        compiler_params=pltpu.CompilerParams(vmem_limit_bytes=2 * MIB),
+        cost_estimate=pl.CostEstimate(flops=1000, bytes_accessed=1000, transcendentals=0),
+        name="tables",
+    )(lengths, frequency)
 
 
 def body(
@@ -392,11 +400,10 @@
         return target(peer(lax.axis_index("wide"), t, wide))
 
     frequency, hidden = lax.optimization_barrier((frequencies(head_dim, 100), hidden))
-    cosine, sine = rotation(lengths, frequency)
     hidden_pieces = gather_pieces(hidden, "narrow", narrow)
     parts = project(
         lambda t: place(t) * row_count,
-        collect(hidden_pieces),
+        hidden_pieces,
         load(w_query, key_weight, value_weight),
         key_weight,
         value_weight,
@@ -406,9 +413,10 @@
         heads,
         kv,
     )
-    *parts, cosine, sine = relay(relay([*parts, cosine, sine], 0), 100)
+    *parts, frequency = relay(relay([*parts, frequency], 30), 100)
+    tables = tables_of(lengths, frequency)
     parts = scatter_pieces(parts, "wide", wide)
-    context = attend(lengths, cosine, sine, key_cache, cached_values, parts, heads, kv)
+    context = attend(tables, key_cache, cached_values, parts, heads, kv)
     context_pieces = gather_pieces(context, "wide", wide)
     rows = arrange(place, context_pieces, row_count, heads)
     sums = output(rows, w_out, rows_out, narrow)

time: 43.7 us -> 42.4 us (0.970)
  waiting for transfers between devices: 8.53 us -> 7.93 us
    ppermute x6, waiting for transfers between devices: 6.44 us -> 5.84 us  [scatter_pieces(): lax.ppermute(pieces[t], axis, xor_pairs(count, t))]
    pallas_call x1, Pallas kernels: 1.52 us -> 0.99 us  [attend(): pl.pallas_call(functools.partial(attend_kernel, heads=heads, kv=kv, strid...]
  transfers between devices with their start and end apart: 12 -> 12, of which waited for: 6 -> 6; matrix products, arithmetic and copies ran while one was open for 0% -> 0% of each run, Pallas kernels for 8% -> 10%
where the time goes in v4:
time: 42.4 us; the launch traced here: 42.2 us
  Pallas kernels  18.8 us (44%)
  starting transfers between devices  13.9 us (33%)
  waiting for transfers between devices  7.93 us (19%)
  local copies, waits for them, and re-layouts  0.74 us (2%)
  other arithmetic  0.64 us (2%)
    pallas_call x1, Pallas kernels, project(): pl.pallas_call(functools.partial(project_kernel, pieces=len(hidden_pieces...  9.17 us
    ppermute x6, starting transfers between devices, gather_pieces(): lax.ppermute(piece, axis, xor_pairs(count, t))  7.51 us
    ppermute x6, starting transfers between devices, scatter_pieces(): lax.ppermute(pieces[t], axis, xor_pairs(count, t))  6.43 us
    ppermute x6, waiting for transfers between devices, scatter_pieces(): lax.ppermute(pieces[t], axis, xor_pairs(count, t))  5.84 us
    pallas_call x1, Pallas kernels, output(): pl.pallas_call(functools.partial(output_kernel, rows_out=rows_out), out_s...  4.44 us
    pallas_call x1, Pallas kernels, load(): pl.pallas_call(load_kernel, out_shape=jax.ShapeDtypeStruct(shape, w_query...  3.5 us
    ppermute x6, waiting for transfers between devices, gather_pieces(): lax.ppermute(piece, axis, xor_pairs(count, t))  2.09 us
    pallas_call x1, Pallas kernels, attend(): pl.pallas_call(functools.partial(attend_kernel, heads=heads, kv=kv, strid...  0.99 us
  transfers between devices with their start and end apart: 12, of which 6 were waited for; matrix products, arithmetic and copies ran while one was open for 0% of the time, Pallas kernels for 10%

profile of v4, /device:TPU:0, one launch (start us, length us, event | category | flops | bytes accessed | tf_op | source)
XLA Modules:
  0.0 42.2 jit_solution(7939824494311475508)
XLA Ops:
  0.0 0.7 %copy-done.5 = bf16[2,4096]{1,0:T(2,128)(2,1)S(1)} copy-done((bf16[2,4096]{1,0:T(2,128)(2,1)S(1)}, bf16[2,4096]{1,0:T(2,128)(2,1)}, u32[]{:S(2)}) %copy-start.5) | copy-done | bytes 16408
  0.7 2.4 %collective-permute-start.2 = (bf16[2,4096]{1,0:T(2,128)(2,1)S(1)}, bf16[2,4096]{1,0:T(2,128)(2,1)S(1)}, u32[]{:S(2)}, u32[]{:S(2)}) collective-permute-start(bf16[2,4096]{1,0:T(2,128)(2,1)S(1)} %copy-done.5), channel_id=1, source_target_pairs={{0,3},{1,2},{2,1},{3,0},{4,7},{5,6},{6,5},{7,4},{8,11},{9,10},{10,... | collective-permute-start | bytes 49160 | tf_op jit(solution)/shard_map/ppermute | solution.py:31
  3.1 0.6 %collective-permute-start.1 = (bf16[2,4096]{1,0:T(2,128)(2,1)S(1)}, bf16[2,4096]{1,0:T(2,128)(2,1)S(1)}, u32[]{:S(2)}, u32[]{:S(2)}) collective-permute-start(bf16[2,4096]{1,0:T(2,128)(2,1)S(1)} %copy-done.5), channel_id=1, source_target_pairs={{0,2},{1,3},{2,0},{3,1},{4,6},{5,7},{6,4},{7,5},{8,10},{9,11},{10,... | collective-permute-start | bytes 49160 | tf_op jit(solution)/shard_map/ppermute | solution.py:31
  3.7 0.1 collective-permute-start
  3.8 3.5 %load.1.head = bf16[1024,4096]{1,0:T(8,128)(2,1)S(1)} custom-call(bf16[4096,4096]{1,0:T(8,128)(2,1)} %w_query.3, bf16[4096,256]{1,0:T(8,128)(2,1)S(1)} %copy-done.1, bf16[4096,256]{1,0:T(8,128)(2,1)S(1)} %copy-done.2), custom_call_target="tpu_custom_call" | custom-call | flops 1000 | bytes 8388608 | tf_op jit(solution)/shard_map/load/pallas_call | solution.py:78
  7.3 9.2 %project.1 = (f32[80,128]{1,0:T(8,128)S(1)}, f32[80,128]{1,0:T(8,128)S(1)}, f32[80,128]{1,0:T(8,128)S(1)}, f32[80,128]{1,0:T(8,128)S(1)}) custom-call(bf16[1024,4096]{1,0:T(8,128)(2,1)S(1)} %load.1.head, bf16[4096,256]{1,0:T(8,128)(2,1)S(1)} %copy-done.1, bf16[4096,256]{1,0:T(8,128)(2,1)S(1)} %copy-done.2, bf16[4096,4096]{1,0:T(8,128)(2,1)} %w_query.3, ...), custom_call_target="tpu_custom_call" | custom-call | flops 1000 | bytes 1000 | tf_op jit(solution)/shard_map/project/pallas_call | solution.py:154
  16.6 3.9 %collective-permute-start.3 = (f32[80,128]{1,0:T(8,128)S(1)}, f32[80,128]{1,0:T(8,128)S(1)}, u32[]{:S(2)}, u32[]{:S(2)}) collective-permute-start(f32[80,128]{1,0:T(8,128)S(1)} %get-tuple-element.44), channel_id=1, source_target_pairs={{0,12},{4,8},{8,4},{12,0},{1,13},{5,9},{9,5},{13,1},{2,14},{6,10},... | collective-permute-start | bytes 122888 | tf_op jit(solution)/shard_map/ppermute | solution.py:39
  20.5 0.6 %collective-permute-start.5 = (f32[80,128]{1,0:T(8,128)S(1)}, f32[80,128]{1,0:T(8,128)S(1)}, u32[]{:S(2)}, u32[]{:S(2)}) collective-permute-start(f32[80,128]{1,0:T(8,128)S(1)} %get-tuple-element.46), channel_id=1, source_target_pairs={{0,4},{4,0},{8,12},{12,8},{1,5},{5,1},{9,13},{13,9},{2,6},{6,2},{1... | collective-permute-start | bytes 122888 | tf_op jit(solution)/shard_map/ppermute | solution.py:39
  21.2 0.6 %tables.1 = (s32[2,128]{1,0:T(2,128)S(1)}, f32[2,128]{1,0:T(2,128)S(1)}, f32[2,128]{1,0:T(2,128)S(1)}) custom-call(s32[2]{0:T(128)S(1)} %copy-done.6, f32[8,128]{1,0:T(8,128)S(1)} %get-tuple-element.39.frequency), custom_call_target="tpu_custom_call" | custom-call | flops 1000 | bytes 1000 | tf_op jit(solution)/shard_map/tables/pallas_call | solution.py:364
  21.8 0.8 %collective-permute-done.3.refs_1_ = f32[80,128]{1,0:T(8,128)S(1)} collective-permute-done((f32[80,128]{1,0:T(8,128)S(1)}, f32[80,128]{1,0:T(8,128)S(1)}, u32[]{:S(2)}, u32[]{:S(2)}) %collective-permute-start.3) | collective-permute-done | bytes 40992 | tf_op jit(solution)/shard_map/ppermute | solution.py:39
  22.6 2.9 %collective-permute-done.4.refs_2_ = f32[80,128]{1,0:T(8,128)S(1)} collective-permute-done((f32[80,128]{1,0:T(8,128)S(1)}, f32[80,128]{1,0:T(8,128)S(1)}, u32[]{:S(2)}, u32[]{:S(2)}) %collective-permute-start.4) | collective-permute-done | bytes 40992 | tf_op jit(solution)/shard_map/ppermute | solution.py:39
  25.4 1.0 %attend.1.refs_0_ = bf16[64,128]{1,0:T(8,128)(2,1)S(1)} custom-call(s32[2,128]{1,0:T(2,128)S(1)} %get-tuple-element.40.limits, f32[2,128]{1,0:T(2,128)S(1)} %get-tuple-element.41.cosine, f32[2,128]{1,0:T(2,128)S(1)} %get-tuple-element.42.sine, bf16[2,2,2048,128]{3,2,1,0:T(8,128)(2,1)S(1)} %copy-done.3, bf16[2,2,2048,128]{3,2,1,0:T(8,128)(2,1)S(1)} %copy-done.4, ...), custom_call_target="tpu_custom_call" | custom-call | flops 1000 | bytes 1000 | tf_op jit(solution)/shard_map/attend/pallas_call | solution.py:260
  26.4 1.9 %collective-permute-start.8 = (bf16[64,128]{1,0:T(8,128)(2,1)S(1)}, bf16[64,128]{1,0:T(8,128)(2,1)S(1)}, u32[]{:S(2)}, u32[]{:S(2)}) collective-permute-start(bf16[64,128]{1,0:T(8,128)(2,1)S(1)} %attend.1.refs_0_), channel_id=1, source_target_pairs={{0,12},{4,8},{8,4},{12,0},{1,13},{5,9},{9,5},{13,1},{2,14},{6,10},... | collective-permute-start | bytes 49160 | tf_op jit(solution)/shard_map/ppermute | solution.py:31
  28.3 0.3 collective-permute-start.7
  28.6 2.3 %collective-permute-start.6 = (bf16[64,128]{1,0:T(8,128)(2,1)S(1)}, bf16[64,128]{1,0:T(8,128)(2,1)S(1)}, u32[]{:S(2)}, u32[]{:S(2)}) collective-permute-start(bf16[64,128]{1,0:T(8,128)(2,1)S(1)} %attend.1.refs_0_), channel_id=1, source_target_pairs={{0,4},{4,0},{8,12},{12,8},{1,5},{5,1},{9,13},{13,9},{2,6},{6,2},{1... | collective-permute-start | bytes 49160 | tf_op jit(solution)/shard_map/ppermute | solution.py:31
  30.9 1.2 %collective-permute-done.8.refs_3_ = bf16[64,128]{1,0:T(8,128)(2,1)S(1)} collective-permute-done((bf16[64,128]{1,0:T(8,128)(2,1)S(1)}, bf16[64,128]{1,0:T(8,128)(2,1)S(1)}, u32[]{:S(2)}, u32[]{:S(2)}) %collective-permute-start.8) | collective-permute-done | bytes 16416 | tf_op jit(solution)/shard_map/ppermute | solution.py:31
  32.1 0.9 %collective-permute-done.7.refs_2_ = bf16[64,128]{1,0:T(8,128)(2,1)S(1)} collective-permute-done((bf16[64,128]{1,0:T(8,128)(2,1)S(1)}, bf16[64,128]{1,0:T(8,128)(2,1)S(1)}, u32[]{:S(2)}, u32[]{:S(2)}) %collective-permute-start.7) | collective-permute-done | bytes 16416 | tf_op jit(solution)/shard_map/ppermute | solution.py:31
  33.0 0.1 arrange.1.rows
  33.1 4.4 %output.1 = (f32[2,4096]{1,0:T(2,128)S(1)}, f32[2,4096]{1,0:T(2,128)S(1)}, f32[2,4096]{1,0:T(2,128)S(1)}, f32[2,4096]{1,0:T(2,128)S(1)}) custom-call(bf16[8,4096]{1,0:T(8,128)(2,1)S(1)} %arrange.1.rows, bf16[4096,4096]{1,0:T(8,128)(2,1)S(1)} %copy-done), custom_call_target="tpu_custom_call" | custom-call | flops 1000 | bytes 1000 | tf_op jit(solution)/shard_map/output/pallas_call | solution.py:319
  37.5 1.5 %collective-permute-start.10 = (f32[2,4096]{1,0:T(2,128)S(1)}, f32[2,4096]{1,0:T(2,128)S(1)}, u32[]{:S(2)}, u32[]{:S(2)}) collective-permute-start(f32[2,4096]{1,0:T(2,128)S(1)} %get-tuple-element.49), channel_id=1, source_target_pairs={{0,2},{1,3},{2,0},{3,1},{4,6},{5,7},{6,4},{7,5},{8,10},{9,11},{10,... | collective-permute-start | bytes 98312 | tf_op jit(solution)/shard_map/ppermute | solution.py:39
  39.0 0.4 collective-permute-start.11
  39.4 1.8 %collective-permute-done.9 = f32[2,4096]{1,0:T(2,128)S(1)} collective-permute-done((f32[2,4096]{1,0:T(2,128)S(1)}, f32[2,4096]{1,0:T(2,128)S(1)}, u32[]{:S(2)}, u32[]{:S(2)}) %collective-permute-start.9) | collective-permute-done | bytes 32800 | tf_op jit(solution)/shard_map/ppermute | solution.py:39
  41.2 0.4 collective-permute-done.10
  41.6 0.6 %add_convert_fusion = bf16[2,4096]{1,0:T(2,128)(2,1)} fusion(f32[2,4096]{1,0:T(2,128)S(1)} %collective-permute-done.11, f32[2,4096]{1,0:T(2,128)S(1)} %collective-permute-done.10, f32[2,4096]{1,0:T(2,128)S(1)} %get-tuple-element.47, f32[2,4096]{1,0:T(2,128)S(1)} %collective-permute-done.9), kind=kLoop, calls=%fused_computation | loop fusion | flops 32768 | bytes 147456 | tf_op jit(solution)/shard_map/convert_element_type | solution.py:427
  (24 shorter events, 0.1 us)
Async XLA Ops:
  0.0 0.7 %copy-start.5 = (bf16[2,4096]{1,0:T(2,128)(2,1)S(1)}, bf16[2,4096]{1,0:T(2,128)(2,1)}, u32[]{:S(2)}) copy-start(bf16[2,4096]{1,0:T(2,128)(2,1)} %refs_0_) | copy-start | bytes 49156
  0.0 3.8 %copy-start.2 = (bf16[4096,256]{1,0:T(8,128)(2,1)S(1)}, bf16[4096,256]{1,0:T(8,128)(2,1)}, u32[]{:S(2)}) copy-start(bf16[4096,256]{1,0:T(8,128)(2,1)} %value_weight.3) | copy-start | bytes 6291460
  0.0 3.8 %copy-start.1 = (bf16[4096,256]{1,0:T(8,128)(2,1)S(1)}, bf16[4096,256]{1,0:T(8,128)(2,1)}, u32[]{:S(2)}) copy-start(bf16[4096,256]{1,0:T(8,128)(2,1)} %key_weight.3) | copy-start | bytes 6291460
  0.7 6.6 %collective-permute-start.2 = (bf16[2,4096]{1,0:T(2,128)(2,1)S(1)}, bf16[2,4096]{1,0:T(2,128)(2,1)S(1)}, u32[]{:S(2)}, u32[]{:S(2)}) collective-permute-start(bf16[2,4096]{1,0:T(2,128)(2,1)S(1)} %copy-done.5), channel_id=1, source_target_pairs={{0,3},{1,2},{2,1},{3,0},{4,7},{5,6},{6,5},{7,4},{8,11},{9,10},{10,... | collective-permute-start | bytes 49160 | tf_op jit(solution)/shard_map/ppermute | solution.py:31
  3.1 4.2 %collective-permute-start.1 = (bf16[2,4096]{1,0:T(2,128)(2,1)S(1)}, bf16[2,4096]{1,0:T(2,128)(2,1)S(1)}, u32[]{:S(2)}, u32[]{:S(2)}) collective-permute-start(bf16[2,4096]{1,0:T(2,128)(2,1)S(1)} %copy-done.5), channel_id=1, source_target_pairs={{0,2},{1,3},{2,0},{3,1},{4,6},{5,7},{6,4},{7,5},{8,10},{9,11},{10,... | collective-permute-start | bytes 49160 | tf_op jit(solution)/shard_map/ppermute | solution.py:31
  3.7 3.6 %collective-permute-start = (bf16[2,4096]{1,0:T(2,128)(2,1)S(1)}, bf16[2,4096]{1,0:T(2,128)(2,1)S(1)}, u32[]{:S(2)}, u32[]{:S(2)}) collective-permute-start(bf16[2,4096]{1,0:T(2,128)(2,1)S(1)} %copy-done.5), channel_id=1, source_target_pairs={{0,1},{1,0},{2,3},{3,2},{4,5},{5,4},{6,7},{7,6},{8,9},{9,8},{10,11... | collective-permute-start | bytes 49160 | tf_op jit(solution)/shard_map/ppermute | solution.py:31
  16.5 4.6 %copy-start.6 = (s32[2]{0:T(128)S(1)}, s32[2]{0:T(128)}, u32[]{:S(2)}) copy-start(s32[2]{0:T(128)} %lengths.1) | copy-start | bytes 28
  16.5 8.9 %copy-start.3 = (bf16[2,2,2048,128]{3,2,1,0:T(8,128)(2,1)S(1)}, bf16[2,2,2048,128]{3,2,1,0:T(8,128)(2,1)}, u32[]{:S(2)}) copy-start(bf16[2,2,2048,128]{3,2,1,0:T(8,128)(2,1)} %key_cache.1) | copy-start | bytes 6291460
  16.5 8.9 %copy-start.4 = (bf16[2,2,2048,128]{3,2,1,0:T(8,128)(2,1)S(1)}, bf16[2,2,2048,128]{3,2,1,0:T(8,128)(2,1)}, u32[]{:S(2)}) copy-start(bf16[2,2,2048,128]{3,2,1,0:T(8,128)(2,1)} %cached_values.1) | copy-start | bytes 6291460
  16.6 16.5 %copy-start = (bf16[4096,4096]{1,0:T(8,128)(2,1)S(1)}, bf16[4096,4096]{1,0:T(8,128)(2,1)}, u32[]{:S(2)}) copy-start(bf16[4096,4096]{1,0:T(8,128)(2,1)} %w_out.1) | copy-start | bytes 100663296
  16.6 6.0 %collective-permute-start.3 = (f32[80,128]{1,0:T(8,128)S(1)}, f32[80,128]{1,0:T(8,128)S(1)}, u32[]{:S(2)}, u32[]{:S(2)}) collective-permute-start(f32[80,128]{1,0:T(8,128)S(1)} %get-tuple-element.44), channel_id=1, source_target_pairs={{0,12},{4,8},{8,4},{12,0},{1,13},{5,9},{9,5},{13,1},{2,14},{6,10},... | collective-permute-start | bytes 122888 | tf_op jit(solution)/shard_map/ppermute | solution.py:39
  20.5 4.9 %collective-permute-start.4 = (f32[80,128]{1,0:T(8,128)S(1)}, f32[80,128]{1,0:T(8,128)S(1)}, u32[]{:S(2)}, u32[]{:S(2)}) collective-permute-start(f32[80,128]{1,0:T(8,128)S(1)} %get-tuple-element.45), channel_id=1, source_target_pairs={{0,8},{4,12},{8,0},{12,4},{1,9},{5,13},{9,1},{13,5},{2,10},{6,14},... | collective-permute-start | bytes 122888 | tf_op jit(solution)/shard_map/ppermute | solution.py:39
  20.5 4.9 %collective-permute-start.5 = (f32[80,128]{1,0:T(8,128)S(1)}, f32[80,128]{1,0:T(8,128)S(1)}, u32[]{:S(2)}, u32[]{:S(2)}) collective-permute-start(f32[80,128]{1,0:T(8,128)S(1)} %get-tuple-element.46), channel_id=1, source_target_pairs={{0,4},{4,0},{8,12},{12,8},{1,5},{5,1},{9,13},{13,9},{2,6},{6,2},{1... | collective-permute-start | bytes 122888 | tf_op jit(solution)/shard_map/ppermute | solution.py:39
  26.4 5.7 %collective-permute-start.8 = (bf16[64,128]{1,0:T(8,128)(2,1)S(1)}, bf16[64,128]{1,0:T(8,128)(2,1)S(1)}, u32[]{:S(2)}, u32[]{:S(2)}) collective-permute-start(bf16[64,128]{1,0:T(8,128)(2,1)S(1)} %attend.1.refs_0_), channel_id=1, source_target_pairs={{0,12},{4,8},{8,4},{12,0},{1,13},{5,9},{9,5},{13,1},{2,14},{6,10},... | collective-permute-start | bytes 49160 | tf_op jit(solution)/shard_map/ppermute | solution.py:31
  28.3 4.6 %collective-permute-start.7 = (bf16[64,128]{1,0:T(8,128)(2,1)S(1)}, bf16[64,128]{1,0:T(8,128)(2,1)S(1)}, u32[]{:S(2)}, u32[]{:S(2)}) collective-permute-start(bf16[64,128]{1,0:T(8,128)(2,1)S(1)} %attend.1.refs_0_), channel_id=1, source_target_pairs={{0,8},{4,12},{8,0},{12,4},{1,9},{5,13},{9,1},{13,5},{2,10},{6,14},... | collective-permute-start | bytes 49160 | tf_op jit(solution)/shard_map/ppermute | solution.py:31
  28.6 4.4 %collective-permute-start.6 = (bf16[64,128]{1,0:T(8,128)(2,1)S(1)}, bf16[64,128]{1,0:T(8,128)(2,1)S(1)}, u32[]{:S(2)}, u32[]{:S(2)}) collective-permute-start(bf16[64,128]{1,0:T(8,128)(2,1)S(1)} %attend.1.refs_0_), channel_id=1, source_target_pairs={{0,4},{4,0},{8,12},{12,8},{1,5},{5,1},{9,13},{13,9},{2,6},{6,2},{1... | collective-permute-start | bytes 49160 | tf_op jit(solution)/shard_map/ppermute | solution.py:31
  37.5 3.7 %collective-permute-start.9 = (f32[2,4096]{1,0:T(2,128)S(1)}, f32[2,4096]{1,0:T(2,128)S(1)}, u32[]{:S(2)}, u32[]{:S(2)}) collective-permute-start(f32[2,4096]{1,0:T(2,128)S(1)} %get-tuple-element.48), channel_id=1, source_target_pairs={{0,3},{1,2},{2,1},{3,0},{4,7},{5,6},{6,5},{7,4},{8,11},{9,10},{10,... | collective-permute-start | bytes 98312 | tf_op jit(solution)/shard_map/ppermute | solution.py:39
  37.5 4.0 %collective-permute-start.10 = (f32[2,4096]{1,0:T(2,128)S(1)}, f32[2,4096]{1,0:T(2,128)S(1)}, u32[]{:S(2)}, u32[]{:S(2)}) collective-permute-start(f32[2,4096]{1,0:T(2,128)S(1)} %get-tuple-element.49), channel_id=1, source_target_pairs={{0,2},{1,3},{2,0},{3,1},{4,6},{5,7},{6,4},{7,5},{8,10},{9,11},{10,... | collective-permute-start | bytes 98312 | tf_op jit(solution)/shard_map/ppermute | solution.py:39
  39.0 2.6 %collective-permute-start.11 = (f32[2,4096]{1,0:T(2,128)S(1)}, f32[2,4096]{1,0:T(2,128)S(1)}, u32[]{:S(2)}, u32[]{:S(2)}) collective-permute-start(f32[2,4096]{1,0:T(2,128)S(1)} %get-tuple-element.50), channel_id=1, source_target_pairs={{0,1},{1,0},{2,3},{3,2},{4,5},{5,4},{6,7},{7,6},{8,9},{9,8},{10,11... | collective-permute-start | bytes 98312 | tf_op jit(solution)/shard_map/ppermute | solution.py:39

commit v5 on v4

--- a/solution.py
+++ b/solution.py
@@ -274,7 +274,7 @@
 
 
 def arrange_kernel(*refs, pieces, heads, place):
-    inputs, (rows, laid, total) = refs[:pieces], refs[pieces:]
+    inputs, (rows, laid, total) = refs[:pieces][::-1], refs[pieces:]
     for t, piece in enumerate(inputs):
         laid[place(t)] = piece[...].astype(jnp.float32)
     flat = laid.reshape(laid.shape[0] * laid.shape[1], LANES)
@@ -302,7 +302,7 @@
         compiler_params=pltpu.CompilerParams(vmem_limit_bytes=6 * MIB),
         cost_estimate=pl.CostEstimate(flops=1000, bytes_accessed=1000, transcendentals=0),
         name="arrange",
-    )(*pieces)
+    )(*pieces[::-1])
 
 
 def output_kernel(rows, w_out, *outs, rows_out):
@@ -399,7 +399,7 @@
     def place(t):
         return target(peer(lax.axis_index("wide"), t, wide))
 
-    frequency, hidden = lax.optimization_barrier((frequencies(head_dim, 100), hidden))
+    frequency = frequencies(head_dim, 100)
     hidden_pieces = gather_pieces(hidden, "narrow", narrow)
     parts = project(
         lambda t: place(t) * row_count,
@@ -422,7 +422,7 @@
     sums = output(rows, w_out, rows_out, narrow)
     sums = scatter_pieces(sums, "narrow", narrow)
     result = sums[0]
-    for s in sums[1:]:
+    for s in sums[-1:] + sums[1:-1]:
         result = result + s
     return result.astype(jnp.bfloat16)
 

time: 42.4 us -> 41.9 us (0.988)
  local copies, waits for them, and re-layouts: 0.74 us -> 0.04 us
    unnamed x14, local copies, waits for them, and re-layouts: 0.74 us -> 0.04 us
where the time goes in v5:
time: 41.9 us; the launch traced here: 41.7 us
  Pallas kernels  18.8 us (45%)
  starting transfers between devices  14.3 us (34%)
  waiting for transfers between devices  7.81 us (19%)
  other arithmetic  0.64 us (2%)
    pallas_call x1, Pallas kernels, project(): pl.pallas_call(functools.partial(project_kernel, pieces=len(hidden_pieces...  9.17 us
    ppermute x6, starting transfers between devices, gather_pieces(): lax.ppermute(piece, axis, xor_pairs(count, t))  7.54 us
    ppermute x6, starting transfers between devices, scatter_pieces(): lax.ppermute(pieces[t], axis, xor_pairs(count, t))  6.72 us
    ppermute x6, waiting for transfers between devices, scatter_pieces(): lax.ppermute(pieces[t], axis, xor_pairs(count, t))  5.84 us
    pallas_call x1, Pallas kernels, output(): pl.pallas_call(functools.partial(output_kernel, rows_out=rows_out), out_s...  4.44 us
    pallas_call x1, Pallas kernels, load(): pl.pallas_call(load_kernel, out_shape=jax.ShapeDtypeStruct(shape, w_query...  3.51 us
    ppermute x6, waiting for transfers between devices, gather_pieces(): lax.ppermute(piece, axis, xor_pairs(count, t))  1.97 us
    pallas_call x1, Pallas kernels, attend(): pl.pallas_call(functools.partial(attend_kernel, heads=heads, kv=kv, strid...  0.99 us
  transfers between devices with their start and end apart: 12, of which 6 were waited for; matrix products, arithmetic and copies ran while one was open for 0% of the time, Pallas kernels for 10%

profile of v5, /device:TPU:0, one launch (start us, length us, event | category | flops | bytes accessed | tf_op | source)
XLA Modules:
  0.0 41.7 jit_solution(18349224789723469239)
XLA Ops:
  0.0 0.5 %collective-permute-start = (bf16[2,4096]{1,0:T(2,128)(2,1)}, bf16[2,4096]{1,0:T(2,128)(2,1)S(1)}, u32[]{:S(2)}, u32[]{:S(2)}) collective-permute-start(bf16[2,4096]{1,0:T(2,128)(2,1)} %refs_0_.1), channel_id=1, source_target_pairs={{0,1},{1,0},{2,3},{3,2},{4,5},{5,4},{6,7},{7,6},{8,9},{9,8},{10,11... | collective-permute-start | bytes 49160 | tf_op jit(solution)/shard_map/ppermute | solution.py:31
  0.5 2.6 %collective-permute-start.1 = (bf16[2,4096]{1,0:T(2,128)(2,1)}, bf16[2,4096]{1,0:T(2,128)(2,1)S(1)}, u32[]{:S(2)}, u32[]{:S(2)}) collective-permute-start(bf16[2,4096]{1,0:T(2,128)(2,1)} %refs_0_.1), channel_id=1, source_target_pairs={{0,2},{1,3},{2,0},{3,1},{4,6},{5,7},{6,4},{7,5},{8,10},{9,11},{10,... | collective-permute-start | bytes 49160 | tf_op jit(solution)/shard_map/ppermute | solution.py:31
  3.0 0.1 collective-permute-start.2
  3.1 3.5 %load.1.head = bf16[1024,4096]{1,0:T(8,128)(2,1)S(1)} custom-call(bf16[4096,4096]{1,0:T(8,128)(2,1)} %w_query.3, bf16[4096,256]{1,0:T(8,128)(2,1)S(1)} %copy-done.1, bf16[4096,256]{1,0:T(8,128)(2,1)S(1)} %copy-done.2), custom_call_target="tpu_custom_call" | custom-call | flops 1000 | bytes 8388608 | tf_op jit(solution)/shard_map/load/pallas_call | solution.py:78
  6.7 9.2 %project.1 = (f32[80,128]{1,0:T(8,128)S(1)}, f32[80,128]{1,0:T(8,128)S(1)}, f32[80,128]{1,0:T(8,128)S(1)}, f32[80,128]{1,0:T(8,128)S(1)}) custom-call(bf16[1024,4096]{1,0:T(8,128)(2,1)S(1)} %load.1.head, bf16[4096,256]{1,0:T(8,128)(2,1)S(1)} %copy-done.1, bf16[4096,256]{1,0:T(8,128)(2,1)S(1)} %copy-done.2, bf16[4096,4096]{1,0:T(8,128)(2,1)} %w_query.3, ...), custom_call_target="tpu_custom_call" | custom-call | flops 1000 | bytes 1000 | tf_op jit(solution)/shard_map/project/pallas_call | solution.py:154
  15.9 0.0 copy-start.4
  16.0 4.2 %collective-permute-start.3 = (f32[80,128]{1,0:T(8,128)S(1)}, f32[80,128]{1,0:T(8,128)S(1)}, u32[]{:S(2)}, u32[]{:S(2)}) collective-permute-start(f32[80,128]{1,0:T(8,128)S(1)} %get-tuple-element.40), channel_id=1, source_target_pairs={{0,12},{4,8},{8,4},{12,0},{1,13},{5,9},{9,5},{13,1},{2,14},{6,10},... | collective-permute-start | bytes 122888 | tf_op jit(solution)/shard_map/ppermute | solution.py:39
  20.2 0.6 %collective-permute-start.5 = (f32[80,128]{1,0:T(8,128)S(1)}, f32[80,128]{1,0:T(8,128)S(1)}, u32[]{:S(2)}, u32[]{:S(2)}) collective-permute-start(f32[80,128]{1,0:T(8,128)S(1)} %get-tuple-element.42), channel_id=1, source_target_pairs={{0,4},{4,0},{8,12},{12,8},{1,5},{5,1},{9,13},{13,9},{2,6},{6,2},{1... | collective-permute-start | bytes 122888 | tf_op jit(solution)/shard_map/ppermute | solution.py:39
  20.8 0.6 %tables.1 = (s32[2,128]{1,0:T(2,128)S(1)}, f32[2,128]{1,0:T(2,128)S(1)}, f32[2,128]{1,0:T(2,128)S(1)}) custom-call(s32[2]{0:T(128)S(1)} %copy-done.6, f32[8,128]{1,0:T(8,128)S(1)} %get-tuple-element.35.frequency), custom_call_target="tpu_custom_call" | custom-call | flops 1000 | bytes 1000 | tf_op jit(solution)/shard_map/tables/pallas_call | solution.py:364
  21.4 0.8 %collective-permute-done.3.refs_1_ = f32[80,128]{1,0:T(8,128)S(1)} collective-permute-done((f32[80,128]{1,0:T(8,128)S(1)}, f32[80,128]{1,0:T(8,128)S(1)}, u32[]{:S(2)}, u32[]{:S(2)}) %collective-permute-start.3) | collective-permute-done | bytes 40992 | tf_op jit(solution)/shard_map/ppermute | solution.py:39
  22.2 2.9 %collective-permute-done.4.refs_2_ = f32[80,128]{1,0:T(8,128)S(1)} collective-permute-done((f32[80,128]{1,0:T(8,128)S(1)}, f32[80,128]{1,0:T(8,128)S(1)}, u32[]{:S(2)}, u32[]{:S(2)}) %collective-permute-start.4) | collective-permute-done | bytes 40992 | tf_op jit(solution)/shard_map/ppermute | solution.py:39
  25.1 1.0 %attend.1.refs_3_ = bf16[64,128]{1,0:T(8,128)(2,1)S(1)} custom-call(s32[2,128]{1,0:T(2,128)S(1)} %get-tuple-element.36.limits, f32[2,128]{1,0:T(2,128)S(1)} %get-tuple-element.37.cosine, f32[2,128]{1,0:T(2,128)S(1)} %get-tuple-element.38.sine, bf16[2,2,2048,128]{3,2,1,0:T(8,128)(2,1)S(1)} %copy-done.3, bf16[2,2,2048,128]{3,2,1,0:T(8,128)(2,1)S(1)} %copy-done.4, ...), custom_call_target="tpu_custom_call" | custom-call | flops 1000 | bytes 1000 | tf_op jit(solution)/shard_map/attend/pallas_call | solution.py:260
  26.1 1.8 %collective-permute-start.6 = (bf16[64,128]{1,0:T(8,128)(2,1)S(1)}, bf16[64,128]{1,0:T(8,128)(2,1)S(1)}, u32[]{:S(2)}, u32[]{:S(2)}) collective-permute-start(bf16[64,128]{1,0:T(8,128)(2,1)S(1)} %attend.1.refs_3_), channel_id=1, source_target_pairs={{0,12},{4,8},{8,4},{12,0},{1,13},{5,9},{9,5},{13,1},{2,14},{6,10},... | collective-permute-start | bytes 49160 | tf_op jit(solution)/shard_map/ppermute | solution.py:31
  27.9 0.4 collective-permute-start.7
  28.2 2.3 %collective-permute-start.8 = (bf16[64,128]{1,0:T(8,128)(2,1)S(1)}, bf16[64,128]{1,0:T(8,128)(2,1)S(1)}, u32[]{:S(2)}, u32[]{:S(2)}) collective-permute-start(bf16[64,128]{1,0:T(8,128)(2,1)S(1)} %attend.1.refs_3_), channel_id=1, source_target_pairs={{0,4},{4,0},{8,12},{12,8},{1,5},{5,1},{9,13},{13,9},{2,6},{6,2},{1... | collective-permute-start | bytes 49160 | tf_op jit(solution)/shard_map/ppermute | solution.py:31
  30.5 1.1 %collective-permute-done.6.refs_0_ = bf16[64,128]{1,0:T(8,128)(2,1)S(1)} collective-permute-done((bf16[64,128]{1,0:T(8,128)(2,1)S(1)}, bf16[64,128]{1,0:T(8,128)(2,1)S(1)}, u32[]{:S(2)}, u32[]{:S(2)}) %collective-permute-start.6) | collective-permute-done | bytes 16416 | tf_op jit(solution)/shard_map/ppermute | solution.py:31
  31.7 0.8 %collective-permute-done.7.refs_1_ = bf16[64,128]{1,0:T(8,128)(2,1)S(1)} collective-permute-done((bf16[64,128]{1,0:T(8,128)(2,1)S(1)}, bf16[64,128]{1,0:T(8,128)(2,1)S(1)}, u32[]{:S(2)}, u32[]{:S(2)}) %collective-permute-start.7) | collective-permute-done | bytes 16416 | tf_op jit(solution)/shard_map/ppermute | solution.py:31
  32.5 0.1 arrange.1.rows
  32.6 4.4 %output.1 = (f32[2,4096]{1,0:T(2,128)S(1)}, f32[2,4096]{1,0:T(2,128)S(1)}, f32[2,4096]{1,0:T(2,128)S(1)}, f32[2,4096]{1,0:T(2,128)S(1)}) custom-call(bf16[8,4096]{1,0:T(8,128)(2,1)S(1)} %arrange.1.rows, bf16[4096,4096]{1,0:T(8,128)(2,1)S(1)} %copy-done), custom_call_target="tpu_custom_call" | custom-call | flops 1000 | bytes 1000 | tf_op jit(solution)/shard_map/output/pallas_call | solution.py:319
  37.0 1.5 %collective-permute-start.11 = (f32[2,4096]{1,0:T(2,128)S(1)}, f32[2,4096]{1,0:T(2,128)S(1)}, u32[]{:S(2)}, u32[]{:S(2)}) collective-permute-start(f32[2,4096]{1,0:T(2,128)S(1)} %get-tuple-element.46), channel_id=1, source_target_pairs={{0,2},{1,3},{2,0},{3,1},{4,6},{5,7},{6,4},{7,5},{8,10},{9,11},{10,... | collective-permute-start | bytes 98312 | tf_op jit(solution)/shard_map/ppermute | solution.py:39
  38.6 0.3 collective-permute-start.9
  38.9 1.8 %collective-permute-done.10 = f32[2,4096]{1,0:T(2,128)S(1)} collective-permute-done((f32[2,4096]{1,0:T(2,128)S(1)}, f32[2,4096]{1,0:T(2,128)S(1)}, u32[]{:S(2)}, u32[]{:S(2)}) %collective-permute-start.10) | collective-permute-done | bytes 32800 | tf_op jit(solution)/shard_map/ppermute | solution.py:39
  40.7 0.4 collective-permute-done.11
  41.1 0.6 %add_convert_fusion = bf16[2,4096]{1,0:T(2,128)(2,1)} fusion(f32[2,4096]{1,0:T(2,128)S(1)} %collective-permute-done.11, f32[2,4096]{1,0:T(2,128)S(1)} %collective-permute-done.10, f32[2,4096]{1,0:T(2,128)S(1)} %get-tuple-element.43, f32[2,4096]{1,0:T(2,128)S(1)} %collective-permute-done.9), kind=kLoop, calls=%fused_computation | loop fusion | flops 32768 | bytes 147456 | tf_op jit(solution)/shard_map/convert_element_type | solution.py:427
  (24 shorter events, 0.1 us)
Async XLA Ops:
  0.0 3.1 %copy-start.1 = (bf16[4096,256]{1,0:T(8,128)(2,1)S(1)}, bf16[4096,256]{1,0:T(8,128)(2,1)}, u32[]{:S(2)}) copy-start(bf16[4096,256]{1,0:T(8,128)(2,1)} %key_weight.3) | copy-start | bytes 6291460
  0.0 3.1 %copy-start.2 = (bf16[4096,256]{1,0:T(8,128)(2,1)S(1)}, bf16[4096,256]{1,0:T(8,128)(2,1)}, u32[]{:S(2)}) copy-start(bf16[4096,256]{1,0:T(8,128)(2,1)} %value_weight.3) | copy-start | bytes 6291460
  0.0 6.6 %collective-permute-start = (bf16[2,4096]{1,0:T(2,128)(2,1)}, bf16[2,4096]{1,0:T(2,128)(2,1)S(1)}, u32[]{:S(2)}, u32[]{:S(2)}) collective-permute-start(bf16[2,4096]{1,0:T(2,128)(2,1)} %refs_0_.1), channel_id=1, source_target_pairs={{0,1},{1,0},{2,3},{3,2},{4,5},{5,4},{6,7},{7,6},{8,9},{9,8},{10,11... | collective-permute-start | bytes 49160 | tf_op jit(solution)/shard_map/ppermute | solution.py:31
  0.5 6.2 %collective-permute-start.1 = (bf16[2,4096]{1,0:T(2,128)(2,1)}, bf16[2,4096]{1,0:T(2,128)(2,1)S(1)}, u32[]{:S(2)}, u32[]{:S(2)}) collective-permute-start(bf16[2,4096]{1,0:T(2,128)(2,1)} %refs_0_.1), channel_id=1, source_target_pairs={{0,2},{1,3},{2,0},{3,1},{4,6},{5,7},{6,4},{7,5},{8,10},{9,11},{10,... | collective-permute-start | bytes 49160 | tf_op jit(solution)/shard_map/ppermute | solution.py:31
  3.0 3.6 %collective-permute-start.2 = (bf16[2,4096]{1,0:T(2,128)(2,1)}, bf16[2,4096]{1,0:T(2,128)(2,1)S(1)}, u32[]{:S(2)}, u32[]{:S(2)}) collective-permute-start(bf16[2,4096]{1,0:T(2,128)(2,1)} %refs_0_.1), channel_id=1, source_target_pairs={{0,3},{1,2},{2,1},{3,0},{4,7},{5,6},{6,5},{7,4},{8,11},{9,10},{10,... | collective-permute-start | bytes 49160 | tf_op jit(solution)/shard_map/ppermute | solution.py:31
  3.1 3.6 %copy-start.5 = (bf16[2,4096]{1,0:T(2,128)(2,1)S(1)}, bf16[2,4096]{1,0:T(2,128)(2,1)}, u32[]{:S(2)}) copy-start(bf16[2,4096]{1,0:T(2,128)(2,1)} %refs_0_.1) | copy-start | bytes 49156
  15.9 4.9 %copy-start.6 = (s32[2]{0:T(128)S(1)}, s32[2]{0:T(128)}, u32[]{:S(2)}) copy-start(s32[2]{0:T(128)} %lengths.1) | copy-start | bytes 28
  15.9 9.2 %copy-start.3 = (bf16[2,2,2048,128]{3,2,1,0:T(8,128)(2,1)S(1)}, bf16[2,2,2048,128]{3,2,1,0:T(8,128)(2,1)}, u32[]{:S(2)}) copy-start(bf16[2,2,2048,128]{3,2,1,0:T(8,128)(2,1)} %key_cache.1) | copy-start | bytes 6291460
  15.9 9.2 %copy-start.4 = (bf16[2,2,2048,128]{3,2,1,0:T(8,128)(2,1)S(1)}, bf16[2,2,2048,128]{3,2,1,0:T(8,128)(2,1)}, u32[]{:S(2)}) copy-start(bf16[2,2,2048,128]{3,2,1,0:T(8,128)(2,1)} %cached_values.1) | copy-start | bytes 6291460
  15.9 16.7 %copy-start = (bf16[4096,4096]{1,0:T(8,128)(2,1)S(1)}, bf16[4096,4096]{1,0:T(8,128)(2,1)}, u32[]{:S(2)}) copy-start(bf16[4096,4096]{1,0:T(8,128)(2,1)} %w_out.1) | copy-start | bytes 100663296
  16.0 6.2 %collective-permute-start.3 = (f32[80,128]{1,0:T(8,128)S(1)}, f32[80,128]{1,0:T(8,128)S(1)}, u32[]{:S(2)}, u32[]{:S(2)}) collective-permute-start(f32[80,128]{1,0:T(8,128)S(1)} %get-tuple-element.40), channel_id=1, source_target_pairs={{0,12},{4,8},{8,4},{12,0},{1,13},{5,9},{9,5},{13,1},{2,14},{6,10},... | collective-permute-start | bytes 122888 | tf_op jit(solution)/shard_map/ppermute | solution.py:39
  20.2 4.9 %collective-permute-start.4 = (f32[80,128]{1,0:T(8,128)S(1)}, f32[80,128]{1,0:T(8,128)S(1)}, u32[]{:S(2)}, u32[]{:S(2)}) collective-permute-start(f32[80,128]{1,0:T(8,128)S(1)} %get-tuple-element.41), channel_id=1, source_target_pairs={{0,8},{4,12},{8,0},{12,4},{1,9},{5,13},{9,1},{13,5},{2,10},{6,14},... | collective-permute-start | bytes 122888 | tf_op jit(solution)/shard_map/ppermute | solution.py:39
  20.2 4.9 %collective-permute-start.5 = (f32[80,128]{1,0:T(8,128)S(1)}, f32[80,128]{1,0:T(8,128)S(1)}, u32[]{:S(2)}, u32[]{:S(2)}) collective-permute-start(f32[80,128]{1,0:T(8,128)S(1)} %get-tuple-element.42), channel_id=1, source_target_pairs={{0,4},{4,0},{8,12},{12,8},{1,5},{5,1},{9,13},{13,9},{2,6},{6,2},{1... | collective-permute-start | bytes 122888 | tf_op jit(solution)/shard_map/ppermute | solution.py:39
  26.1 5.6 %collective-permute-start.6 = (bf16[64,128]{1,0:T(8,128)(2,1)S(1)}, bf16[64,128]{1,0:T(8,128)(2,1)S(1)}, u32[]{:S(2)}, u32[]{:S(2)}) collective-permute-start(bf16[64,128]{1,0:T(8,128)(2,1)S(1)} %attend.1.refs_3_), channel_id=1, source_target_pairs={{0,12},{4,8},{8,4},{12,0},{1,13},{5,9},{9,5},{13,1},{2,14},{6,10},... | collective-permute-start | bytes 49160 | tf_op jit(solution)/shard_map/ppermute | solution.py:31
  27.9 4.6 %collective-permute-start.7 = (bf16[64,128]{1,0:T(8,128)(2,1)S(1)}, bf16[64,128]{1,0:T(8,128)(2,1)S(1)}, u32[]{:S(2)}, u32[]{:S(2)}) collective-permute-start(bf16[64,128]{1,0:T(8,128)(2,1)S(1)} %attend.1.refs_3_), channel_id=1, source_target_pairs={{0,8},{4,12},{8,0},{12,4},{1,9},{5,13},{9,1},{13,5},{2,10},{6,14},... | collective-permute-start | bytes 49160 | tf_op jit(solution)/shard_map/ppermute | solution.py:31
  28.2 4.3 %collective-permute-start.8 = (bf16[64,128]{1,0:T(8,128)(2,1)S(1)}, bf16[64,128]{1,0:T(8,128)(2,1)S(1)}, u32[]{:S(2)}, u32[]{:S(2)}) collective-permute-start(bf16[64,128]{1,0:T(8,128)(2,1)S(1)} %attend.1.refs_3_), channel_id=1, source_target_pairs={{0,4},{4,0},{8,12},{12,8},{1,5},{5,1},{9,13},{13,9},{2,6},{6,2},{1... | collective-permute-start | bytes 49160 | tf_op jit(solution)/shard_map/ppermute | solution.py:31
  37.0 3.7 %collective-permute-start.10 = (f32[2,4096]{1,0:T(2,128)S(1)}, f32[2,4096]{1,0:T(2,128)S(1)}, u32[]{:S(2)}, u32[]{:S(2)}) collective-permute-start(f32[2,4096]{1,0:T(2,128)S(1)} %get-tuple-element.45), channel_id=1, source_target_pairs={{0,3},{1,2},{2,1},{3,0},{4,7},{5,6},{6,5},{7,4},{8,11},{9,10},{10,... | collective-permute-start | bytes 98312 | tf_op jit(solution)/shard_map/ppermute | solution.py:39
  37.0 4.0 %collective-permute-start.11 = (f32[2,4096]{1,0:T(2,128)S(1)}, f32[2,4096]{1,0:T(2,128)S(1)}, u32[]{:S(2)}, u32[]{:S(2)}) collective-permute-start(f32[2,4096]{1,0:T(2,128)S(1)} %get-tuple-element.46), channel_id=1, source_target_pairs={{0,2},{1,3},{2,0},{3,1},{4,6},{5,7},{6,4},{7,5},{8,10},{9,11},{10,... | collective-permute-start | bytes 98312 | tf_op jit(solution)/shard_map/ppermute | solution.py:39
  38.6 2.5 %collective-permute-start.9 = (f32[2,4096]{1,0:T(2,128)S(1)}, f32[2,4096]{1,0:T(2,128)S(1)}, u32[]{:S(2)}, u32[]{:S(2)}) collective-permute-start(f32[2,4096]{1,0:T(2,128)S(1)} %get-tuple-element.44), channel_id=1, source_target_pairs={{0,1},{1,0},{2,3},{3,2},{4,5},{5,4},{6,7},{7,6},{8,9},{9,8},{10,11... | collective-permute-start | bytes 98312 | tf_op jit(solution)/shard_map/ppermute | solution.py:39

commit v6 on v5

--- a/solution.py
+++ b/solution.py
@@ -170,7 +170,7 @@
         scratch_shapes=[
             pltpu.VMEM((count, width), jnp.bfloat16),
             pltpu.VMEM((count, columns), jnp.float32),
-            pltpu.VMEM((count * stride, LANES), jnp.float32),
+            pltpu.VMEM(((count + 1) * stride, LANES), jnp.float32),
             pltpu.VMEM((SLOTS, depth, columns // CUTS), jnp.bfloat16),
             pltpu.SemaphoreType.DMA((SLOTS,)),
         ],
@@ -296,7 +296,7 @@
         in_specs=[vmem()] * len(pieces),
         out_specs=vmem(),
         scratch_shapes=[
-            pltpu.VMEM((len(pieces), row_count * heads, LANES), jnp.float32),
+            pltpu.VMEM((len(pieces) + 1, row_count * heads, LANES), jnp.float32),
             pltpu.VMEM((count, heads * LANES), jnp.float32),
         ],
         compiler_params=pltpu.CompilerParams(vmem_limit_bytes=6 * MIB),

time: 41.9 us -> 41.9 us (level)
  no operation moved by 1% of the time
where the time goes in v6:
time: 41.9 us; the launch traced here: 41.7 us
  Pallas kernels  18.8 us (45%)
  starting transfers between devices  14.3 us (34%)
  waiting for transfers between devices  7.81 us (19%)
  other arithmetic  0.64 us (2%)
    pallas_call x1, Pallas kernels, project(): pl.pallas_call(functools.partial(project_kernel, pieces=len(hidden_pieces...  9.17 us
    ppermute x6, starting transfers between devices, gather_pieces(): lax.ppermute(piece, axis, xor_pairs(count, t))  7.54 us
    ppermute x6, starting transfers between devices, scatter_pieces(): lax.ppermute(pieces[t], axis, xor_pairs(count, t))  6.72 us
    ppermute x6, waiting for transfers between devices, scatter_pieces(): lax.ppermute(pieces[t], axis, xor_pairs(count, t))  5.84 us
    pallas_call x1, Pallas kernels, output(): pl.pallas_call(functools.partial(output_kernel, rows_out=rows_out), out_s...  4.44 us
    pallas_call x1, Pallas kernels, load(): pl.pallas_call(load_kernel, out_shape=jax.ShapeDtypeStruct(shape, w_query...  3.51 us
    ppermute x6, waiting for transfers between devices, gather_pieces(): lax.ppermute(piece, axis, xor_pairs(count, t))  1.97 us
    pallas_call x1, Pallas kernels, attend(): pl.pallas_call(functools.partial(attend_kernel, heads=heads, kv=kv, strid...  0.99 us
  transfers between devices with their start and end apart: 12, of which 6 were waited for; matrix products, arithmetic and copies ran while one was open for 0% of the time, Pallas kernels for 10%

profile of v6, /device:TPU:0, one launch (start us, length us, event | category | flops | bytes accessed | tf_op | source)
XLA Modules:
  0.0 41.7 jit_solution(9494892111353774167)
XLA Ops:
  0.0 0.5 %collective-permute-start = (bf16[2,4096]{1,0:T(2,128)(2,1)}, bf16[2,4096]{1,0:T(2,128)(2,1)S(1)}, u32[]{:S(2)}, u32[]{:S(2)}) collective-permute-start(bf16[2,4096]{1,0:T(2,128)(2,1)} %refs_0_.1), channel_id=1, source_target_pairs={{0,1},{1,0},{2,3},{3,2},{4,5},{5,4},{6,7},{7,6},{8,9},{9,8},{10,11... | collective-permute-start | bytes 49160 | tf_op jit(solution)/shard_map/ppermute | solution.py:31
  0.5 2.6 %collective-permute-start.1 = (bf16[2,4096]{1,0:T(2,128)(2,1)}, bf16[2,4096]{1,0:T(2,128)(2,1)S(1)}, u32[]{:S(2)}, u32[]{:S(2)}) collective-permute-start(bf16[2,4096]{1,0:T(2,128)(2,1)} %refs_0_.1), channel_id=1, source_target_pairs={{0,2},{1,3},{2,0},{3,1},{4,6},{5,7},{6,4},{7,5},{8,10},{9,11},{10,... | collective-permute-start | bytes 49160 | tf_op jit(solution)/shard_map/ppermute | solution.py:31
  3.0 0.1 collective-permute-start.2
  3.1 3.5 %load.1.head = bf16[1024,4096]{1,0:T(8,128)(2,1)S(1)} custom-call(bf16[4096,4096]{1,0:T(8,128)(2,1)} %w_query.3, bf16[4096,256]{1,0:T(8,128)(2,1)S(1)} %copy-done.1, bf16[4096,256]{1,0:T(8,128)(2,1)S(1)} %copy-done.2), custom_call_target="tpu_custom_call" | custom-call | flops 1000 | bytes 8388608 | tf_op jit(solution)/shard_map/load/pallas_call | solution.py:78
  6.7 9.2 %project.1 = (f32[80,128]{1,0:T(8,128)S(1)}, f32[80,128]{1,0:T(8,128)S(1)}, f32[80,128]{1,0:T(8,128)S(1)}, f32[80,128]{1,0:T(8,128)S(1)}) custom-call(bf16[1024,4096]{1,0:T(8,128)(2,1)S(1)} %load.1.head, bf16[4096,256]{1,0:T(8,128)(2,1)S(1)} %copy-done.1, bf16[4096,256]{1,0:T(8,128)(2,1)S(1)} %copy-done.2, bf16[4096,4096]{1,0:T(8,128)(2,1)} %w_query.3, ...), custom_call_target="tpu_custom_call" | custom-call | flops 1000 | bytes 1000 | tf_op jit(solution)/shard_map/project/pallas_call | solution.py:154
  15.9 0.0 copy-start.4
  16.0 4.2 %collective-permute-start.3 = (f32[80,128]{1,0:T(8,128)S(1)}, f32[80,128]{1,0:T(8,128)S(1)}, u32[]{:S(2)}, u32[]{:S(2)}) collective-permute-start(f32[80,128]{1,0:T(8,128)S(1)} %get-tuple-element.40), channel_id=1, source_target_pairs={{0,12},{4,8},{8,4},{12,0},{1,13},{5,9},{9,5},{13,1},{2,14},{6,10},... | collective-permute-start | bytes 122888 | tf_op jit(solution)/shard_map/ppermute | solution.py:39
  20.2 0.6 %collective-permute-start.5 = (f32[80,128]{1,0:T(8,128)S(1)}, f32[80,128]{1,0:T(8,128)S(1)}, u32[]{:S(2)}, u32[]{:S(2)}) collective-permute-start(f32[80,128]{1,0:T(8,128)S(1)} %get-tuple-element.42), channel_id=1, source_target_pairs={{0,4},{4,0},{8,12},{12,8},{1,5},{5,1},{9,13},{13,9},{2,6},{6,2},{1... | collective-permute-start | bytes 122888 | tf_op jit(solution)/shard_map/ppermute | solution.py:39
  20.8 0.6 %tables.1 = (s32[2,128]{1,0:T(2,128)S(1)}, f32[2,128]{1,0:T(2,128)S(1)}, f32[2,128]{1,0:T(2,128)S(1)}) custom-call(s32[2]{0:T(128)S(1)} %copy-done.6, f32[8,128]{1,0:T(8,128)S(1)} %get-tuple-element.35.frequency), custom_call_target="tpu_custom_call" | custom-call | flops 1000 | bytes 1000 | tf_op jit(solution)/shard_map/tables/pallas_call | solution.py:364
  21.4 0.8 %collective-permute-done.3.refs_1_ = f32[80,128]{1,0:T(8,128)S(1)} collective-permute-done((f32[80,128]{1,0:T(8,128)S(1)}, f32[80,128]{1,0:T(8,128)S(1)}, u32[]{:S(2)}, u32[]{:S(2)}) %collective-permute-start.3) | collective-permute-done | bytes 40992 | tf_op jit(solution)/shard_map/ppermute | solution.py:39
  22.2 2.9 %collective-permute-done.4.refs_2_ = f32[80,128]{1,0:T(8,128)S(1)} collective-permute-done((f32[80,128]{1,0:T(8,128)S(1)}, f32[80,128]{1,0:T(8,128)S(1)}, u32[]{:S(2)}, u32[]{:S(2)}) %collective-permute-start.4) | collective-permute-done | bytes 40992 | tf_op jit(solution)/shard_map/ppermute | solution.py:39
  25.1 1.0 %attend.1.refs_3_ = bf16[64,128]{1,0:T(8,128)(2,1)S(1)} custom-call(s32[2,128]{1,0:T(2,128)S(1)} %get-tuple-element.36.limits, f32[2,128]{1,0:T(2,128)S(1)} %get-tuple-element.37.cosine, f32[2,128]{1,0:T(2,128)S(1)} %get-tuple-element.38.sine, bf16[2,2,2048,128]{3,2,1,0:T(8,128)(2,1)S(1)} %copy-done.3, bf16[2,2,2048,128]{3,2,1,0:T(8,128)(2,1)S(1)} %copy-done.4, ...), custom_call_target="tpu_custom_call" | custom-call | flops 1000 | bytes 1000 | tf_op jit(solution)/shard_map/attend/pallas_call | solution.py:260
  26.1 1.8 %collective-permute-start.6 = (bf16[64,128]{1,0:T(8,128)(2,1)S(1)}, bf16[64,128]{1,0:T(8,128)(2,1)S(1)}, u32[]{:S(2)}, u32[]{:S(2)}) collective-permute-start(bf16[64,128]{1,0:T(8,128)(2,1)S(1)} %attend.1.refs_3_), channel_id=1, source_target_pairs={{0,12},{4,8},{8,4},{12,0},{1,13},{5,9},{9,5},{13,1},{2,14},{6,10},... | collective-permute-start | bytes 49160 | tf_op jit(solution)/shard_map/ppermute | solution.py:31
  27.9 0.4 collective-permute-start.7
  28.2 2.3 %collective-permute-start.8 = (bf16[64,128]{1,0:T(8,128)(2,1)S(1)}, bf16[64,128]{1,0:T(8,128)(2,1)S(1)}, u32[]{:S(2)}, u32[]{:S(2)}) collective-permute-start(bf16[64,128]{1,0:T(8,128)(2,1)S(1)} %attend.1.refs_3_), channel_id=1, source_target_pairs={{0,4},{4,0},{8,12},{12,8},{1,5},{5,1},{9,13},{13,9},{2,6},{6,2},{1... | collective-permute-start | bytes 49160 | tf_op jit(solution)/shard_map/ppermute | solution.py:31
  30.5 1.1 %collective-permute-done.6.refs_0_ = bf16[64,128]{1,0:T(8,128)(2,1)S(1)} collective-permute-done((bf16[64,128]{1,0:T(8,128)(2,1)S(1)}, bf16[64,128]{1,0:T(8,128)(2,1)S(1)}, u32[]{:S(2)}, u32[]{:S(2)}) %collective-permute-start.6) | collective-permute-done | bytes 16416 | tf_op jit(solution)/shard_map/ppermute | solution.py:31
  31.7 0.8 %collective-permute-done.7.refs_1_ = bf16[64,128]{1,0:T(8,128)(2,1)S(1)} collective-permute-done((bf16[64,128]{1,0:T(8,128)(2,1)S(1)}, bf16[64,128]{1,0:T(8,128)(2,1)S(1)}, u32[]{:S(2)}, u32[]{:S(2)}) %collective-permute-start.7) | collective-permute-done | bytes 16416 | tf_op jit(solution)/shard_map/ppermute | solution.py:31
  32.5 0.1 arrange.1.rows
  32.6 4.4 %output.1 = (f32[2,4096]{1,0:T(2,128)S(1)}, f32[2,4096]{1,0:T(2,128)S(1)}, f32[2,4096]{1,0:T(2,128)S(1)}, f32[2,4096]{1,0:T(2,128)S(1)}) custom-call(bf16[8,4096]{1,0:T(8,128)(2,1)S(1)} %arrange.1.rows, bf16[4096,4096]{1,0:T(8,128)(2,1)S(1)} %copy-done), custom_call_target="tpu_custom_call" | custom-call | flops 1000 | bytes 1000 | tf_op jit(solution)/shard_map/output/pallas_call | solution.py:319
  37.0 1.5 %collective-permute-start.11 = (f32[2,4096]{1,0:T(2,128)S(1)}, f32[2,4096]{1,0:T(2,128)S(1)}, u32[]{:S(2)}, u32[]{:S(2)}) collective-permute-start(f32[2,4096]{1,0:T(2,128)S(1)} %get-tuple-element.46), channel_id=1, source_target_pairs={{0,2},{1,3},{2,0},{3,1},{4,6},{5,7},{6,4},{7,5},{8,10},{9,11},{10,... | collective-permute-start | bytes 98312 | tf_op jit(solution)/shard_map/ppermute | solution.py:39
  38.6 0.3 collective-permute-start.9
  38.9 1.8 %collective-permute-done.10 = f32[2,4096]{1,0:T(2,128)S(1)} collective-permute-done((f32[2,4096]{1,0:T(2,128)S(1)}, f32[2,4096]{1,0:T(2,128)S(1)}, u32[]{:S(2)}, u32[]{:S(2)}) %collective-permute-start.10) | collective-permute-done | bytes 32800 | tf_op jit(solution)/shard_map/ppermute | solution.py:39
  40.7 0.4 collective-permute-done.11
  41.1 0.6 %add_convert_fusion = bf16[2,4096]{1,0:T(2,128)(2,1)} fusion(f32[2,4096]{1,0:T(2,128)S(1)} %collective-permute-done.11, f32[2,4096]{1,0:T(2,128)S(1)} %collective-permute-done.10, f32[2,4096]{1,0:T(2,128)S(1)} %get-tuple-element.43, f32[2,4096]{1,0:T(2,128)S(1)} %collective-permute-done.9), kind=kLoop, calls=%fused_computation | loop fusion | flops 32768 | bytes 147456 | tf_op jit(solution)/shard_map/convert_element_type | solution.py:427
  (24 shorter events, 0.1 us)
Async XLA Ops:
  0.0 3.1 %copy-start.1 = (bf16[4096,256]{1,0:T(8,128)(2,1)S(1)}, bf16[4096,256]{1,0:T(8,128)(2,1)}, u32[]{:S(2)}) copy-start(bf16[4096,256]{1,0:T(8,128)(2,1)} %key_weight.3) | copy-start | bytes 6291460
  0.0 3.1 %copy-start.2 = (bf16[4096,256]{1,0:T(8,128)(2,1)S(1)}, bf16[4096,256]{1,0:T(8,128)(2,1)}, u32[]{:S(2)}) copy-start(bf16[4096,256]{1,0:T(8,128)(2,1)} %value_weight.3) | copy-start | bytes 6291460
  0.0 6.6 %collective-permute-start = (bf16[2,4096]{1,0:T(2,128)(2,1)}, bf16[2,4096]{1,0:T(2,128)(2,1)S(1)}, u32[]{:S(2)}, u32[]{:S(2)}) collective-permute-start(bf16[2,4096]{1,0:T(2,128)(2,1)} %refs_0_.1), channel_id=1, source_target_pairs={{0,1},{1,0},{2,3},{3,2},{4,5},{5,4},{6,7},{7,6},{8,9},{9,8},{10,11... | collective-permute-start | bytes 49160 | tf_op jit(solution)/shard_map/ppermute | solution.py:31
  0.5 6.2 %collective-permute-start.1 = (bf16[2,4096]{1,0:T(2,128)(2,1)}, bf16[2,4096]{1,0:T(2,128)(2,1)S(1)}, u32[]{:S(2)}, u32[]{:S(2)}) collective-permute-start(bf16[2,4096]{1,0:T(2,128)(2,1)} %refs_0_.1), channel_id=1, source_target_pairs={{0,2},{1,3},{2,0},{3,1},{4,6},{5,7},{6,4},{7,5},{8,10},{9,11},{10,... | collective-permute-start | bytes 49160 | tf_op jit(solution)/shard_map/ppermute | solution.py:31
  3.0 3.6 %collective-permute-start.2 = (bf16[2,4096]{1,0:T(2,128)(2,1)}, bf16[2,4096]{1,0:T(2,128)(2,1)S(1)}, u32[]{:S(2)}, u32[]{:S(2)}) collective-permute-start(bf16[2,4096]{1,0:T(2,128)(2,1)} %refs_0_.1), channel_id=1, source_target_pairs={{0,3},{1,2},{2,1},{3,0},{4,7},{5,6},{6,5},{7,4},{8,11},{9,10},{10,... | collective-permute-start | bytes 49160 | tf_op jit(solution)/shard_map/ppermute | solution.py:31
  3.1 3.6 %copy-start.5 = (bf16[2,4096]{1,0:T(2,128)(2,1)S(1)}, bf16[2,4096]{1,0:T(2,128)(2,1)}, u32[]{:S(2)}) copy-start(bf16[2,4096]{1,0:T(2,128)(2,1)} %refs_0_.1) | copy-start | bytes 49156
  15.9 4.9 %copy-start.6 = (s32[2]{0:T(128)S(1)}, s32[2]{0:T(128)}, u32[]{:S(2)}) copy-start(s32[2]{0:T(128)} %lengths.1) | copy-start | bytes 28
  15.9 9.2 %copy-start.3 = (bf16[2,2,2048,128]{3,2,1,0:T(8,128)(2,1)S(1)}, bf16[2,2,2048,128]{3,2,1,0:T(8,128)(2,1)}, u32[]{:S(2)}) copy-start(bf16[2,2,2048,128]{3,2,1,0:T(8,128)(2,1)} %key_cache.1) | copy-start | bytes 6291460
  15.9 9.2 %copy-start.4 = (bf16[2,2,2048,128]{3,2,1,0:T(8,128)(2,1)S(1)}, bf16[2,2,2048,128]{3,2,1,0:T(8,128)(2,1)}, u32[]{:S(2)}) copy-start(bf16[2,2,2048,128]{3,2,1,0:T(8,128)(2,1)} %cached_values.1) | copy-start | bytes 6291460
  15.9 16.7 %copy-start = (bf16[4096,4096]{1,0:T(8,128)(2,1)S(1)}, bf16[4096,4096]{1,0:T(8,128)(2,1)}, u32[]{:S(2)}) copy-start(bf16[4096,4096]{1,0:T(8,128)(2,1)} %w_out.1) | copy-start | bytes 100663296
  16.0 6.2 %collective-permute-start.3 = (f32[80,128]{1,0:T(8,128)S(1)}, f32[80,128]{1,0:T(8,128)S(1)}, u32[]{:S(2)}, u32[]{:S(2)}) collective-permute-start(f32[80,128]{1,0:T(8,128)S(1)} %get-tuple-element.40), channel_id=1, source_target_pairs={{0,12},{4,8},{8,4},{12,0},{1,13},{5,9},{9,5},{13,1},{2,14},{6,10},... | collective-permute-start | bytes 122888 | tf_op jit(solution)/shard_map/ppermute | solution.py:39
  20.2 4.9 %collective-permute-start.4 = (f32[80,128]{1,0:T(8,128)S(1)}, f32[80,128]{1,0:T(8,128)S(1)}, u32[]{:S(2)}, u32[]{:S(2)}) collective-permute-start(f32[80,128]{1,0:T(8,128)S(1)} %get-tuple-element.41), channel_id=1, source_target_pairs={{0,8},{4,12},{8,0},{12,4},{1,9},{5,13},{9,1},{13,5},{2,10},{6,14},... | collective-permute-start | bytes 122888 | tf_op jit(solution)/shard_map/ppermute | solution.py:39
  20.2 4.9 %collective-permute-start.5 = (f32[80,128]{1,0:T(8,128)S(1)}, f32[80,128]{1,0:T(8,128)S(1)}, u32[]{:S(2)}, u32[]{:S(2)}) collective-permute-start(f32[80,128]{1,0:T(8,128)S(1)} %get-tuple-element.42), channel_id=1, source_target_pairs={{0,4},{4,0},{8,12},{12,8},{1,5},{5,1},{9,13},{13,9},{2,6},{6,2},{1... | collective-permute-start | bytes 122888 | tf_op jit(solution)/shard_map/ppermute | solution.py:39
  26.1 5.6 %collective-permute-start.6 = (bf16[64,128]{1,0:T(8,128)(2,1)S(1)}, bf16[64,128]{1,0:T(8,128)(2,1)S(1)}, u32[]{:S(2)}, u32[]{:S(2)}) collective-permute-start(bf16[64,128]{1,0:T(8,128)(2,1)S(1)} %attend.1.refs_3_), channel_id=1, source_target_pairs={{0,12},{4,8},{8,4},{12,0},{1,13},{5,9},{9,5},{13,1},{2,14},{6,10},... | collective-permute-start | bytes 49160 | tf_op jit(solution)/shard_map/ppermute | solution.py:31
  27.9 4.6 %collective-permute-start.7 = (bf16[64,128]{1,0:T(8,128)(2,1)S(1)}, bf16[64,128]{1,0:T(8,128)(2,1)S(1)}, u32[]{:S(2)}, u32[]{:S(2)}) collective-permute-start(bf16[64,128]{1,0:T(8,128)(2,1)S(1)} %attend.1.refs_3_), channel_id=1, source_target_pairs={{0,8},{4,12},{8,0},{12,4},{1,9},{5,13},{9,1},{13,5},{2,10},{6,14},... | collective-permute-start | bytes 49160 | tf_op jit(solution)/shard_map/ppermute | solution.py:31
  28.2 4.3 %collective-permute-start.8 = (bf16[64,128]{1,0:T(8,128)(2,1)S(1)}, bf16[64,128]{1,0:T(8,128)(2,1)S(1)}, u32[]{:S(2)}, u32[]{:S(2)}) collective-permute-start(bf16[64,128]{1,0:T(8,128)(2,1)S(1)} %attend.1.refs_3_), channel_id=1, source_target_pairs={{0,4},{4,0},{8,12},{12,8},{1,5},{5,1},{9,13},{13,9},{2,6},{6,2},{1... | collective-permute-start | bytes 49160 | tf_op jit(solution)/shard_map/ppermute | solution.py:31
  37.0 3.7 %collective-permute-start.10 = (f32[2,4096]{1,0:T(2,128)S(1)}, f32[2,4096]{1,0:T(2,128)S(1)}, u32[]{:S(2)}, u32[]{:S(2)}) collective-permute-start(f32[2,4096]{1,0:T(2,128)S(1)} %get-tuple-element.45), channel_id=1, source_target_pairs={{0,3},{1,2},{2,1},{3,0},{4,7},{5,6},{6,5},{7,4},{8,11},{9,10},{10,... | collective-permute-start | bytes 98312 | tf_op jit(solution)/shard_map/ppermute | solution.py:39
  37.0 4.0 %collective-permute-start.11 = (f32[2,4096]{1,0:T(2,128)S(1)}, f32[2,4096]{1,0:T(2,128)S(1)}, u32[]{:S(2)}, u32[]{:S(2)}) collective-permute-start(f32[2,4096]{1,0:T(2,128)S(1)} %get-tuple-element.46), channel_id=1, source_target_pairs={{0,2},{1,3},{2,0},{3,1},{4,6},{5,7},{6,4},{7,5},{8,10},{9,11},{10,... | collective-permute-start | bytes 98312 | tf_op jit(solution)/shard_map/ppermute | solution.py:39
  38.6 2.5 %collective-permute-start.9 = (f32[2,4096]{1,0:T(2,128)S(1)}, f32[2,4096]{1,0:T(2,128)S(1)}, u32[]{:S(2)}, u32[]{:S(2)}) collective-permute-start(f32[2,4096]{1,0:T(2,128)S(1)} %get-tuple-element.44), channel_id=1, source_target_pairs={{0,1},{1,0},{2,3},{3,2},{4,5},{5,4},{6,7},{7,6},{8,9},{9,8},{10,11... | collective-permute-start | bytes 98312 | tf_op jit(solution)/shard_map/ppermute | solution.py:39

commit v7 on v6

--- a/solution.py
+++ b/solution.py
@@ -421,8 +421,8 @@
     rows = arrange(place, context_pieces, row_count, heads)
     sums = output(rows, w_out, rows_out, narrow)
     sums = scatter_pieces(sums, "narrow", narrow)
-    result = sums[0]
-    for s in sums[-1:] + sums[1:-1]:
+    result, *others = sums
+    for s in others[-1:] + others[:-1]:
         result = result + s
     return result.astype(jnp.bfloat16)
 

time: 41.9 us -> 41.9 us (level)
  no operation moved by 1% of the time
where the time goes in v7:
time: 41.9 us; the launch traced here: 41.7 us
  Pallas kernels  18.8 us (45%)
  starting transfers between devices  14.3 us (34%)
  waiting for transfers between devices  7.81 us (19%)
  other arithmetic  0.64 us (2%)
    pallas_call x1, Pallas kernels, project(): pl.pallas_call(functools.partial(project_kernel, pieces=len(hidden_pieces...  9.17 us
    ppermute x6, starting transfers between devices, gather_pieces(): lax.ppermute(piece, axis, xor_pairs(count, t))  7.54 us
    ppermute x6, starting transfers between devices, scatter_pieces(): lax.ppermute(pieces[t], axis, xor_pairs(count, t))  6.72 us
    ppermute x6, waiting for transfers between devices, scatter_pieces(): lax.ppermute(pieces[t], axis, xor_pairs(count, t))  5.84 us
    pallas_call x1, Pallas kernels, output(): pl.pallas_call(functools.partial(output_kernel, rows_out=rows_out), out_s...  4.44 us
    pallas_call x1, Pallas kernels, load(): pl.pallas_call(load_kernel, out_shape=jax.ShapeDtypeStruct(shape, w_query...  3.51 us
    ppermute x6, waiting for transfers between devices, gather_pieces(): lax.ppermute(piece, axis, xor_pairs(count, t))  1.97 us
    pallas_call x1, Pallas kernels, attend(): pl.pallas_call(functools.partial(attend_kernel, heads=heads, kv=kv, strid...  0.99 us
  transfers between devices with their start and end apart: 12, of which 6 were waited for; matrix products, arithmetic and copies ran while one was open for 0% of the time, Pallas kernels for 10%

profile of v7, /device:TPU:0, one launch (start us, length us, event | category | flops | bytes accessed | tf_op | source)
XLA Modules:
  0.0 41.7 jit_solution(9494892111353774167)
XLA Ops:
  0.0 0.5 %collective-permute-start = (bf16[2,4096]{1,0:T(2,128)(2,1)}, bf16[2,4096]{1,0:T(2,128)(2,1)S(1)}, u32[]{:S(2)}, u32[]{:S(2)}) collective-permute-start(bf16[2,4096]{1,0:T(2,128)(2,1)} %refs_0_.1), channel_id=1, source_target_pairs={{0,1},{1,0},{2,3},{3,2},{4,5},{5,4},{6,7},{7,6},{8,9},{9,8},{10,11... | collective-permute-start | bytes 49160 | tf_op jit(solution)/shard_map/ppermute | solution.py:31
  0.5 2.6 %collective-permute-start.1 = (bf16[2,4096]{1,0:T(2,128)(2,1)}, bf16[2,4096]{1,0:T(2,128)(2,1)S(1)}, u32[]{:S(2)}, u32[]{:S(2)}) collective-permute-start(bf16[2,4096]{1,0:T(2,128)(2,1)} %refs_0_.1), channel_id=1, source_target_pairs={{0,2},{1,3},{2,0},{3,1},{4,6},{5,7},{6,4},{7,5},{8,10},{9,11},{10,... | collective-permute-start | bytes 49160 | tf_op jit(solution)/shard_map/ppermute | solution.py:31
  3.0 0.1 collective-permute-start.2
  3.1 3.5 %load.1.head = bf16[1024,4096]{1,0:T(8,128)(2,1)S(1)} custom-call(bf16[4096,4096]{1,0:T(8,128)(2,1)} %w_query.3, bf16[4096,256]{1,0:T(8,128)(2,1)S(1)} %copy-done.1, bf16[4096,256]{1,0:T(8,128)(2,1)S(1)} %copy-done.2), custom_call_target="tpu_custom_call" | custom-call | flops 1000 | bytes 8388608 | tf_op jit(solution)/shard_map/load/pallas_call | solution.py:78
  6.7 9.2 %project.1 = (f32[80,128]{1,0:T(8,128)S(1)}, f32[80,128]{1,0:T(8,128)S(1)}, f32[80,128]{1,0:T(8,128)S(1)}, f32[80,128]{1,0:T(8,128)S(1)}) custom-call(bf16[1024,4096]{1,0:T(8,128)(2,1)S(1)} %load.1.head, bf16[4096,256]{1,0:T(8,128)(2,1)S(1)} %copy-done.1, bf16[4096,256]{1,0:T(8,128)(2,1)S(1)} %copy-done.2, bf16[4096,4096]{1,0:T(8,128)(2,1)} %w_query.3, ...), custom_call_target="tpu_custom_call" | custom-call | flops 1000 | bytes 1000 | tf_op jit(solution)/shard_map/project/pallas_call | solution.py:154
  15.9 0.0 copy-start.4
  16.0 4.2 %collective-permute-start.3 = (f32[80,128]{1,0:T(8,128)S(1)}, f32[80,128]{1,0:T(8,128)S(1)}, u32[]{:S(2)}, u32[]{:S(2)}) collective-permute-start(f32[80,128]{1,0:T(8,128)S(1)} %get-tuple-element.40), channel_id=1, source_target_pairs={{0,12},{4,8},{8,4},{12,0},{1,13},{5,9},{9,5},{13,1},{2,14},{6,10},... | collective-permute-start | bytes 122888 | tf_op jit(solution)/shard_map/ppermute | solution.py:39
  20.2 0.6 %collective-permute-start.5 = (f32[80,128]{1,0:T(8,128)S(1)}, f32[80,128]{1,0:T(8,128)S(1)}, u32[]{:S(2)}, u32[]{:S(2)}) collective-permute-start(f32[80,128]{1,0:T(8,128)S(1)} %get-tuple-element.42), channel_id=1, source_target_pairs={{0,4},{4,0},{8,12},{12,8},{1,5},{5,1},{9,13},{13,9},{2,6},{6,2},{1... | collective-permute-start | bytes 122888 | tf_op jit(solution)/shard_map/ppermute | solution.py:39
  20.8 0.6 %tables.1 = (s32[2,128]{1,0:T(2,128)S(1)}, f32[2,128]{1,0:T(2,128)S(1)}, f32[2,128]{1,0:T(2,128)S(1)}) custom-call(s32[2]{0:T(128)S(1)} %copy-done.6, f32[8,128]{1,0:T(8,128)S(1)} %get-tuple-element.35.frequency), custom_call_target="tpu_custom_call" | custom-call | flops 1000 | bytes 1000 | tf_op jit(solution)/shard_map/tables/pallas_call | solution.py:364
  21.4 0.8 %collective-permute-done.3.refs_1_ = f32[80,128]{1,0:T(8,128)S(1)} collective-permute-done((f32[80,128]{1,0:T(8,128)S(1)}, f32[80,128]{1,0:T(8,128)S(1)}, u32[]{:S(2)}, u32[]{:S(2)}) %collective-permute-start.3) | collective-permute-done | bytes 40992 | tf_op jit(solution)/shard_map/ppermute | solution.py:39
  22.2 2.9 %collective-permute-done.4.refs_2_ = f32[80,128]{1,0:T(8,128)S(1)} collective-permute-done((f32[80,128]{1,0:T(8,128)S(1)}, f32[80,128]{1,0:T(8,128)S(1)}, u32[]{:S(2)}, u32[]{:S(2)}) %collective-permute-start.4) | collective-permute-done | bytes 40992 | tf_op jit(solution)/shard_map/ppermute | solution.py:39
  25.1 1.0 %attend.1.refs_3_ = bf16[64,128]{1,0:T(8,128)(2,1)S(1)} custom-call(s32[2,128]{1,0:T(2,128)S(1)} %get-tuple-element.36.limits, f32[2,128]{1,0:T(2,128)S(1)} %get-tuple-element.37.cosine, f32[2,128]{1,0:T(2,128)S(1)} %get-tuple-element.38.sine, bf16[2,2,2048,128]{3,2,1,0:T(8,128)(2,1)S(1)} %copy-done.3, bf16[2,2,2048,128]{3,2,1,0:T(8,128)(2,1)S(1)} %copy-done.4, ...), custom_call_target="tpu_custom_call" | custom-call | flops 1000 | bytes 1000 | tf_op jit(solution)/shard_map/attend/pallas_call | solution.py:260
  26.1 1.8 %collective-permute-start.6 = (bf16[64,128]{1,0:T(8,128)(2,1)S(1)}, bf16[64,128]{1,0:T(8,128)(2,1)S(1)}, u32[]{:S(2)}, u32[]{:S(2)}) collective-permute-start(bf16[64,128]{1,0:T(8,128)(2,1)S(1)} %attend.1.refs_3_), channel_id=1, source_target_pairs={{0,12},{4,8},{8,4},{12,0},{1,13},{5,9},{9,5},{13,1},{2,14},{6,10},... | collective-permute-start | bytes 49160 | tf_op jit(solution)/shard_map/ppermute | solution.py:31
  27.9 0.4 collective-permute-start.7
  28.2 2.3 %collective-permute-start.8 = (bf16[64,128]{1,0:T(8,128)(2,1)S(1)}, bf16[64,128]{1,0:T(8,128)(2,1)S(1)}, u32[]{:S(2)}, u32[]{:S(2)}) collective-permute-start(bf16[64,128]{1,0:T(8,128)(2,1)S(1)} %attend.1.refs_3_), channel_id=1, source_target_pairs={{0,4},{4,0},{8,12},{12,8},{1,5},{5,1},{9,13},{13,9},{2,6},{6,2},{1... | collective-permute-start | bytes 49160 | tf_op jit(solution)/shard_map/ppermute | solution.py:31
  30.5 1.1 %collective-permute-done.6.refs_0_ = bf16[64,128]{1,0:T(8,128)(2,1)S(1)} collective-permute-done((bf16[64,128]{1,0:T(8,128)(2,1)S(1)}, bf16[64,128]{1,0:T(8,128)(2,1)S(1)}, u32[]{:S(2)}, u32[]{:S(2)}) %collective-permute-start.6) | collective-permute-done | bytes 16416 | tf_op jit(solution)/shard_map/ppermute | solution.py:31
  31.7 0.8 %collective-permute-done.7.refs_1_ = bf16[64,128]{1,0:T(8,128)(2,1)S(1)} collective-permute-done((bf16[64,128]{1,0:T(8,128)(2,1)S(1)}, bf16[64,128]{1,0:T(8,128)(2,1)S(1)}, u32[]{:S(2)}, u32[]{:S(2)}) %collective-permute-start.7) | collective-permute-done | bytes 16416 | tf_op jit(solution)/shard_map/ppermute | solution.py:31
  32.5 0.1 arrange.1.rows
  32.6 4.4 %output.1 = (f32[2,4096]{1,0:T(2,128)S(1)}, f32[2,4096]{1,0:T(2,128)S(1)}, f32[2,4096]{1,0:T(2,128)S(1)}, f32[2,4096]{1,0:T(2,128)S(1)}) custom-call(bf16[8,4096]{1,0:T(8,128)(2,1)S(1)} %arrange.1.rows, bf16[4096,4096]{1,0:T(8,128)(2,1)S(1)} %copy-done), custom_call_target="tpu_custom_call" | custom-call | flops 1000 | bytes 1000 | tf_op jit(solution)/shard_map/output/pallas_call | solution.py:319
  37.0 1.5 %collective-permute-start.11 = (f32[2,4096]{1,0:T(2,128)S(1)}, f32[2,4096]{1,0:T(2,128)S(1)}, u32[]{:S(2)}, u32[]{:S(2)}) collective-permute-start(f32[2,4096]{1,0:T(2,128)S(1)} %get-tuple-element.46), channel_id=1, source_target_pairs={{0,2},{1,3},{2,0},{3,1},{4,6},{5,7},{6,4},{7,5},{8,10},{9,11},{10,... | collective-permute-start | bytes 98312 | tf_op jit(solution)/shard_map/ppermute | solution.py:39
  38.6 0.3 collective-permute-start.9
  38.9 1.8 %collective-permute-done.10 = f32[2,4096]{1,0:T(2,128)S(1)} collective-permute-done((f32[2,4096]{1,0:T(2,128)S(1)}, f32[2,4096]{1,0:T(2,128)S(1)}, u32[]{:S(2)}, u32[]{:S(2)}) %collective-permute-start.10) | collective-permute-done | bytes 32800 | tf_op jit(solution)/shard_map/ppermute | solution.py:39
  40.7 0.4 collective-permute-done.11
  41.1 0.6 %add_convert_fusion = bf16[2,4096]{1,0:T(2,128)(2,1)} fusion(f32[2,4096]{1,0:T(2,128)S(1)} %collective-permute-done.11, f32[2,4096]{1,0:T(2,128)S(1)} %collective-permute-done.10, f32[2,4096]{1,0:T(2,128)S(1)} %get-tuple-element.43, f32[2,4096]{1,0:T(2,128)S(1)} %collective-permute-done.9), kind=kLoop, calls=%fused_computation | loop fusion | flops 32768 | bytes 147456 | tf_op jit(solution)/shard_map/convert_element_type | solution.py:427
  (24 shorter events, 0.1 us)
Async XLA Ops:
  0.0 3.1 %copy-start.1 = (bf16[4096,256]{1,0:T(8,128)(2,1)S(1)}, bf16[4096,256]{1,0:T(8,128)(2,1)}, u32[]{:S(2)}) copy-start(bf16[4096,256]{1,0:T(8,128)(2,1)} %key_weight.3) | copy-start | bytes 6291460
  0.0 3.1 %copy-start.2 = (bf16[4096,256]{1,0:T(8,128)(2,1)S(1)}, bf16[4096,256]{1,0:T(8,128)(2,1)}, u32[]{:S(2)}) copy-start(bf16[4096,256]{1,0:T(8,128)(2,1)} %value_weight.3) | copy-start | bytes 6291460
  0.0 6.6 %collective-permute-start = (bf16[2,4096]{1,0:T(2,128)(2,1)}, bf16[2,4096]{1,0:T(2,128)(2,1)S(1)}, u32[]{:S(2)}, u32[]{:S(2)}) collective-permute-start(bf16[2,4096]{1,0:T(2,128)(2,1)} %refs_0_.1), channel_id=1, source_target_pairs={{0,1},{1,0},{2,3},{3,2},{4,5},{5,4},{6,7},{7,6},{8,9},{9,8},{10,11... | collective-permute-start | bytes 49160 | tf_op jit(solution)/shard_map/ppermute | solution.py:31
  0.5 6.2 %collective-permute-start.1 = (bf16[2,4096]{1,0:T(2,128)(2,1)}, bf16[2,4096]{1,0:T(2,128)(2,1)S(1)}, u32[]{:S(2)}, u32[]{:S(2)}) collective-permute-start(bf16[2,4096]{1,0:T(2,128)(2,1)} %refs_0_.1), channel_id=1, source_target_pairs={{0,2},{1,3},{2,0},{3,1},{4,6},{5,7},{6,4},{7,5},{8,10},{9,11},{10,... | collective-permute-start | bytes 49160 | tf_op jit(solution)/shard_map/ppermute | solution.py:31
  3.0 3.6 %collective-permute-start.2 = (bf16[2,4096]{1,0:T(2,128)(2,1)}, bf16[2,4096]{1,0:T(2,128)(2,1)S(1)}, u32[]{:S(2)}, u32[]{:S(2)}) collective-permute-start(bf16[2,4096]{1,0:T(2,128)(2,1)} %refs_0_.1), channel_id=1, source_target_pairs={{0,3},{1,2},{2,1},{3,0},{4,7},{5,6},{6,5},{7,4},{8,11},{9,10},{10,... | collective-permute-start | bytes 49160 | tf_op jit(solution)/shard_map/ppermute | solution.py:31
  3.1 3.6 %copy-start.5 = (bf16[2,4096]{1,0:T(2,128)(2,1)S(1)}, bf16[2,4096]{1,0:T(2,128)(2,1)}, u32[]{:S(2)}) copy-start(bf16[2,4096]{1,0:T(2,128)(2,1)} %refs_0_.1) | copy-start | bytes 49156
  15.9 4.9 %copy-start.6 = (s32[2]{0:T(128)S(1)}, s32[2]{0:T(128)}, u32[]{:S(2)}) copy-start(s32[2]{0:T(128)} %lengths.1) | copy-start | bytes 28
  15.9 9.2 %copy-start.3 = (bf16[2,2,2048,128]{3,2,1,0:T(8,128)(2,1)S(1)}, bf16[2,2,2048,128]{3,2,1,0:T(8,128)(2,1)}, u32[]{:S(2)}) copy-start(bf16[2,2,2048,128]{3,2,1,0:T(8,128)(2,1)} %key_cache.1) | copy-start | bytes 6291460
  15.9 9.2 %copy-start.4 = (bf16[2,2,2048,128]{3,2,1,0:T(8,128)(2,1)S(1)}, bf16[2,2,2048,128]{3,2,1,0:T(8,128)(2,1)}, u32[]{:S(2)}) copy-start(bf16[2,2,2048,128]{3,2,1,0:T(8,128)(2,1)} %cached_values.1) | copy-start | bytes 6291460
  15.9 16.7 %copy-start = (bf16[4096,4096]{1,0:T(8,128)(2,1)S(1)}, bf16[4096,4096]{1,0:T(8,128)(2,1)}, u32[]{:S(2)}) copy-start(bf16[4096,4096]{1,0:T(8,128)(2,1)} %w_out.1) | copy-start | bytes 100663296
  16.0 6.2 %collective-permute-start.3 = (f32[80,128]{1,0:T(8,128)S(1)}, f32[80,128]{1,0:T(8,128)S(1)}, u32[]{:S(2)}, u32[]{:S(2)}) collective-permute-start(f32[80,128]{1,0:T(8,128)S(1)} %get-tuple-element.40), channel_id=1, source_target_pairs={{0,12},{4,8},{8,4},{12,0},{1,13},{5,9},{9,5},{13,1},{2,14},{6,10},... | collective-permute-start | bytes 122888 | tf_op jit(solution)/shard_map/ppermute | solution.py:39
  20.2 4.9 %collective-permute-start.4 = (f32[80,128]{1,0:T(8,128)S(1)}, f32[80,128]{1,0:T(8,128)S(1)}, u32[]{:S(2)}, u32[]{:S(2)}) collective-permute-start(f32[80,128]{1,0:T(8,128)S(1)} %get-tuple-element.41), channel_id=1, source_target_pairs={{0,8},{4,12},{8,0},{12,4},{1,9},{5,13},{9,1},{13,5},{2,10},{6,14},... | collective-permute-start | bytes 122888 | tf_op jit(solution)/shard_map/ppermute | solution.py:39
  20.2 4.9 %collective-permute-start.5 = (f32[80,128]{1,0:T(8,128)S(1)}, f32[80,128]{1,0:T(8,128)S(1)}, u32[]{:S(2)}, u32[]{:S(2)}) collective-permute-start(f32[80,128]{1,0:T(8,128)S(1)} %get-tuple-element.42), channel_id=1, source_target_pairs={{0,4},{4,0},{8,12},{12,8},{1,5},{5,1},{9,13},{13,9},{2,6},{6,2},{1... | collective-permute-start | bytes 122888 | tf_op jit(solution)/shard_map/ppermute | solution.py:39
  26.1 5.6 %collective-permute-start.6 = (bf16[64,128]{1,0:T(8,128)(2,1)S(1)}, bf16[64,128]{1,0:T(8,128)(2,1)S(1)}, u32[]{:S(2)}, u32[]{:S(2)}) collective-permute-start(bf16[64,128]{1,0:T(8,128)(2,1)S(1)} %attend.1.refs_3_), channel_id=1, source_target_pairs={{0,12},{4,8},{8,4},{12,0},{1,13},{5,9},{9,5},{13,1},{2,14},{6,10},... | collective-permute-start | bytes 49160 | tf_op jit(solution)/shard_map/ppermute | solution.py:31
  27.9 4.6 %collective-permute-start.7 = (bf16[64,128]{1,0:T(8,128)(2,1)S(1)}, bf16[64,128]{1,0:T(8,128)(2,1)S(1)}, u32[]{:S(2)}, u32[]{:S(2)}) collective-permute-start(bf16[64,128]{1,0:T(8,128)(2,1)S(1)} %attend.1.refs_3_), channel_id=1, source_target_pairs={{0,8},{4,12},{8,0},{12,4},{1,9},{5,13},{9,1},{13,5},{2,10},{6,14},... | collective-permute-start | bytes 49160 | tf_op jit(solution)/shard_map/ppermute | solution.py:31
  28.2 4.3 %collective-permute-start.8 = (bf16[64,128]{1,0:T(8,128)(2,1)S(1)}, bf16[64,128]{1,0:T(8,128)(2,1)S(1)}, u32[]{:S(2)}, u32[]{:S(2)}) collective-permute-start(bf16[64,128]{1,0:T(8,128)(2,1)S(1)} %attend.1.refs_3_), channel_id=1, source_target_pairs={{0,4},{4,0},{8,12},{12,8},{1,5},{5,1},{9,13},{13,9},{2,6},{6,2},{1... | collective-permute-start | bytes 49160 | tf_op jit(solution)/shard_map/ppermute | solution.py:31
  37.0 3.7 %collective-permute-start.10 = (f32[2,4096]{1,0:T(2,128)S(1)}, f32[2,4096]{1,0:T(2,128)S(1)}, u32[]{:S(2)}, u32[]{:S(2)}) collective-permute-start(f32[2,4096]{1,0:T(2,128)S(1)} %get-tuple-element.45), channel_id=1, source_target_pairs={{0,3},{1,2},{2,1},{3,0},{4,7},{5,6},{6,5},{7,4},{8,11},{9,10},{10,... | collective-permute-start | bytes 98312 | tf_op jit(solution)/shard_map/ppermute | solution.py:39
  37.0 4.0 %collective-permute-start.11 = (f32[2,4096]{1,0:T(2,128)S(1)}, f32[2,4096]{1,0:T(2,128)S(1)}, u32[]{:S(2)}, u32[]{:S(2)}) collective-permute-start(f32[2,4096]{1,0:T(2,128)S(1)} %get-tuple-element.46), channel_id=1, source_target_pairs={{0,2},{1,3},{2,0},{3,1},{4,6},{5,7},{6,4},{7,5},{8,10},{9,11},{10,... | collective-permute-start | bytes 98312 | tf_op jit(solution)/shard_map/ppermute | solution.py:39
  38.6 2.5 %collective-permute-start.9 = (f32[2,4096]{1,0:T(2,128)S(1)}, f32[2,4096]{1,0:T(2,128)S(1)}, u32[]{:S(2)}, u32[]{:S(2)}) collective-permute-start(f32[2,4096]{1,0:T(2,128)S(1)} %get-tuple-element.44), channel_id=1, source_target_pairs={{0,1},{1,0},{2,3},{3,2},{4,5},{5,4},{6,7},{7,6},{8,9},{9,8},{10,11... | collective-permute-start | bytes 98312 | tf_op jit(solution)/shard_map/ppermute | solution.py:39
